TPU v7x, 128 devices: a whole 4x4x4 slice. The times are simulated.
128 devices in a mesh: dp: 8 (over z, core), vocab: 16 (over y, x).
Axes of the slice: x: 4, y: 4, z: 4, core: 2. Of those that a mesh axis runs over, the one named last changes fastest.
Arguments:
- hidden: bfloat16 [2048, 4096], P(('dp', 'vocab')), may hold values from -64 to 64
- head_weight: bfloat16 [4096, 128256], P(None, ('dp', 'vocab')), may hold values from -0.0625 to 0.0625
- targets: int32 [2048], P(('dp', 'vocab')), may hold values from 0 to 128255
- bench_ids: int32 [2048], P(('dp', 'vocab')), may hold values from 0 to 39, as said below
- valid: int32 [2048], P(('dp', 'vocab')), may hold values from 0 to 1, as said below
- seq_lengths: int32 [64], replicated, may hold values from 1 to 64, 2048 in all
Outputs:
- token_loss: float32 [2048], P(('dp', 'vocab'))
- bench_loss: float32 [40], replicated
- bench_count: float32 [40], replicated
Inputs may be any that keep to these rules, and one draw needn't show every extreme that they name: `valid`: among the 16 positions of one device (aligned blocks) at most 8 have validity 1, and some block has exactly 8. `bench_ids`: A benchmark may have no positions in the window.
All inputs are finite; a program needn't handle non-finite values.
Results may differ from a plain program's by a relative error of at most 0.0003.
Values may be sent and summed in bfloat16 or wider, within the bound.
No kernel may reach another device: no remote copies, remote signals or barrier semaphores. Data moves between devices by JAX's collectives and lax.ppermute only.
A program may use at most 64 MiB of HBM per device.

v0:
```python
import jax
import jax.numpy as jnp
from jax import lax
from jax.sharding import Mesh
from jax.sharding import PartitionSpec as P

BENCH = 40
DP_VOCAB = ("dp_0", "dp_1", "vocab_0", "vocab_1")


def all_in_one(x, axis):
    leaves = jax.tree.leaves(x)
    order = sorted(range(len(leaves)), key=lambda k: -leaves[k].size)
    width = (1, *leaves[order[0]].shape)[-1]
    lines = [
        jnp.pad(leaves[k].reshape(-1), (0, -leaves[k].size % width)).reshape(-1, width)
        for k in order
    ]
    both, at, found = (lax.all_gather(jnp.concatenate(lines), axis), 0, {})
    for k, line in zip(order, lines):
        section = both[:, at : at + len(line)].reshape(len(both), -1)
        found[k] = section[:, : leaves[k].size].reshape(-1, *leaves[k].shape)
        at += len(line)
    numbers = iter(range(len(leaves)))
    return jax.tree.map(lambda _: found[next(numbers)], x)


def combined_by_axis(x, axes, combine):
    for axis in axes:
        pieces = all_in_one(x, axis)
        x = jax.tree.map(lambda part: part[0], pieces)
        for k in range(1, lax.axis_size(axis)):
            x = combine(x, jax.tree.map(lambda part: part[k], pieces))
    return x


def combine_stats(first, second):
    best = jnp.maximum(first[0], second[0])
    merged_total = first[1] * jnp.exp(first[0] - best) + second[1] * jnp.exp(second[0] - best)
    return (best, merged_total, first[2] + second[2])


def body(hidden, head_weight, targets, bench_ids, valid, seq_lengths):
    row_count = hidden.shape[0]
    col_width = head_weight.shape[1]
    device_index = lax.axis_index(DP_VOCAB)
    col_offset = device_index * col_width
    seq_ends = jnp.cumsum(seq_lengths) - 1
    positions = device_index * row_count + jnp.arange(row_count, dtype=jnp.int32)
    is_end = jnp.any(positions[:, None] == seq_ends[None, :], axis=1)
    scored = valid * (1 - is_end.astype(jnp.int32))
    scored_float = scored.astype(jnp.float32)
    labels = jnp.stack([targets, bench_ids, scored], axis=1)
    kept_rows = row_count // 2
    valid_rank = jnp.cumsum(valid) - 1
    other_rank = jnp.sum(valid) + jnp.cumsum(1 - valid) - 1
    slot = jnp.where(valid == 1, valid_rank, other_rank)
    selector = jnp.arange(kept_rows, dtype=jnp.int32)[:, None] == slot[None, :]
    outgoing = jnp.dot(
        selector.astype(jnp.bfloat16), hidden, preferred_element_type=jnp.float32
    ).astype(jnp.bfloat16)
    outgoing_labels = jnp.dot(selector.astype(jnp.int32), labels)
    gathered_rows = kept_rows * lax.axis_size(DP_VOCAB)
    column_ids = jnp.arange(col_width, dtype=jnp.int32)
    empty = jnp.zeros((gathered_rows,), jnp.float32)
    empty_labels = jnp.zeros((gathered_rows, 3), jnp.int32)
    block_rows = lax.all_gather(outgoing, DP_VOCAB, axis=0, tiled=True)
    block_labels = lax.all_gather(outgoing_labels, DP_VOCAB, axis=0, tiled=True)
    logits = jnp.dot(block_rows, head_weight, preferred_element_type=jnp.float32)
    row_top = jnp.max(logits, axis=1)
    row_total = jnp.sum(jnp.exp(logits - row_top[:, None]), axis=1)
    local_ids = block_labels[:, 0] - col_offset
    hits = column_ids[None, :] == local_ids[:, None]
    target_logit = jnp.sum(jnp.where(hits, logits, 0.0), axis=1)
    row_top, row_total, target_logit, all_labels = (
        row_top,
        row_total,
        target_logit,
        lax.dynamic_update_slice_in_dim(
            (empty, empty, empty, empty_labels)[3], block_labels, jnp.int32(0), 0
        ),
    )
    best, summed, target_sum = combined_by_axis(
        (row_top, row_total, target_logit), DP_VOCAB, combine_stats
    )
    all_losses = best + jnp.log(summed) - target_sum
    own_losses = lax.dynamic_slice_in_dim(all_losses, device_index * kept_rows, kept_rows)
    placed = jnp.dot(own_losses, selector.astype(jnp.float32), precision=lax.Precision.HIGHEST)
    token_loss = placed * scored_float
    bench_range = jnp.arange(BENCH, dtype=jnp.int32)
    scored_all = all_labels[:, 2].astype(jnp.float32)
    onehot_all = (all_labels[:, 1][:, None] == bench_range[None, :]).astype(jnp.float32)
    loss_sums = jnp.sum(onehot_all * (all_losses * scored_all)[:, None], axis=0)
    token_counts = jnp.sum(onehot_all * scored_all[:, None], axis=0)
    bench_loss = loss_sums / jnp.maximum(token_counts, 1.0)
    return (token_loss, bench_loss, token_counts)


def solution(mesh):
    torus = Mesh(mesh.devices.reshape(4, 2, 4, 4), ("dp_0", "dp_1", "vocab_0", "vocab_1"))
    in_specs = (P(DP_VOCAB, None), P(None, DP_VOCAB), P(DP_VOCAB), P(DP_VOCAB), P(DP_VOCAB), P())
    out_specs = (P(DP_VOCAB), P(), P())
    return jax.shard_map(body, mesh=torus, in_specs=in_specs, out_specs=out_specs, check_vma=False)
```

profile of v0, /device:TPU:0, one launch (start us, length us, event | category | flops | bytes accessed | tf_op | source)
XLA Modules:
  0.0 145.7 jit_solution(15104096766677652005)
XLA Ops:
  7.2 0.0 copy-start
  7.2 0.0 all-gather.11.cloned.1.call-start
  7.2 0.7 copy.20
  8.0 0.7 copy.22
  8.8 0.1 reduce-window.28
  8.9 0.1 add_reduce_fusion
  9.0 0.2 compare_reduce_fusion
  9.2 1.3 fusion.64
  10.5 0.1 copy.21
  10.6 0.8 add_reduce_fusion.1
  11.3 0.7 compare_select_fusion
  12.0 0.0 copy-done
  12.0 0.8 convolution_convert_fusion
  12.8 0.0 all-gather.11.cloned.1.call-update
  12.8 0.8 convolution_bitcast_fusion
  13.6 64.2 %all-gather.4 = s32[128,8,3]{1,2,0:T(4,128)S(1)} all-gather(s32[1,8,3]{1,2,0:T(4,128)S(1)} %convolution_bitcast_fusion), channel_id=1, replica_groups=mesh['dp_0'=4,'dp_1'=2,'vocab_0'=4,'vocab_1'=4] {'dp_0','dp_1','vocab_0'..., dimensions={0}, use_global_device_ids=true | all-gather | bytes 12384 | tf_op jit(solution)/shard_map/all_gather | solution.py:68
  77.8 0.1 reshape.928
  77.9 7.7 %all-gather.11.cloned.1.call-done = bf16[1024,4096]{1,0:T(8,128)(2,1)} async-done(((bf16[8,4096]{1,0:T(8,128)(2,1)}), bf16[1024,4096]{1,0:T(8,128)(2,1)}) %all-gather.11.cloned.1.call-update) | async-done | bytes 8388624 | tf_op jit(solution)/shard_map/all_gather | solution.py:67
  85.6 12.8 %fusion.70 = (f32[1024]{0:T(1024)S(1)}, f32[1024,1002]{0,1:T(8,128)S(1)}) fusion(bf16[1024,4096]{1,0:T(8,128)(2,1)} %all-gather.11.cloned.1.call-done, bf16[4096,1002]{0,1:T(8,128)(2,1)} %param.7), kind=kOutput, calls=%fused_computation.138 | convolution fusion | flops 8406410240 | bytes 20705280 | tf_op jit(solution)/shard_map/dot_general | solution.py:69
  98.4 0.0 copy-start.1
  98.4 1.1 exponential_reduce_fusion
  99.5 11.9 %all-gather.5 = f32[4,3,1024]{2,1,0:T(4,128)S(1)} all-gather(f32[1,3,1024]{2,1,0:T(4,128)S(1)} %maximum_bitcast_fusion), channel_id=2, replica_groups=mesh['dp_0'=4,'dp_1'=2,'vocab_0'=4,'vocab_1'=4] {'dp_0'}, dimensions={0}, use_global_device_ids=true | all-gather | bytes 61440 | tf_op jit(solution)/shard_map/all_gather | solution.py:19
  111.5 0.1 fusion.17
  111.6 1.8 %all-gather.6 = f32[2,3,1024]{2,1,0:T(4,128)S(1)} all-gather(f32[1,3,1024]{2,1,0:T(4,128)S(1)} %maximum_bitcast_fusion.1), channel_id=3, replica_groups=mesh['dp_0'=4,'dp_1'=2,'vocab_0'=4,'vocab_1'=4] {'dp_1'}, dimensions={0}, use_global_device_ids=true | all-gather | bytes 36864 | tf_op jit(solution)/shard_map/all_gather | solution.py:19
  113.5 11.9 %all-gather.7 = f32[4,3,1024]{2,1,0:T(4,128)S(1)} all-gather(f32[1,3,1024]{2,1,0:T(4,128)S(1)} %maximum_bitcast_fusion.2), channel_id=4, replica_groups=mesh['dp_0'=4,'dp_1'=2,'vocab_0'=4,'vocab_1'=4] {'vocab_0'}, dimensions={0}, use_global_device_ids=true | all-gather | bytes 61440 | tf_op jit(solution)/shard_map/all_gather | solution.py:19
  125.3 0.1 fusion.3
  125.4 11.9 %all-gather.8 = f32[4,3,1024]{2,1,0:T(4,128)S(1)} all-gather(f32[1,3,1024]{2,1,0:T(4,128)S(1)} %maximum_bitcast_fusion.3), channel_id=5, replica_groups=mesh['dp_0'=4,'dp_1'=2,'vocab_0'=4,'vocab_1'=4] {'vocab_1'}, dimensions={0}, use_global_device_ids=true | all-gather | bytes 61440 | tf_op jit(solution)/shard_map/all_gather | solution.py:19
  137.3 0.1 fusion.25
  137.4 0.1 select_reduce_fusion.1
  137.5 0.5 maximum_divide_fusion
  138.1 0.0 copy-done.1
  138.1 0.7 fusion
  (17 shorter events, 0.3 us)
Async XLA Ops:
  7.2 4.8 %copy-start = (bf16[16,4096]{1,0:T(8,128)(2,1)S(1)}, bf16[16,4096]{1,0:T(8,128)(2,1)}, u32[]{:S(2)}) copy-start(bf16[16,4096]{1,0:T(8,128)(2,1)} %param.6) | copy-start | bytes 393220
  7.2 78.4 %all-gather.11.cloned.1.call-start = ((), (), s32[]{:S(2)}) async-start(), calls=%async_computation | async-start | bytes 8454144 | tf_op jit(solution)/shard_map/all_gather | solution.py:67
  98.4 39.7 %copy-start.1 = (s32[16]{0:T(128)S(1)}, s32[16]{0:T(128)}, u32[]{:S(2)}) copy-start(s32[16]{0:T(128)} %param.10) | copy-start | bytes 196
  137.5 1.3 copy-start.2
Sparse Core Ops, SparseCore 0:
  12.9 72.6 all-gather.10
where the time goes:
time: 146 us
  blocking collectives  102 us (70%)
  matrix products  15.1 us (10%)
  between operations  14.2 us (10%)
  waiting for transfers between devices  7.69 us (5%)
  other arithmetic  5.29 us (4%)
  local copies, waits for them, and re-layouts  1.76 us (1%)
    all_gather x1, blocking collectives, body(): block_labels = lax.all_gather(outgoing_labels, DP_VOCAB, axis=0, tiled=True)  64.2 us
    all_gather x4, blocking collectives, all_in_one(): both, at, found = (lax.all_gather(jnp.concatenate(lines), axis), 0, {})  37.5 us
    dot_general x1, matrix products, body(): jnp.dot(block_rows, head_weight, preferred_element_type=jnp.float32)  12.8 us
    all_gather x1, waiting for transfers between devices, body(): block_rows = lax.all_gather(outgoing, DP_VOCAB, axis=0, tiled=True)  7.67 us
  transfers between devices with their start and end apart: 1, of which 1 were waited for; matrix products, arithmetic and copies ran while one was open for 1% of the time, Pallas kernels for 0%

commit v1 on v0

v1 whole, which is shorter than its diff:
```python
import jax
import jax.numpy as jnp
from jax import lax
from jax.experimental import pallas as pl
from jax.experimental.pallas import tpu as pltpu
from jax.sharding import Mesh
from jax.sharding import PartitionSpec as P

BENCH = 40
N_DEV = 128
LAB = 128
ROWS = (24, 24, 16)
STARTS = (0, 24, 48)
HALF_STARTS = (0, 96, 192)
F32 = jnp.float32


def coords(d):
    return (d // 32, (d // 4) % 4, d % 4), (d // 16) % 2


def flipped(d, axis, bit):
    (z, y, x), core = coords(d)
    p = [z, y, x]
    p[axis] = 3 - p[axis] if bit else p[axis] ^ 1
    return ((p[0] * 2 + core) * 4 + p[1]) * 4 + p[2]


def exchange(v, axis, bits):
    pairs = [(d, flipped(d, axis, bits[coords(d)[1]])) for d in range(N_DEV)]
    return lax.ppermute(v, "d", pairs)


def core_swap(v):
    return lax.ppermute(v, "d", [(d, d ^ 16) for d in range(N_DEV)])


def cube_bits(p):
    return (p ^ (p >> 1)) & 1, p >> 1


def score_kernel(offset_ref, x_ref, w_ref, out_ref, acc_ref):
    depth = w_ref.shape[1]
    rows = x_ref.shape[0]
    r = lax.broadcasted_iota(jnp.int32, (8, LAB), 0)
    c = lax.broadcasted_iota(jnp.int32, (8, LAB), 1)
    digit = jnp.where(c == 0, 65536.0, jnp.where(c == 1, 256.0, 1.0))
    sel = jnp.where((r == 5) & (c < 3), digit, jnp.where(((r == 3) | (r == 4)) & (r == c), 1.0, 0.0))
    dims = (((1,), (1,)), ((), ()))
    labels = lax.dot_general(
        sel.astype(jnp.bfloat16), x_ref[:, depth:], dims, preferred_element_type=F32
    )
    acc_ref[...] = lax.dot_general(w_ref[...], x_ref[:, :depth], dims, preferred_element_type=F32)
    logits = acc_ref[...]
    top = jnp.max(logits, axis=0, keepdims=True)
    total = jnp.sum(jnp.exp(logits - top), axis=0, keepdims=True)
    local = labels[5:6].astype(jnp.int32) - offset_ref[0]
    hit = lax.broadcasted_iota(jnp.int32, logits.shape, 0) == local
    target = jnp.sum(jnp.where(hit, logits, 0.0), axis=0, keepdims=True)
    k = lax.broadcasted_iota(jnp.int32, (8, rows), 0)
    out_ref[...] = jnp.where(k == 0, top, jnp.where(k == 1, total, jnp.where(k == 2, target, labels)))


def score(offset, x, w):
    rows = x.shape[0]
    vocab, depth = w.shape
    return pl.pallas_call(
        score_kernel,
        out_shape=jax.ShapeDtypeStruct((8, rows), F32),
        in_specs=[
            pl.BlockSpec(memory_space=pltpu.SMEM),
            pl.BlockSpec(memory_space=pltpu.VMEM),
            pl.BlockSpec(memory_space=pltpu.VMEM),
        ],
        out_specs=pl.BlockSpec(memory_space=pltpu.VMEM),
        scratch_shapes=[pltpu.VMEM((vocab, rows), F32)],
        compiler_params=pltpu.CompilerParams(vmem_limit_bytes=40 << 20),
        cost_estimate=pl.CostEstimate(
            flops=2 * rows * vocab * depth, bytes_accessed=2 * vocab * depth, transcendentals=rows * vocab
        ),
        name="score",
    )(offset, x, w)


def place_kernel(where_ref, own1, sib1, own2, sib2, stats_ref, labels_ref, all_ref):
    first = where_ref[0] == 0
    for half, (own, sib) in enumerate(((own1, sib1), (own2, sib2))):
        a, b = own[...], sib[...]
        by_core = (jnp.where(first, a, b), jnp.where(first, b, a))
        for g in range(3):
            for i in range(4):
                r = 4 * half + i
                rel = sum(((r >> k) & 1) << ((g + k) % 3) for k in range(3))
                at = HALF_STARTS[g] + i * ROWS[g]
                for core in range(2):
                    row = where_ref[1 + core] ^ rel
                    to = core * 64 + STARTS[g]
                    all_ref[row, :, to : to + ROWS[g]] = by_core[core][:, at : at + ROWS[g]]
    for kind in range(3):
        stats_ref[kind] = all_ref[:, kind, :]
    for kind in range(2):
        labels_ref[kind] = all_ref[:, 3 + kind, :]


def place(where, *parts):
    return pl.pallas_call(
        place_kernel,
        out_shape=(jax.ShapeDtypeStruct((3, 8, 128), F32), jax.ShapeDtypeStruct((2, 8, 128), F32)),
        in_specs=[pl.BlockSpec(memory_space=pltpu.SMEM)] + [pl.BlockSpec(memory_space=pltpu.VMEM)] * 4,
        out_specs=(pl.BlockSpec(memory_space=pltpu.VMEM),) * 2,
        scratch_shapes=[pltpu.VMEM((8, 8, 128), F32)],
        name="place",
    )(where, *parts)


def merged(a, b):
    best = jnp.maximum(a[0], b[0])
    total = a[1] * jnp.exp(a[0] - best) + b[1] * jnp.exp(b[0] - best)
    return jnp.stack([best, total, a[2] + b[2]])


def body(hidden, head_weight, targets, bench_ids, valid, seq_lengths):
    rows, depth = hidden.shape
    vocab = head_weight.shape[1]
    me = lax.axis_index("d")
    place_of, core = coords(me)
    bits = [cube_bits(p) for p in place_of]
    is_first = core == 0
    early = [jnp.where(is_first, b[1], b[0]) for b in bits]

    seqs = jnp.arange(seq_lengths.shape[0])
    seq_ends = jnp.sum(jnp.where(seqs[None, :] <= seqs[:, None], seq_lengths[None, :], 0), axis=1) - 1
    token = jnp.arange(rows, dtype=jnp.int32)
    is_end = jnp.any(seq_ends[:, None] == (me * rows + token)[None, :], axis=0)
    scored = valid * (1 - is_end.astype(jnp.int32))
    kept = rows // 2
    upto = token[None, :] <= token[:, None]
    valid_rank = jnp.sum(jnp.where(upto, valid[None, :], 0), axis=1) - 1
    slot = jnp.where(valid == 1, valid_rank, jnp.sum(valid) + token - valid_rank - 1)
    selector = jnp.arange(kept, dtype=jnp.int32)[:, None] == slot[None, :]
    column = jnp.arange(LAB)[None, :]
    labels = jnp.where(column == 0, (targets >> 16)[:, None], 0)
    labels = jnp.where(column == 1, ((targets >> 8) & 255)[:, None], labels)
    labels = jnp.where(column == 2, (targets & 255)[:, None], labels)
    labels = jnp.where(column == 3, bench_ids[:, None], labels)
    labels = jnp.where(column == 4, scored[:, None], labels)
    wide = jnp.concatenate([hidden, labels.astype(jnp.bfloat16)], axis=1)
    x = jnp.dot(selector.astype(jnp.bfloat16), wide, preferred_element_type=F32).astype(jnp.bfloat16)

    for axis in range(3):
        got = exchange(x, axis, (1, 0))
        x = jnp.where(
            early[axis] == 0, jnp.concatenate([x, got], 0), jnp.concatenate([got, x], 0)
        )
    held = [x[s : s + n] for s, n in zip(STARTS, ROWS)]
    for k in range(2):
        got = [exchange(held[g], (g + k) % 3, (0, 1)) for g in range(3)]
        held = [jnp.concatenate([a, b], 0) for a, b in zip(held, got)]
    w = head_weight.T
    offset = (me * vocab).reshape(1)
    last = [exchange(held[g], (g + 2) % 3, (0, 1)) for g in range(3)]
    own1 = jnp.concatenate(held, 0)
    sib1 = core_swap(own1)
    own2 = jnp.concatenate(last, 0)
    sib2 = core_swap(own2)
    parts = [score(offset, v, w) for v in (own1, sib1, own2, sib2)]
    by_core = [sum(b[k] << axis for axis, b in enumerate(bits)) for k in range(2)]
    stats, label_rows = place(jnp.stack([core, *by_core]), *parts)
    stats = merged(stats, core_swap(stats))
    for axis in range(3):
        for bit in range(2):
            stats = merged(stats, exchange(stats, axis, (bit, bit)))
    losses = stats[0] + jnp.log(stats[1]) - stats[2]
    bench_all, scored_all = label_rows[0], label_rows[1]
    me_early = early[0] + 2 * early[1] + 4 * early[2]
    own_at = jnp.where(is_first, *by_core) * 128 + core * 64 + me_early * kept
    own = lax.dynamic_slice_in_dim(losses.reshape(-1), own_at, kept)
    spread = jnp.sum(jnp.where(selector, own[:, None], 0.0), axis=0)
    token_loss = spread * scored.astype(F32)
    onehot = bench_all.reshape(-1)[:, None] == jnp.arange(BENCH, dtype=F32)[None, :]
    loss_sums = jnp.sum(jnp.where(onehot, (losses * scored_all).reshape(-1)[:, None], 0.0), axis=0)
    counts = jnp.sum(jnp.where(onehot, scored_all.reshape(-1)[:, None], 0.0), axis=0)
    return token_loss, loss_sums / jnp.maximum(counts, 1.0), counts


def solution(mesh):
    flat = Mesh(mesh.devices.reshape(-1), ("d",))
    in_specs = (P("d", None), P(None, "d"), P("d"), P("d"), P("d"), P())
    return jax.shard_map(
        body, mesh=flat, in_specs=in_specs, out_specs=(P("d"), P(), P()), check_vma=False
    )
```

time: 146 us -> 132 us (0.904)
  blocking collectives: 102 us -> 0 us
  waiting for transfers between devices: 7.69 us -> 62.6 us
  starting transfers between devices: 0.04 us -> 24.7 us
  Pallas kernels: 0 us -> 16.7 us
  local copies, waits for them, and re-layouts: 1.76 us -> 16.5 us
  matrix products: 15.1 us -> 1.05 us
  between operations: 14.2 us -> 0.88 us
  other arithmetic: 5.29 us -> 8.87 us
    all_gather x5 -> x0, blocking collectives: 102 us -> none  [the longest x1 64.2 us: body(): block_labels = lax.all_gather(outgoing_labels, DP_VOCAB, axis=0, tiled=True)]
    ppermute x0 -> x21, waiting for transfers between devices: none -> 62.6 us  [the longest x18 61.2 us: exchange(): return lax.ppermute(v, 'd', pairs)]
    ppermute x0 -> x21, starting transfers between devices: none -> 24.7 us  [the longest x18 23.8 us: exchange(): return lax.ppermute(v, 'd', pairs)]
    pallas_call x0 -> x5, Pallas kernels: none -> 16.7 us  [the longest x4 15.1 us: score(): pl.pallas_call(score_kernel, out_shape=jax.ShapeDtypeStruct((8, rows), F3...]
    dot_general x4 -> x1, matrix products: 15.1 us -> 1.05 us  [body(): jnp.dot(selector.astype(jnp.bfloat16), wide, preferred_element_type=F32)]
    unnamed x7 -> x22, local copies, waits for them, and re-layouts: 0.16 us -> 13.6 us
    all_gather x1 -> x0, waiting for transfers between devices: 7.67 us -> none  [body(): block_rows = lax.all_gather(outgoing, DP_VOCAB, axis=0, tiled=True)]
    reduce_sum x2 -> x5, other arithmetic: 1.23 us -> 3.06 us  [the longest x1 1.3 us: body(): jnp.sum(valid) + token - valid_rank - 1]
  transfers between devices with their start and end apart: 1 -> 21, of which waited for: 1 -> 15; matrix products, arithmetic and copies ran while one was open for 1% -> 5% of each run, Pallas kernels for 0% -> 8%
where the time goes in v1:
time: 132 us; the launch traced here: 131 us
  waiting for transfers between devices  62.6 us (47%)
  starting transfers between devices  24.7 us (19%)
  Pallas kernels  16.7 us (13%)
  local copies, waits for them, and re-layouts  16.5 us (12%)
  other arithmetic  8.87 us (7%)
    ppermute x18, waiting for transfers between devices, exchange(): return lax.ppermute(v, 'd', pairs)  61.2 us
    ppermute x18, starting transfers between devices, exchange(): return lax.ppermute(v, 'd', pairs)  23.8 us
    pallas_call x4, Pallas kernels, score(): pl.pallas_call(score_kernel, out_shape=jax.ShapeDtypeStruct((8, rows), F3...  15.1 us
    unnamed x22, local copies, waits for them, and re-layouts  13.6 us
  transfers between devices with their start and end apart: 21, of which 15 were waited for; matrix products, arithmetic and copies ran while one was open for 5% of the time, Pallas kernels for 8%

profile of v1, /device:TPU:0, one launch (start us, length us, event | category | flops | bytes accessed | tf_op | source)
XLA Modules:
  0.0 131.2 jit_solution(11626534529249710261)
XLA Ops:
  1.4 1.3 reduce_sum.55
  3.7 1.3 %compare_select_fusion = (s32[16]{0:T(128)S(1)}, s32[16]{0:T(128)S(1)}, s32[16]{0:T(128)S(1)}, s32[16]{0:T(128)S(1)}, s32[16]{0:T(128)S(1)}) fusion(s32[16]{0:T(128)} %param.10, s32[16]{0:T(128)S(1)} %select_reduce_fusion.3, s32[]{:T(128)} %reduce_sum.55, pred[16]{0:T(512)(128)(4,1)S(1)} %compare_reduce_fusion, s32[16]{0:T(128)} %param.8), kind=kLoop, calls=%fused_computation.123 | loop fusion | flops 208 | bytes 532 | tf_op jit(solution)/shard_map/jit(_where)/select_n | solution.py:139
  5.8 1.1 convolution_convert_fusion
  6.8 4.2 %collective-permute-start = (bf16[8,4224]{1,0:T(8,128)(2,1)S(1)}, bf16[8,4224]{1,0:T(8,128)(2,1)S(1)}, u32[]{:S(2)}, u32[]{:S(2)}) collective-permute-start(bf16[8,4224]{1,0:T(8,128)(2,1)S(1)} %convolution_convert_fusion), channel_id=1, source_target_pairs={{0,96},{1,97},{2,98},{3,99},{4,100},{5,101},{6,102},{7,103},{8,104... | collective-permute-start | bytes 202760 | tf_op jit(solution)/shard_map/ppermute | solution.py:31
  11.0 2.3 %collective-permute-done = bf16[8,4224]{1,0:T(8,128)(2,1)S(1)} collective-permute-done((bf16[8,4224]{1,0:T(8,128)(2,1)S(1)}, bf16[8,4224]{1,0:T(8,128)(2,1)S(1)}, u32[]{:S(2)}, u32[]{:S(2)}) %collective-permute-start) | collective-permute-done | bytes 67616 | tf_op jit(solution)/shard_map/ppermute | solution.py:31
  13.3 3.1 %collective-permute-start.1 = (bf16[16,4224]{1,0:T(8,128)(2,1)S(1)}, bf16[16,4224]{1,0:T(8,128)(2,1)S(1)}, u32[]{:S(2)}, u32[]{:S(2)}) collective-permute-start(bf16[16,4224]{1,0:T(8,128)(2,1)S(1)} %maximum_select_fusion.2), channel_id=1, source_target_pairs={{0,12},{1,13},{2,14},{3,15},{4,8},{5,9},{6,10},{7,11},{8,4},{9,5},... | collective-permute-start | bytes 405512 | tf_op jit(solution)/shard_map/ppermute | solution.py:31
  16.4 3.2 %collective-permute-done.1 = bf16[16,4224]{1,0:T(8,128)(2,1)S(1)} collective-permute-done((bf16[16,4224]{1,0:T(8,128)(2,1)S(1)}, bf16[16,4224]{1,0:T(8,128)(2,1)S(1)}, u32[]{:S(2)}, u32[]{:S(2)}) %collective-permute-start.1) | collective-permute-done | bytes 135200 | tf_op jit(solution)/shard_map/ppermute | solution.py:31
  19.7 2.8 %collective-permute-start.2 = (bf16[32,4224]{1,0:T(8,128)(2,1)S(1)}, bf16[32,4224]{1,0:T(8,128)(2,1)S(1)}, u32[]{:S(2)}, u32[]{:S(2)}) collective-permute-start(bf16[32,4224]{1,0:T(8,128)(2,1)S(1)} %maximum_select_fusion.1), channel_id=1, source_target_pairs={{0,3},{1,2},{2,1},{3,0},{4,7},{5,6},{6,5},{7,4},{8,11},{9,10},{10,... | collective-permute-start | bytes 811016 | tf_op jit(solution)/shard_map/ppermute | solution.py:31
  22.5 4.9 %collective-permute-done.2 = bf16[32,4224]{1,0:T(8,128)(2,1)S(1)} collective-permute-done((bf16[32,4224]{1,0:T(8,128)(2,1)S(1)}, bf16[32,4224]{1,0:T(8,128)(2,1)S(1)}, u32[]{:S(2)}, u32[]{:S(2)}) %collective-permute-start.2) | collective-permute-done | bytes 270368 | tf_op jit(solution)/shard_map/ppermute | solution.py:31
  28.6 5.4 %collective-permute-done.3 = bf16[24,4224]{1,0:T(8,128)(2,1)S(1)} collective-permute-done((bf16[24,4224]{1,0:T(8,128)(2,1)S(1)}, bf16[24,4224]{1,0:T(8,128)(2,1)S(1)}, u32[]{:S(2)}, u32[]{:S(2)}) %collective-permute-start.3) | collective-permute-done | bytes 202784 | tf_op jit(solution)/shard_map/ppermute | solution.py:31
  35.6 6.4 %collective-permute-done.4 = bf16[48,4224]{1,0:T(8,128)(2,1)S(1)} collective-permute-done((bf16[48,4224]{1,0:T(8,128)(2,1)S(1)}, bf16[48,4224]{1,0:T(8,128)(2,1)S(1)}, u32[]{:S(2)}, u32[]{:S(2)}) %collective-permute-start.4) | collective-permute-done | bytes 405536 | tf_op jit(solution)/shard_map/ppermute | solution.py:31
  46.0 1.8 %collective-permute-start.10 = (bf16[96,4224]{1,0:T(8,128)(2,1)S(1)}, bf16[96,4224]{1,0:T(8,128)(2,1)S(1)}, u32[]{:S(2)}, u32[]{:S(2)}) collective-permute-start(bf16[96,4224]{1,0:T(8,128)(2,1)S(1)} %pad_maximum_fusion), channel_id=1, source_target_pairs={{0,1},{1,0},{2,3},{3,2},{4,5},{5,4},{6,7},{7,6},{8,9},{9,8},{10,11... | collective-permute-start | bytes 2433032 | tf_op jit(solution)/shard_map/ppermute | solution.py:31
  48.0 2.7 %collective-permute-done.7 = bf16[16,4224]{1,0:T(8,128)(2,1)S(1)} collective-permute-done((bf16[16,4224]{1,0:T(8,128)(2,1)S(1)}, bf16[16,4224]{1,0:T(8,128)(2,1)S(1)}, u32[]{:S(2)}, u32[]{:S(2)}) %collective-permute-start.7) | collective-permute-done | bytes 135200 | tf_op jit(solution)/shard_map/ppermute | solution.py:31
  51.5 11.7 %collective-permute-done.8 = bf16[32,4224]{1,0:T(8,128)(2,1)S(1)} collective-permute-done((bf16[32,4224]{1,0:T(8,128)(2,1)S(1)}, bf16[32,4224]{1,0:T(8,128)(2,1)S(1)}, u32[]{:S(2)}, u32[]{:S(2)}) %collective-permute-start.8) | collective-permute-done | bytes 270368 | tf_op jit(solution)/shard_map/ppermute | solution.py:31
  64.5 8.8 %collective-permute-done.12 = bf16[64,4224]{1,0:T(8,128)(2,1)S(1)} collective-permute-done((bf16[64,4224]{1,0:T(8,128)(2,1)S(1)}, bf16[64,4224]{1,0:T(8,128)(2,1)S(1)}, u32[]{:S(2)}, u32[]{:S(2)}) %collective-permute-start.12) | collective-permute-done | bytes 540704 | tf_op jit(solution)/shard_map/ppermute | solution.py:31
  74.9 3.3 %copy-done = bf16[4096,1002]{0,1:T(8,128)(2,1)S(1)} copy-done((bf16[4096,1002]{0,1:T(8,128)(2,1)S(1)}, bf16[4096,1002]{0,1:T(8,128)(2,1)}, u32[]{:S(2)}) %copy-start) | copy-done | bytes 8208408
  78.2 4.2 %score.4.own1 = f32[8,256]{1,0:T(8,128)S(1)} custom-call(s32[1]{0:T(128)} %bitcast.3.offset_ref, bf16[256,4224]{1,0:T(8,128)(2,1)} %constant_dynamic-update-slice_fusion.x_ref, bf16[1002,4096]{1,0:T(8,128)(2,1)S(1)} %bitcast.235), custom_call_target="tpu_custom_call" | custom-call | flops 2101346304 | bytes 8208384 | tf_op jit(solution)/shard_map/score/pallas_call | solution.py:67
  83.0 3.3 %copy-done.1 = bf16[4096,1002]{0,1:T(8,128)(2,1)S(1)} copy-done((bf16[4096,1002]{0,1:T(8,128)(2,1)S(1)}, bf16[4096,1002]{0,1:T(8,128)(2,1)}, u32[]{:S(2)}) %copy-start.1) | copy-done | bytes 8208408
  86.4 2.6 %score.6.own2 = f32[8,256]{1,0:T(8,128)S(1)} custom-call(s32[1]{0:T(128)} %bitcast.3.offset_ref, bf16[256,4224]{1,0:T(8,128)(2,1)S(1)} %constant_dynamic-update-slice_fusion.9.x_ref, bf16[1002,4096]{1,0:T(8,128)(2,1)S(1)} %bitcast.236), custom_call_target="tpu_custom_call" | custom-call | flops 2101346304 | bytes 8208384 | tf_op jit(solution)/shard_map/score/pallas_call | solution.py:67
  89.6 4.2 %score.5.sib1 = f32[8,256]{1,0:T(8,128)S(1)} custom-call(s32[1]{0:T(128)} %bitcast.3.offset_ref, bf16[256,4224]{1,0:T(8,128)(2,1)} %collective-permute-done.9.x_ref, bf16[1002,4096]{1,0:T(8,128)(2,1)S(1)} %bitcast.237), custom_call_target="tpu_custom_call" | custom-call | flops 2101346304 | bytes 8208384 | tf_op jit(solution)/shard_map/score/pallas_call | solution.py:67
  94.3 4.2 %score.7.sib2 = f32[8,256]{1,0:T(8,128)S(1)} custom-call(s32[1]{0:T(128)} %bitcast.3.offset_ref, bf16[256,4224]{1,0:T(8,128)(2,1)} %collective-permute-done.13.x_ref, bf16[1002,4096]{1,0:T(8,128)(2,1)S(1)} %bitcast.238), custom_call_target="tpu_custom_call" | custom-call | flops 2101346304 | bytes 8208384 | tf_op jit(solution)/shard_map/score/pallas_call | solution.py:67
  99.1 1.5 %place.1 = (f32[3,8,128]{2,1,0:T(8,128)}, f32[2,8,128]{2,1,0:T(8,128)}) custom-call(s32[3]{0:T(128)} %pad_add_fusion.where_ref, f32[8,256]{1,0:T(8,128)} %copy-done.2, f32[8,256]{1,0:T(8,128)} %copy-done.4, f32[8,256]{1,0:T(8,128)} %copy-done.3, f32[8,256]{1,0:T(8,128)} %copy-done.5), custom_call_target="tpu_custom_call" | custom-call | tf_op jit(solution)/shard_map/place/pallas_call | solution.py:106
  100.7 1.3 %collective-permute-done.14 = f32[3,8,128]{2,1,0:T(8,128)S(1)} collective-permute-done((f32[3,8,128]{2,1,0:T(8,128)}, f32[3,8,128]{2,1,0:T(8,128)S(1)}, u32[]{:S(2)}, u32[]{:S(2)}) %collective-permute-start.14) | collective-permute-done | bytes 12320 | tf_op jit(solution)/shard_map/ppermute | solution.py:35
  102.8 3.7 %collective-permute-done.15 = f32[3,8,128]{2,1,0:T(8,128)S(1)} collective-permute-done((f32[3,8,128]{2,1,0:T(8,128)S(1)}, f32[3,8,128]{2,1,0:T(8,128)S(1)}, u32[]{:S(2)}, u32[]{:S(2)}) %collective-permute-start.15) | collective-permute-done | bytes 12320 | tf_op jit(solution)/shard_map/ppermute | solution.py:31
  106.5 3.3 %collective-permute-start.16 = (f32[3,8,128]{2,1,0:T(8,128)S(1)}, f32[3,8,128]{2,1,0:T(8,128)S(1)}, u32[]{:S(2)}, u32[]{:S(2)}) collective-permute-start(f32[3,8,128]{2,1,0:T(8,128)S(1)} %pad_maximum_fusion.7), channel_id=1, source_target_pairs={{0,96},{1,97},{2,98},{3,99},{4,100},{5,101},{6,102},{7,103},{8,104... | collective-permute-start | bytes 36872 | tf_op jit(solution)/shard_map/ppermute | solution.py:31
  109.9 1.7 %collective-permute-done.16 = f32[3,8,128]{2,1,0:T(8,128)S(1)} collective-permute-done((f32[3,8,128]{2,1,0:T(8,128)S(1)}, f32[3,8,128]{2,1,0:T(8,128)S(1)}, u32[]{:S(2)}, u32[]{:S(2)}) %collective-permute-start.16) | collective-permute-done | bytes 12320 | tf_op jit(solution)/shard_map/ppermute | solution.py:31
  111.7 3.7 %collective-permute-done.17 = f32[3,8,128]{2,1,0:T(8,128)S(1)} collective-permute-done((f32[3,8,128]{2,1,0:T(8,128)S(1)}, f32[3,8,128]{2,1,0:T(8,128)S(1)}, u32[]{:S(2)}, u32[]{:S(2)}) %collective-permute-start.17) | collective-permute-done | bytes 12320 | tf_op jit(solution)/shard_map/ppermute | solution.py:31
  115.4 3.0 %collective-permute-start.18 = (f32[3,8,128]{2,1,0:T(8,128)S(1)}, f32[3,8,128]{2,1,0:T(8,128)S(1)}, u32[]{:S(2)}, u32[]{:S(2)}) collective-permute-start(f32[3,8,128]{2,1,0:T(8,128)S(1)} %pad_maximum_fusion.9), channel_id=1, source_target_pairs={{0,12},{1,13},{2,14},{3,15},{4,8},{5,9},{6,10},{7,11},{8,4},{9,5},... | collective-permute-start | bytes 36872 | tf_op jit(solution)/shard_map/ppermute | solution.py:31
  118.4 1.9 %collective-permute-done.18 = f32[3,8,128]{2,1,0:T(8,128)S(1)} collective-permute-done((f32[3,8,128]{2,1,0:T(8,128)S(1)}, f32[3,8,128]{2,1,0:T(8,128)S(1)}, u32[]{:S(2)}, u32[]{:S(2)}) %collective-permute-start.18) | collective-permute-done | bytes 12320 | tf_op jit(solution)/shard_map/ppermute | solution.py:31
  120.7 3.4 %collective-permute-done.19 = f32[3,8,128]{2,1,0:T(8,128)S(1)} collective-permute-done((f32[3,8,128]{2,1,0:T(8,128)S(1)}, f32[3,8,128]{2,1,0:T(8,128)S(1)}, u32[]{:S(2)}, u32[]{:S(2)}) %collective-permute-start.19) | collective-permute-done | bytes 12320 | tf_op jit(solution)/shard_map/ppermute | solution.py:31
  124.2 2.8 %collective-permute-start.20 = (f32[3,8,128]{2,1,0:T(8,128)S(1)}, f32[3,8,128]{2,1,0:T(8,128)S(1)}, u32[]{:S(2)}, u32[]{:S(2)}) collective-permute-start(f32[3,8,128]{2,1,0:T(8,128)S(1)} %pad_maximum_fusion.11), channel_id=1, source_target_pairs={{0,3},{1,2},{2,1},{3,0},{4,7},{5,6},{6,5},{7,4},{8,11},{9,10},{10,... | collective-permute-start | bytes 36872 | tf_op jit(solution)/shard_map/ppermute | solution.py:31
  127.7 1.5 %collective-permute-done.20 = f32[3,8,128]{2,1,0:T(8,128)S(1)} collective-permute-done((f32[3,8,128]{2,1,0:T(8,128)S(1)}, f32[3,8,128]{2,1,0:T(8,128)S(1)}, u32[]{:S(2)}, u32[]{:S(2)}) %collective-permute-start.20) | collective-permute-done | bytes 12320 | tf_op jit(solution)/shard_map/ppermute | solution.py:31
  (82 shorter events, 19.6 us)
Async XLA Ops:
  6.8 6.5 %collective-permute-start = (bf16[8,4224]{1,0:T(8,128)(2,1)S(1)}, bf16[8,4224]{1,0:T(8,128)(2,1)S(1)}, u32[]{:S(2)}, u32[]{:S(2)}) collective-permute-start(bf16[8,4224]{1,0:T(8,128)(2,1)S(1)} %convolution_convert_fusion), channel_id=1, source_target_pairs={{0,96},{1,97},{2,98},{3,99},{4,100},{5,101},{6,102},{7,103},{8,104... | collective-permute-start | bytes 202760 | tf_op jit(solution)/shard_map/ppermute | solution.py:31
  13.3 6.3 %collective-permute-start.1 = (bf16[16,4224]{1,0:T(8,128)(2,1)S(1)}, bf16[16,4224]{1,0:T(8,128)(2,1)S(1)}, u32[]{:S(2)}, u32[]{:S(2)}) collective-permute-start(bf16[16,4224]{1,0:T(8,128)(2,1)S(1)} %maximum_select_fusion.2), channel_id=1, source_target_pairs={{0,12},{1,13},{2,14},{3,15},{4,8},{5,9},{6,10},{7,11},{8,4},{9,5},... | collective-permute-start | bytes 405512 | tf_op jit(solution)/shard_map/ppermute | solution.py:31
  19.7 7.8 %collective-permute-start.2 = (bf16[32,4224]{1,0:T(8,128)(2,1)S(1)}, bf16[32,4224]{1,0:T(8,128)(2,1)S(1)}, u32[]{:S(2)}, u32[]{:S(2)}) collective-permute-start(bf16[32,4224]{1,0:T(8,128)(2,1)S(1)} %maximum_select_fusion.1), channel_id=1, source_target_pairs={{0,3},{1,2},{2,1},{3,0},{4,7},{5,6},{6,5},{7,4},{8,11},{9,10},{10,... | collective-permute-start | bytes 811016 | tf_op jit(solution)/shard_map/ppermute | solution.py:31
  28.2 5.7 %collective-permute-start.3 = (bf16[24,4224]{1,0:T(8,128)(2,1)S(1)}, bf16[24,4224]{1,0:T(8,128)(2,1)S(1)}, u32[]{:S(2)}, u32[]{:S(2)}) collective-permute-start(bf16[24,4224]{1,0:T(8,128)(2,1)S(1)} %get-tuple-element.25), channel_id=1, source_target_pairs={{0,32},{1,33},{2,34},{3,35},{4,36},{5,37},{6,38},{7,39},{8,40},{9,... | collective-permute-start | bytes 608264 | tf_op jit(solution)/shard_map/ppermute | solution.py:31
  28.2 6.2 %collective-permute-start.5 = (bf16[24,4224]{1,0:T(8,128)(2,1)S(1)}, bf16[24,4224]{1,0:T(8,128)(2,1)S(1)}, u32[]{:S(2)}, u32[]{:S(2)}) collective-permute-start(bf16[24,4224]{1,0:T(8,128)(2,1)S(1)} %get-tuple-element.23), channel_id=1, source_target_pairs={{0,4},{1,5},{2,6},{3,7},{4,0},{5,1},{6,2},{7,3},{8,12},{9,13},{10,... | collective-permute-start | bytes 608264 | tf_op jit(solution)/shard_map/ppermute | solution.py:31
  34.0 8.0 %collective-permute-start.4 = (bf16[48,4224]{1,0:T(8,128)(2,1)S(1)}, bf16[48,4224]{1,0:T(8,128)(2,1)S(1)}, u32[]{:S(2)}, u32[]{:S(2)}) collective-permute-start(bf16[48,4224]{1,0:T(8,128)(2,1)S(1)} %pad_maximum_fusion.3), channel_id=1, source_target_pairs={{0,4},{1,5},{2,6},{3,7},{4,0},{5,1},{6,2},{7,3},{8,12},{9,13},{10,... | collective-permute-start | bytes 1216520 | tf_op jit(solution)/shard_map/ppermute | solution.py:31
  34.5 9.7 %collective-permute-start.6 = (bf16[48,4224]{1,0:T(8,128)(2,1)S(1)}, bf16[48,4224]{1,0:T(8,128)(2,1)S(1)}, u32[]{:S(2)}, u32[]{:S(2)}) collective-permute-start(bf16[48,4224]{1,0:T(8,128)(2,1)S(1)} %pad_maximum_fusion.4), channel_id=1, source_target_pairs={{0,1},{1,0},{2,3},{3,2},{4,5},{5,4},{6,7},{7,6},{8,9},{9,8},{10,11... | collective-permute-start | bytes 1216520 | tf_op jit(solution)/shard_map/ppermute | solution.py:31
  45.7 5.0 %collective-permute-start.7 = (bf16[16,4224]{1,0:T(8,128)(2,1)S(1)}, bf16[16,4224]{1,0:T(8,128)(2,1)S(1)}, u32[]{:S(2)}, u32[]{:S(2)}) collective-permute-start(bf16[16,4224]{1,0:T(8,128)(2,1)S(1)} %get-tuple-element.21), channel_id=1, source_target_pairs={{0,1},{1,0},{2,3},{3,2},{4,5},{5,4},{6,7},{7,6},{8,9},{9,8},{10,11... | collective-permute-start | bytes 405512 | tf_op jit(solution)/shard_map/ppermute | solution.py:31
  46.0 18.4 %collective-permute-start.10 = (bf16[96,4224]{1,0:T(8,128)(2,1)S(1)}, bf16[96,4224]{1,0:T(8,128)(2,1)S(1)}, u32[]{:S(2)}, u32[]{:S(2)}) collective-permute-start(bf16[96,4224]{1,0:T(8,128)(2,1)S(1)} %pad_maximum_fusion), channel_id=1, source_target_pairs={{0,1},{1,0},{2,3},{3,2},{4,5},{5,4},{6,7},{7,6},{8,9},{9,8},{10,11... | collective-permute-start | bytes 2433032 | tf_op jit(solution)/shard_map/ppermute | solution.py:31
  47.9 16.5 %collective-permute-start.11 = (bf16[96,4224]{1,0:T(8,128)(2,1)S(1)}, bf16[96,4224]{1,0:T(8,128)(2,1)S(1)}, u32[]{:S(2)}, u32[]{:S(2)}) collective-permute-start(bf16[96,4224]{1,0:T(8,128)(2,1)S(1)} %pad_maximum_fusion.1), channel_id=1, source_target_pairs={{0,32},{1,33},{2,34},{3,35},{4,36},{5,37},{6,38},{7,39},{8,40},{9,... | collective-permute-start | bytes 2433032 | tf_op jit(solution)/shard_map/ppermute | solution.py:31
  50.7 12.4 %collective-permute-start.8 = (bf16[32,4224]{1,0:T(8,128)(2,1)S(1)}, bf16[32,4224]{1,0:T(8,128)(2,1)S(1)}, u32[]{:S(2)}, u32[]{:S(2)}) collective-permute-start(bf16[32,4224]{1,0:T(8,128)(2,1)S(1)} %pad_maximum_fusion.5), channel_id=1, source_target_pairs={{0,32},{1,33},{2,34},{3,35},{4,36},{5,37},{6,38},{7,39},{8,40},{9,... | collective-permute-start | bytes 811016 | tf_op jit(solution)/shard_map/ppermute | solution.py:31
  63.9 25.7 %collective-permute-start.9 = (bf16[256,4224]{1,0:T(8,128)(2,1)}, bf16[256,4224]{1,0:T(8,128)(2,1)}, u32[]{:S(2)}, u32[]{:S(2)}) collective-permute-start(bf16[256,4224]{1,0:T(8,128)(2,1)} %constant_dynamic-update-slice_fusion.x_ref), channel_id=1, source_target_pairs={{0,16},{1,17},{2,18},{3,19},{4,20},{5,21},{6,22},{7,23},{8,24},{9,... | collective-permute-start | bytes 6488072 | tf_op jit(solution)/shard_map/ppermute | solution.py:35
  63.9 9.4 %collective-permute-start.12 = (bf16[64,4224]{1,0:T(8,128)(2,1)S(1)}, bf16[64,4224]{1,0:T(8,128)(2,1)S(1)}, u32[]{:S(2)}, u32[]{:S(2)}) collective-permute-start(bf16[64,4224]{1,0:T(8,128)(2,1)S(1)} %pad_maximum_fusion.2), channel_id=1, source_target_pairs={{0,4},{1,5},{2,6},{3,7},{4,0},{5,1},{6,2},{7,3},{8,12},{9,13},{10,... | collective-permute-start | bytes 1622024 | tf_op jit(solution)/shard_map/ppermute | solution.py:31
  73.4 20.9 %collective-permute-start.13 = (bf16[256,4224]{1,0:T(8,128)(2,1)S(1)}, bf16[256,4224]{1,0:T(8,128)(2,1)}, u32[]{:S(2)}, u32[]{:S(2)}) collective-permute-start(bf16[256,4224]{1,0:T(8,128)(2,1)S(1)} %constant_dynamic-update-slice_fusion.9.x_ref), channel_id=1, source_target_pairs={{0,16},{1,17},{2,18},{3,19},{4,20},{5,21},{6,22},{7,23},{8,24},{9,... | collective-permute-start | bytes 6488072 | tf_op jit(solution)/shard_map/ppermute | solution.py:35
  74.9 3.3 %copy-start = (bf16[4096,1002]{0,1:T(8,128)(2,1)S(1)}, bf16[4096,1002]{0,1:T(8,128)(2,1)}, u32[]{:S(2)}) copy-start(bf16[4096,1002]{0,1:T(8,128)(2,1)} %param.7) | copy-start | bytes 24625156
  82.4 0.6 copy-start.2
  83.0 3.3 %copy-start.1 = (bf16[4096,1002]{0,1:T(8,128)(2,1)S(1)}, bf16[4096,1002]{0,1:T(8,128)(2,1)}, u32[]{:S(2)}) copy-start(bf16[4096,1002]{0,1:T(8,128)(2,1)} %param.7) | copy-start | bytes 24625156
  89.0 0.6 copy-start.3
  93.7 0.6 copy-start.4
  98.5 0.6 copy-start.5
  100.7 1.4 %collective-permute-start.14 = (f32[3,8,128]{2,1,0:T(8,128)}, f32[3,8,128]{2,1,0:T(8,128)S(1)}, u32[]{:S(2)}, u32[]{:S(2)}) collective-permute-start(f32[3,8,128]{2,1,0:T(8,128)} %get-tuple-element.5), channel_id=1, source_target_pairs={{0,16},{1,17},{2,18},{3,19},{4,20},{5,21},{6,22},{7,23},{8,24},{9,... | collective-permute-start | bytes 36872 | tf_op jit(solution)/shard_map/ppermute | solution.py:35
  102.8 3.8 %collective-permute-start.15 = (f32[3,8,128]{2,1,0:T(8,128)S(1)}, f32[3,8,128]{2,1,0:T(8,128)S(1)}, u32[]{:S(2)}, u32[]{:S(2)}) collective-permute-start(f32[3,8,128]{2,1,0:T(8,128)S(1)} %pad_maximum_fusion.6), channel_id=1, source_target_pairs={{0,32},{1,33},{2,34},{3,35},{4,36},{5,37},{6,38},{7,39},{8,40},{9,... | collective-permute-start | bytes 36872 | tf_op jit(solution)/shard_map/ppermute | solution.py:31
  106.5 5.0 %collective-permute-start.16 = (f32[3,8,128]{2,1,0:T(8,128)S(1)}, f32[3,8,128]{2,1,0:T(8,128)S(1)}, u32[]{:S(2)}, u32[]{:S(2)}) collective-permute-start(f32[3,8,128]{2,1,0:T(8,128)S(1)} %pad_maximum_fusion.7), channel_id=1, source_target_pairs={{0,96},{1,97},{2,98},{3,99},{4,100},{5,101},{6,102},{7,103},{8,104... | collective-permute-start | bytes 36872 | tf_op jit(solution)/shard_map/ppermute | solution.py:31
  111.6 3.8 %collective-permute-start.17 = (f32[3,8,128]{2,1,0:T(8,128)S(1)}, f32[3,8,128]{2,1,0:T(8,128)S(1)}, u32[]{:S(2)}, u32[]{:S(2)}) collective-permute-start(f32[3,8,128]{2,1,0:T(8,128)S(1)} %pad_maximum_fusion.8), channel_id=1, source_target_pairs={{0,4},{1,5},{2,6},{3,7},{4,0},{5,1},{6,2},{7,3},{8,12},{9,13},{10,... | collective-permute-start | bytes 36872 | tf_op jit(solution)/shard_map/ppermute | solution.py:31
  115.4 5.0 %collective-permute-start.18 = (f32[3,8,128]{2,1,0:T(8,128)S(1)}, f32[3,8,128]{2,1,0:T(8,128)S(1)}, u32[]{:S(2)}, u32[]{:S(2)}) collective-permute-start(f32[3,8,128]{2,1,0:T(8,128)S(1)} %pad_maximum_fusion.9), channel_id=1, source_target_pairs={{0,12},{1,13},{2,14},{3,15},{4,8},{5,9},{6,10},{7,11},{8,4},{9,5},... | collective-permute-start | bytes 36872 | tf_op jit(solution)/shard_map/ppermute | solution.py:31
  120.4 3.8 %collective-permute-start.19 = (f32[3,8,128]{2,1,0:T(8,128)S(1)}, f32[3,8,128]{2,1,0:T(8,128)S(1)}, u32[]{:S(2)}, u32[]{:S(2)}) collective-permute-start(f32[3,8,128]{2,1,0:T(8,128)S(1)} %pad_maximum_fusion.10), channel_id=1, source_target_pairs={{0,1},{1,0},{2,3},{3,2},{4,5},{5,4},{6,7},{7,6},{8,9},{9,8},{10,11... | collective-permute-start | bytes 36872 | tf_op jit(solution)/shard_map/ppermute | solution.py:31
  124.2 5.0 %collective-permute-start.20 = (f32[3,8,128]{2,1,0:T(8,128)S(1)}, f32[3,8,128]{2,1,0:T(8,128)S(1)}, u32[]{:S(2)}, u32[]{:S(2)}) collective-permute-start(f32[3,8,128]{2,1,0:T(8,128)S(1)} %pad_maximum_fusion.11), channel_id=1, source_target_pairs={{0,3},{1,2},{2,1},{3,0},{4,7},{5,6},{6,5},{7,4},{8,11},{9,10},{10,... | collective-permute-start | bytes 36872 | tf_op jit(solution)/shard_map/ppermute | solution.py:31
  130.7 0.5 copy-start.6

commit v2 on v1

v2 whole, which is shorter than its diff:
```python
import jax
import jax.numpy as jnp
from jax import lax
from jax.experimental import pallas as pl
from jax.experimental.pallas import tpu as pltpu
from jax.sharding import Mesh
from jax.sharding import PartitionSpec as P

BENCH = 40
N_DEV = 128
LAB = 128
ROWS = (24, 24, 16)
STARTS = (0, 24, 48)
HALF_STARTS = (0, 96, 192)
F32 = jnp.float32
CHUNK = 256
LIMIT = 12 << 20


def coords(d):
    return (d // 32, (d // 4) % 4, d % 4), (d // 16) % 2


def flipped(d, axis, bit):
    (z, y, x), core = coords(d)
    p = [z, y, x]
    p[axis] = 3 - p[axis] if bit else p[axis] ^ 1
    return ((p[0] * 2 + core) * 4 + p[1]) * 4 + p[2]


def exchange(v, axis, bits):
    pairs = [(d, flipped(d, axis, bits[coords(d)[1]])) for d in range(N_DEV)]
    return lax.ppermute(v, "d", pairs)


def core_swap(v):
    return lax.ppermute(v, "d", [(d, d ^ 16) for d in range(N_DEV)])


def cube_bits(p):
    return (p ^ (p >> 1)) & 1, p >> 1


NT = (((1,), (1,)), ((), ()))
VMEM = pl.BlockSpec(memory_space=pltpu.VMEM)


def iota(shape, dim):
    return lax.broadcasted_iota(jnp.int32, shape, dim)


def as_column(row, n):
    eye = iota((n, n), 0) == iota((n, n), 1)
    return jnp.sum(jnp.where(eye, row, 0.0), axis=1, keepdims=True)


def as_row(column, n):
    eye = iota((n, n), 0) == iota((n, n), 1)
    return jnp.sum(jnp.where(eye, column, 0.0), axis=0, keepdims=True)


def running_sum(row, n):
    upto = jnp.where(iota((n, n), 0) <= iota((n, n), 1), 1.0, 0.0).astype(jnp.bfloat16)
    wide = jnp.broadcast_to(row, (8, n)).astype(jnp.bfloat16)
    return jnp.dot(wide, upto, preferred_element_type=F32)[0:1]


def pack_kernel(hidden_ref, target_ref, bench_ref, valid_ref, length_ref, x_ref, aux_ref):
    rows, depth = hidden_ref.shape
    kept = rows // 2
    seqs = length_ref.shape[1]
    me = lax.axis_index("d")
    ends = running_sum(length_ref[...].astype(F32), seqs).astype(jnp.int32) - 1
    position = me * rows + iota((rows, seqs), 0)
    is_end = jnp.max(jnp.where(ends == position, 1.0, 0.0), axis=1, keepdims=True)
    valid = valid_ref[...].astype(F32)
    rank = running_sum(valid, rows) - 1.0
    token = iota((1, rows), 1).astype(F32)
    count = jnp.sum(valid, axis=1, keepdims=True)
    slot = jnp.where(valid > 0.5, rank, count + token - rank - 1.0)
    selector = jnp.where(iota((kept, rows), 0).astype(F32) == slot, 1.0, 0.0).astype(jnp.bfloat16)
    scored = as_column(valid, rows) * (1.0 - is_end)
    target = target_ref[...]
    digits = [target >> 16, (target >> 8) & 255, target & 255, bench_ref[...]]
    lane = iota((rows, LAB), 1)
    labels = jnp.where(lane == 4, scored, 0.0)
    for k, digit in enumerate(digits):
        labels = jnp.where(lane == k, as_column(digit.astype(F32), rows), labels)
    x_ref[:, :depth] = jnp.dot(
        selector, hidden_ref[...], preferred_element_type=F32
    ).astype(jnp.bfloat16)
    x_ref[:, depth:] = jnp.dot(
        selector, labels.astype(jnp.bfloat16), preferred_element_type=F32
    ).astype(jnp.bfloat16)
    aux_ref[...] = jnp.where(lane == 0, as_column(slot, rows), jnp.where(lane == 1, scored, 0.0))


def pack(hidden, *ints):
    rows, depth = hidden.shape
    return pl.pallas_call(
        pack_kernel,
        out_shape=(
            jax.ShapeDtypeStruct((rows // 2, depth + LAB), jnp.bfloat16),
            jax.ShapeDtypeStruct((rows, LAB), F32),
        ),
        in_specs=[VMEM] * 5,
        out_specs=(VMEM, VMEM),
        compiler_params=pltpu.CompilerParams(vmem_limit_bytes=4 << 20),
        name="pack",
    )(hidden, *(v.reshape(1, -1) for v in ints))


def scores(x_ref, at, w_ref, acc_ref):
    vocab, depth = w_ref.shape
    r, c = iota((8, LAB), 0), iota((8, LAB), 1)
    digit = jnp.where(c == 0, 65536.0, jnp.where(c == 1, 256.0, 1.0))
    sel = jnp.where((r == 5) & (c < 3), digit, jnp.where(((r == 3) | (r == 4)) & (r == c), 1.0, 0.0))
    rows = pl.ds(at, CHUNK)
    labels = lax.dot_general(
        sel.astype(jnp.bfloat16), x_ref[rows, depth:], NT, preferred_element_type=F32
    )
    acc_ref[...] = lax.dot_general(w_ref[...], x_ref[rows, :depth], NT, preferred_element_type=F32)
    logits = acc_ref[...]
    top = jnp.max(logits, axis=0, keepdims=True)
    total = jnp.sum(jnp.exp(logits - top), axis=0, keepdims=True)
    local = labels[5:6].astype(jnp.int32) - lax.axis_index("d") * vocab
    target = jnp.sum(jnp.where(iota(logits.shape, 0) == local, logits, 0.0), axis=0, keepdims=True)
    k = iota((8, CHUNK), 0)
    return jnp.where(k == 0, top, jnp.where(k == 1, total, jnp.where(k == 2, target, labels)))


def gather_rows(pieces, x_ref):
    at = 0
    for piece in pieces:
        x_ref[at : at + piece.shape[0], :] = piece[...]
        at += piece.shape[0]


def score_kernel(w_ref, *refs):
    *pieces, out_ref, x_ref, acc_ref = refs
    gather_rows(pieces, x_ref)
    for at in range(0, x_ref.shape[0], CHUNK):
        out_ref[:, at : at + CHUNK] = scores(x_ref, at, w_ref, acc_ref)


def score(w, pieces):
    vocab, depth = w.shape
    rows = sum(p.shape[0] for p in pieces)
    return pl.pallas_call(
        score_kernel,
        out_shape=jax.ShapeDtypeStruct((8, rows), F32),
        in_specs=[VMEM] * (1 + len(pieces)),
        out_specs=VMEM,
        scratch_shapes=[
            pltpu.VMEM((rows, depth + LAB), jnp.bfloat16),
            pltpu.VMEM((vocab, CHUNK), F32),
        ],
        compiler_params=pltpu.CompilerParams(vmem_limit_bytes=LIMIT),
        cost_estimate=pl.CostEstimate(
            flops=2 * rows * vocab * depth, bytes_accessed=2 * vocab * depth, transcendentals=rows * vocab
        ),
        name="score",
    )(w, *pieces)


def score_place_kernel(w_ref, first_ref, own_ref, *refs):
    *pieces, stats_ref, labels_ref, x_ref, acc_ref, all_ref = refs
    gather_rows(pieces, x_ref)
    sib = scores(x_ref, 0, w_ref, acc_ref)
    place_of, core = coords(lax.axis_index("d"))
    bits = [cube_bits(p) for p in place_of]
    blocks = [sum(b[k] << axis for axis, b in enumerate(bits)) for k in range(2)]
    is_first = core == 0
    halves = ((first_ref[:, :CHUNK], first_ref[:, CHUNK:]), (own_ref[...], sib))
    for half, (a, b) in enumerate(halves):
        by_core = (jnp.where(is_first, a, b), jnp.where(is_first, b, a))
        for g in range(3):
            for i in range(4):
                r = 4 * half + i
                rel = sum(((r >> k) & 1) << ((g + k) % 3) for k in range(3))
                at = HALF_STARTS[g] + i * ROWS[g]
                for side in range(2):
                    to = side * 64 + STARTS[g]
                    all_ref[blocks[side] ^ rel, :, to : to + ROWS[g]] = by_core[side][:, at : at + ROWS[g]]
    for kind in range(3):
        stats_ref[kind] = all_ref[:, kind, :]
    for kind in range(2):
        labels_ref[kind] = all_ref[:, 3 + kind, :]


def score_place(w, first, own, pieces):
    vocab, depth = w.shape
    rows = sum(p.shape[0] for p in pieces)
    return pl.pallas_call(
        score_place_kernel,
        out_shape=(jax.ShapeDtypeStruct((3, 8, 128), F32), jax.ShapeDtypeStruct((2, 8, 128), F32)),
        in_specs=[VMEM] * (3 + len(pieces)),
        out_specs=(VMEM, VMEM),
        scratch_shapes=[
            pltpu.VMEM((rows, depth + LAB), jnp.bfloat16),
            pltpu.VMEM((vocab, CHUNK), F32),
            pltpu.VMEM((8, 8, 128), F32),
        ],
        compiler_params=pltpu.CompilerParams(vmem_limit_bytes=LIMIT),
        cost_estimate=pl.CostEstimate(
            flops=2 * rows * vocab * depth, bytes_accessed=2 * vocab * depth, transcendentals=rows * vocab
        ),
        name="score_place",
    )(w, first, own, *pieces)


def merged(a, b):
    best = jnp.maximum(a[0], b[0])
    total = a[1] * jnp.exp(a[0] - best) + b[1] * jnp.exp(b[0] - best)
    return best, total, a[2] + b[2]


def final_kernel(mine_ref, got_ref, labels_ref, aux_ref, loss_ref, mean_ref, count_ref, all_ref):
    best, total, target = merged(mine_ref, got_ref)
    losses = best + jnp.log(total) - target
    all_ref[...] = losses
    rows = aux_ref.shape[0]
    place_of, core = coords(lax.axis_index("d"))
    bits = [cube_bits(p) for p in place_of]
    is_first = core == 0
    block = sum(jnp.where(is_first, b[0], b[1]) << axis for axis, b in enumerate(bits))
    base = core * 64 + 8 * sum(jnp.where(is_first, b[1], b[0]) << axis for axis, b in enumerate(bits))
    mine = all_ref[pl.ds(block, 1), :]
    hit = iota((rows, LAB), 1) == base + aux_ref[:, 0:1].astype(jnp.int32)
    column = jnp.sum(jnp.where(hit, mine, 0.0), axis=1, keepdims=True)
    loss_ref[...] = as_row(column * aux_ref[:, 1:2], rows)
    bench, scored = labels_ref[0], labels_ref[1]
    kept = losses * scored
    ids = iota((BENCH, LAB), 0).astype(F32)
    sums, counts = jnp.zeros((BENCH, LAB), F32), jnp.zeros((BENCH, LAB), F32)
    for k in range(8):
        same = ids == bench[k : k + 1]
        sums += jnp.where(same, kept[k : k + 1], 0.0)
        counts += jnp.where(same, scored[k : k + 1], 0.0)
    sums = as_row(jnp.sum(sums, axis=1, keepdims=True), BENCH)
    counts = as_row(jnp.sum(counts, axis=1, keepdims=True), BENCH)
    mean_ref[...] = sums / jnp.maximum(counts, 1.0)
    count_ref[...] = counts


def final(mine, got, labels, aux):
    rows = aux.shape[0]
    outs = pl.pallas_call(
        final_kernel,
        out_shape=tuple(jax.ShapeDtypeStruct((1, n), F32) for n in (rows, BENCH, BENCH)),
        in_specs=[VMEM] * 4,
        out_specs=(VMEM,) * 3,
        scratch_shapes=[pltpu.VMEM((8, LAB), F32)],
        compiler_params=pltpu.CompilerParams(vmem_limit_bytes=4 << 20),
        name="final",
    )(mine, got, labels, aux)
    return tuple(v.reshape(-1) for v in outs)


def tied(*arrays):
    return lax.optimization_barrier(arrays)


def body(hidden, head_weight, targets, bench_ids, valid, seq_lengths):
    me = lax.axis_index("d")
    place_of, core = coords(me)
    early = [jnp.where(core == 0, b[1], b[0]) for b in map(cube_bits, place_of)]
    x, aux = pack(hidden, targets, bench_ids, valid, seq_lengths)
    for axis in range(3):
        got = exchange(x, axis, (1, 0))
        x = jnp.where(
            early[axis] == 0, jnp.concatenate([x, got], 0), jnp.concatenate([got, x], 0)
        )
    held = [x[s : s + n] for s, n in zip(STARTS, ROWS)]
    for k in range(2):
        held = tied(*held)
        got = [exchange(held[g], (g + k) % 3, (0, 1)) for g in range(3)]
        held = [jnp.concatenate([a, b], 0) for a, b in zip(held, got)]
    held = tied(*held)
    w = head_weight.T
    last = [exchange(held[g], (g + 2) % 3, (0, 1)) for g in range(3)]
    first = score(w, [*held, core_swap(jnp.concatenate(held, 0))])
    *last, first = tied(*last, first)
    other = core_swap(jnp.concatenate(last, 0))
    own = score(w, last)
    stats, labels = score_place(w, first, own, [other])
    for axis, bits in [(0, None), *((a, (b, b)) for a in range(3) for b in range(2))]:
        got = core_swap(stats) if bits is None else exchange(stats, axis, bits)
        if (axis, bits) != (2, (1, 1)):
            stats = jnp.stack(merged(stats, got))
    return final(stats, got, labels, aux)


def solution(mesh):
    flat = Mesh(mesh.devices.reshape(-1), ("d",))
    in_specs = (P("d", None), P(None, "d"), P("d"), P("d"), P("d"), P())
    return jax.shard_map(
        body, mesh=flat, in_specs=in_specs, out_specs=(P("d"), P(), P()), check_vma=False
    )
```

time: 132 us -> 94.7 us (0.72)
  waiting for transfers between devices: 62.6 us -> 47.3 us
  local copies, waits for them, and re-layouts: 16.5 us -> 3.56 us
  other arithmetic: 8.87 us -> 0.8 us
  starting transfers between devices: 24.7 us -> 30.8 us
  Pallas kernels: 16.7 us -> 11.3 us
    ppermute x18, waiting for transfers between devices: 61.2 us -> 44.1 us  [exchange(): return lax.ppermute(v, 'd', pairs)]
    unnamed x22 -> x12, local copies, waits for them, and re-layouts: 13.6 us -> 3.52 us
    pallas_call x4 -> x2, Pallas kernels: 15.1 us -> 7.51 us  [score(): pl.pallas_call(score_kernel, out_shape=jax.ShapeDtypeStruct((8, rows), F3...]
    ppermute x18, starting transfers between devices: 23.8 us -> 28.5 us  [exchange(): return lax.ppermute(v, 'd', pairs)]
    reduce_sum x5 -> x0, other arithmetic: 3.06 us -> none  [the longest x1 1.3 us: body(): jnp.sum(valid) + token - valid_rank - 1]
    pallas_call x1 -> x3, Pallas kernels: 1.53 us -> 3.77 us  [the longest x1 2.69 us: score_place(): pl.pallas_call(score_place_kernel, out_shape=(jax.ShapeDtypeStruct((3, 8,...]
    ppermute x3, waiting for transfers between devices: 1.34 us -> 3.17 us  [core_swap(): return lax.ppermute(v, 'd', [(d, d ^ 16) for d in range(N_DEV)])]
    slice x2, local copies, waits for them, and re-layouts: 1.39 us -> 0.04 us  [body(): held = [x[s:s + n] for s, n in zip(STARTS, ROWS)]]
  transfers between devices with their start and end apart: 21 -> 21, of which waited for: 15 -> 21; matrix products, arithmetic and copies ran while one was open for 5% -> 0% of each run, Pallas kernels for 8% -> 8%
where the time goes in v2:
time: 94.7 us; the launch traced here: 94.5 us
  waiting for transfers between devices  47.3 us (50%)
  starting transfers between devices  30.8 us (33%)
  Pallas kernels  11.3 us (12%)
  local copies, waits for them, and re-layouts  3.56 us (4%)
    ppermute x18, waiting for transfers between devices, exchange(): return lax.ppermute(v, 'd', pairs)  44.1 us
    ppermute x18, starting transfers between devices, exchange(): return lax.ppermute(v, 'd', pairs)  28.5 us
    pallas_call x2, Pallas kernels, score(): pl.pallas_call(score_kernel, out_shape=jax.ShapeDtypeStruct((8, rows), F3...  7.51 us
    unnamed x12, local copies, waits for them, and re-layouts  3.52 us
    ppermute x3, waiting for transfers between devices, core_swap(): return lax.ppermute(v, 'd', [(d, d ^ 16) for d in range(N_DEV)])  3.17 us
    pallas_call x1, Pallas kernels, score_place(): pl.pallas_call(score_place_kernel, out_shape=(jax.ShapeDtypeStruct((3, 8,...  2.69 us
    ppermute x3, starting transfers between devices, core_swap(): return lax.ppermute(v, 'd', [(d, d ^ 16) for d in range(N_DEV)])  2.3 us
  transfers between devices with their start and end apart: 21, of which 21 were waited for; matrix products, arithmetic and copies ran while one was open for 0% of the time, Pallas kernels for 8%

profile of v2, /device:TPU:0, one launch (start us, length us, event | category | flops | bytes accessed | tf_op | source)
XLA Modules:
  0.0 94.5 jit_solution(14021677548024441871)
XLA Ops:
  4.5 4.2 %collective-permute-start = (bf16[8,4224]{1,0:T(8,128)(2,1)S(1)}, bf16[8,4224]{1,0:T(8,128)(2,1)S(1)}, u32[]{:S(2)}, u32[]{:S(2)}) collective-permute-start(bf16[8,4224]{1,0:T(8,128)(2,1)S(1)} %get-tuple-element.23), channel_id=1, source_target_pairs={{0,96},{1,97},{2,98},{3,99},{4,100},{5,101},{6,102},{7,103},{8,104... | collective-permute-start | bytes 202760 | tf_op jit(solution)/shard_map/ppermute | solution.py:33
  8.6 2.3 %collective-permute-done = bf16[8,4224]{1,0:T(8,128)(2,1)S(1)} collective-permute-done((bf16[8,4224]{1,0:T(8,128)(2,1)S(1)}, bf16[8,4224]{1,0:T(8,128)(2,1)S(1)}, u32[]{:S(2)}, u32[]{:S(2)}) %collective-permute-start) | collective-permute-done | bytes 67616 | tf_op jit(solution)/shard_map/ppermute | solution.py:33
  10.9 3.1 %collective-permute-start.1 = (bf16[16,4224]{1,0:T(8,128)(2,1)S(1)}, bf16[16,4224]{1,0:T(8,128)(2,1)S(1)}, u32[]{:S(2)}, u32[]{:S(2)}) collective-permute-start(bf16[16,4224]{1,0:T(8,128)(2,1)S(1)} %maximum_select_fusion.2), channel_id=1, source_target_pairs={{0,12},{1,13},{2,14},{3,15},{4,8},{5,9},{6,10},{7,11},{8,4},{9,5},... | collective-permute-start | bytes 405512 | tf_op jit(solution)/shard_map/ppermute | solution.py:33
  14.0 3.2 %collective-permute-done.1 = bf16[16,4224]{1,0:T(8,128)(2,1)S(1)} collective-permute-done((bf16[16,4224]{1,0:T(8,128)(2,1)S(1)}, bf16[16,4224]{1,0:T(8,128)(2,1)S(1)}, u32[]{:S(2)}, u32[]{:S(2)}) %collective-permute-start.1) | collective-permute-done | bytes 135200 | tf_op jit(solution)/shard_map/ppermute | solution.py:33
  17.3 2.8 %collective-permute-start.2 = (bf16[32,4224]{1,0:T(8,128)(2,1)S(1)}, bf16[32,4224]{1,0:T(8,128)(2,1)S(1)}, u32[]{:S(2)}, u32[]{:S(2)}) collective-permute-start(bf16[32,4224]{1,0:T(8,128)(2,1)S(1)} %maximum_select_fusion.1), channel_id=1, source_target_pairs={{0,3},{1,2},{2,1},{3,0},{4,7},{5,6},{6,5},{7,4},{8,11},{9,10},{10,... | collective-permute-start | bytes 811016 | tf_op jit(solution)/shard_map/ppermute | solution.py:33
  20.1 5.6 %collective-permute-done.2 = bf16[32,4224]{1,0:T(8,128)(2,1)S(1)} collective-permute-done((bf16[32,4224]{1,0:T(8,128)(2,1)S(1)}, bf16[32,4224]{1,0:T(8,128)(2,1)S(1)}, u32[]{:S(2)}, u32[]{:S(2)}) %collective-permute-start.2) | collective-permute-done | bytes 270368 | tf_op jit(solution)/shard_map/ppermute | solution.py:33
  26.3 1.1 %collective-permute-start.4 = (bf16[24,4224]{1,0:T(8,128)(2,1)S(1)}, bf16[24,4224]{1,0:T(8,128)(2,1)S(1)}, u32[]{:S(2)}, u32[]{:S(2)}) collective-permute-start(bf16[24,4224]{1,0:T(8,128)(2,1)S(1)} %get-tuple-element.25), channel_id=1, source_target_pairs={{0,4},{1,5},{2,6},{3,7},{4,0},{5,1},{6,2},{7,3},{8,12},{9,13},{10,... | collective-permute-start | bytes 608264 | tf_op jit(solution)/shard_map/ppermute | solution.py:33
  27.4 3.6 %collective-permute-done.5 = bf16[16,4224]{1,0:T(8,128)(2,1)S(1)} collective-permute-done((bf16[16,4224]{1,0:T(8,128)(2,1)S(1)}, bf16[16,4224]{1,0:T(8,128)(2,1)S(1)}, u32[]{:S(2)}, u32[]{:S(2)}) %collective-permute-start.5) | collective-permute-done | bytes 135200 | tf_op jit(solution)/shard_map/ppermute | solution.py:33
  33.2 1.8 %collective-permute-start.7 = (bf16[48,4224]{1,0:T(8,128)(2,1)S(1)}, bf16[48,4224]{1,0:T(8,128)(2,1)S(1)}, u32[]{:S(2)}, u32[]{:S(2)}) collective-permute-start(bf16[48,4224]{1,0:T(8,128)(2,1)S(1)} %pad_maximum_fusion.6), channel_id=1, source_target_pairs={{0,1},{1,0},{2,3},{3,2},{4,5},{5,4},{6,7},{7,6},{8,9},{9,8},{10,11... | collective-permute-start | bytes 1216520 | tf_op jit(solution)/shard_map/ppermute | solution.py:33
  35.1 1.5 %collective-permute-start.6 = (bf16[48,4224]{1,0:T(8,128)(2,1)S(1)}, bf16[48,4224]{1,0:T(8,128)(2,1)S(1)}, u32[]{:S(2)}, u32[]{:S(2)}) collective-permute-start(bf16[48,4224]{1,0:T(8,128)(2,1)S(1)} %pad_maximum_fusion.5), channel_id=1, source_target_pairs={{0,4},{1,5},{2,6},{3,7},{4,0},{5,1},{6,2},{7,3},{8,12},{9,13},{10,... | collective-permute-start | bytes 1216520 | tf_op jit(solution)/shard_map/ppermute | solution.py:33
  36.5 3.2 %collective-permute-done.8 = bf16[32,4224]{1,0:T(8,128)(2,1)S(1)} collective-permute-done((bf16[32,4224]{1,0:T(8,128)(2,1)S(1)}, bf16[32,4224]{1,0:T(8,128)(2,1)S(1)}, u32[]{:S(2)}, u32[]{:S(2)}) %collective-permute-start.8) | collective-permute-done | bytes 270368 | tf_op jit(solution)/shard_map/ppermute | solution.py:33
  39.7 1.5 %collective-permute-done.7 = bf16[48,4224]{1,0:T(8,128)(2,1)S(1)} collective-permute-done((bf16[48,4224]{1,0:T(8,128)(2,1)S(1)}, bf16[48,4224]{1,0:T(8,128)(2,1)S(1)}, u32[]{:S(2)}, u32[]{:S(2)}) %collective-permute-start.7) | collective-permute-done | bytes 405536 | tf_op jit(solution)/shard_map/ppermute | solution.py:33
  41.3 1.7 %collective-permute-done.6 = bf16[48,4224]{1,0:T(8,128)(2,1)S(1)} collective-permute-done((bf16[48,4224]{1,0:T(8,128)(2,1)S(1)}, bf16[48,4224]{1,0:T(8,128)(2,1)S(1)}, u32[]{:S(2)}, u32[]{:S(2)}) %collective-permute-start.6) | collective-permute-done | bytes 405536 | tf_op jit(solution)/shard_map/ppermute | solution.py:33
  43.3 2.0 %collective-permute-start.10 = (bf16[96,4224]{1,0:T(8,128)(2,1)S(1)}, bf16[96,4224]{1,0:T(8,128)(2,1)S(1)}, u32[]{:S(2)}, u32[]{:S(2)}) collective-permute-start(bf16[96,4224]{1,0:T(8,128)(2,1)S(1)} %pad_maximum_fusion.3.refs_1_), channel_id=1, source_target_pairs={{0,32},{1,33},{2,34},{3,35},{4,36},{5,37},{6,38},{7,39},{8,40},{9,... | collective-permute-start | bytes 2433032 | tf_op jit(solution)/shard_map/ppermute | solution.py:33
  47.5 4.9 %score.2.first_ref = f32[8,512]{1,0:T(8,128)S(1)} custom-call(bf16[1002,4096]{1,0:T(8,128)(2,1)S(1)} %bitcast.8, bf16[96,4224]{1,0:T(8,128)(2,1)S(1)} %pad_maximum_fusion.2.refs_0_, bf16[96,4224]{1,0:T(8,128)(2,1)S(1)} %pad_maximum_fusion.3.refs_1_, bf16[64,4224]{1,0:T(8,128)(2,1)S(1)} %pad_maximum_fusion.4.refs_2_, ...), custom_call_target="tpu_custom_call" | custom-call | flops 4202692608 | bytes 8208384 | tf_op jit(solution)/shard_map/score/pallas_call | solution.py:149
  52.5 2.5 %collective-permute-done.11.refs_2_ = bf16[64,4224]{1,0:T(8,128)(2,1)S(1)} collective-permute-done((bf16[64,4224]{1,0:T(8,128)(2,1)S(1)}, bf16[64,4224]{1,0:T(8,128)(2,1)S(1)}, u32[]{:S(2)}, u32[]{:S(2)}) %collective-permute-start.11) | collective-permute-done | bytes 540704 | tf_op jit(solution)/shard_map/ppermute | solution.py:33
  55.6 1.9 %collective-permute-done.9.refs_0_ = bf16[96,4224]{1,0:T(8,128)(2,1)S(1)} collective-permute-done((bf16[96,4224]{1,0:T(8,128)(2,1)S(1)}, bf16[96,4224]{1,0:T(8,128)(2,1)S(1)}, u32[]{:S(2)}, u32[]{:S(2)}) %collective-permute-start.9) | collective-permute-done | bytes 811040 | tf_op jit(solution)/shard_map/ppermute | solution.py:33
  57.7 1.8 %collective-permute-start.13 = (bf16[256,4224]{1,0:T(8,128)(2,1)S(1)}, bf16[256,4224]{1,0:T(8,128)(2,1)S(1)}, u32[]{:S(2)}, u32[]{:S(2)}) collective-permute-start(bf16[256,4224]{1,0:T(8,128)(2,1)S(1)} %pad_maximum_fusion.1), channel_id=1, source_target_pairs={{0,16},{1,17},{2,18},{3,19},{4,20},{5,21},{6,22},{7,23},{8,24},{9,... | collective-permute-start | bytes 6488072 | tf_op jit(solution)/shard_map/ppermute | solution.py:37
  59.5 2.6 %score.3.own_ref = f32[8,256]{1,0:T(8,128)S(1)} custom-call(bf16[1002,4096]{1,0:T(8,128)(2,1)S(1)} %bitcast.9, bf16[96,4224]{1,0:T(8,128)(2,1)S(1)} %collective-permute-done.9.refs_0_, bf16[96,4224]{1,0:T(8,128)(2,1)S(1)} %collective-permute-done.10.refs_1_, bf16[64,4224]{1,0:T(8,128)(2,1)S(1)} %collective-permute-done.11.refs_2_), custom_call_target="tpu_custom_call" | custom-call | flops 2101346304 | bytes 8208384 | tf_op jit(solution)/shard_map/score/pallas_call | solution.py:149
  62.0 1.3 %collective-permute-done.13.refs_0_ = bf16[256,4224]{1,0:T(8,128)(2,1)S(1)} collective-permute-done((bf16[256,4224]{1,0:T(8,128)(2,1)S(1)}, bf16[256,4224]{1,0:T(8,128)(2,1)S(1)}, u32[]{:S(2)}, u32[]{:S(2)}) %collective-permute-start.13) | collective-permute-done | bytes 2162720 | tf_op jit(solution)/shard_map/ppermute | solution.py:37
  63.3 2.7 %score_place.1 = (f32[3,8,128]{2,1,0:T(8,128)S(1)}, f32[2,8,128]{2,1,0:T(8,128)S(1)}) custom-call(bf16[1002,4096]{1,0:T(8,128)(2,1)S(1)} %bitcast.10, f32[8,512]{1,0:T(8,128)S(1)} %score.2.first_ref, f32[8,256]{1,0:T(8,128)S(1)} %score.3.own_ref, bf16[256,4224]{1,0:T(8,128)(2,1)S(1)} %collective-permute-done.13.refs_0_), custom_call_target="tpu_custom_call" | custom-call | flops 2101346304 | bytes 8208384 | tf_op jit(solution)/shard_map/score_place/pallas_call | solution.py:194
  67.3 1.4 %collective-permute-start.15 = (f32[3,8,128]{2,1,0:T(8,128)S(1)}, f32[3,8,128]{2,1,0:T(8,128)S(1)}, u32[]{:S(2)}, u32[]{:S(2)}) collective-permute-start(f32[3,8,128]{2,1,0:T(8,128)S(1)} %pad_maximum_fusion.8), channel_id=1, source_target_pairs={{0,32},{1,33},{2,34},{3,35},{4,36},{5,37},{6,38},{7,39},{8,40},{9,... | collective-permute-start | bytes 36872 | tf_op jit(solution)/shard_map/ppermute | solution.py:33
  68.7 2.4 %collective-permute-done.15 = f32[3,8,128]{2,1,0:T(8,128)S(1)} collective-permute-done((f32[3,8,128]{2,1,0:T(8,128)S(1)}, f32[3,8,128]{2,1,0:T(8,128)S(1)}, u32[]{:S(2)}, u32[]{:S(2)}) %collective-permute-start.15) | collective-permute-done | bytes 12320 | tf_op jit(solution)/shard_map/ppermute | solution.py:33
  71.1 2.2 %collective-permute-start.16 = (f32[3,8,128]{2,1,0:T(8,128)S(1)}, f32[3,8,128]{2,1,0:T(8,128)S(1)}, u32[]{:S(2)}, u32[]{:S(2)}) collective-permute-start(f32[3,8,128]{2,1,0:T(8,128)S(1)} %pad_maximum_fusion.9), channel_id=1, source_target_pairs={{0,96},{1,97},{2,98},{3,99},{4,100},{5,101},{6,102},{7,103},{8,104... | collective-permute-start | bytes 36872 | tf_op jit(solution)/shard_map/ppermute | solution.py:33
  73.3 2.8 %collective-permute-done.16 = f32[3,8,128]{2,1,0:T(8,128)S(1)} collective-permute-done((f32[3,8,128]{2,1,0:T(8,128)S(1)}, f32[3,8,128]{2,1,0:T(8,128)S(1)}, u32[]{:S(2)}, u32[]{:S(2)}) %collective-permute-start.16) | collective-permute-done | bytes 12320 | tf_op jit(solution)/shard_map/ppermute | solution.py:33
  76.2 1.4 %collective-permute-start.17 = (f32[3,8,128]{2,1,0:T(8,128)S(1)}, f32[3,8,128]{2,1,0:T(8,128)S(1)}, u32[]{:S(2)}, u32[]{:S(2)}) collective-permute-start(f32[3,8,128]{2,1,0:T(8,128)S(1)} %pad_maximum_fusion.10), channel_id=1, source_target_pairs={{0,4},{1,5},{2,6},{3,7},{4,0},{5,1},{6,2},{7,3},{8,12},{9,13},{10,... | collective-permute-start | bytes 36872 | tf_op jit(solution)/shard_map/ppermute | solution.py:33
  77.6 2.4 %collective-permute-done.17 = f32[3,8,128]{2,1,0:T(8,128)S(1)} collective-permute-done((f32[3,8,128]{2,1,0:T(8,128)S(1)}, f32[3,8,128]{2,1,0:T(8,128)S(1)}, u32[]{:S(2)}, u32[]{:S(2)}) %collective-permute-start.17) | collective-permute-done | bytes 12320 | tf_op jit(solution)/shard_map/ppermute | solution.py:33
  80.0 2.5 %collective-permute-start.18 = (f32[3,8,128]{2,1,0:T(8,128)S(1)}, f32[3,8,128]{2,1,0:T(8,128)S(1)}, u32[]{:S(2)}, u32[]{:S(2)}) collective-permute-start(f32[3,8,128]{2,1,0:T(8,128)S(1)} %pad_maximum_fusion.11), channel_id=1, source_target_pairs={{0,12},{1,13},{2,14},{3,15},{4,8},{5,9},{6,10},{7,11},{8,4},{9,5},... | collective-permute-start | bytes 36872 | tf_op jit(solution)/shard_map/ppermute | solution.py:33
  82.4 2.5 %collective-permute-done.18 = f32[3,8,128]{2,1,0:T(8,128)S(1)} collective-permute-done((f32[3,8,128]{2,1,0:T(8,128)S(1)}, f32[3,8,128]{2,1,0:T(8,128)S(1)}, u32[]{:S(2)}, u32[]{:S(2)}) %collective-permute-start.18) | collective-permute-done | bytes 12320 | tf_op jit(solution)/shard_map/ppermute | solution.py:33
  85.1 3.7 %collective-permute-done.19 = f32[3,8,128]{2,1,0:T(8,128)S(1)} collective-permute-done((f32[3,8,128]{2,1,0:T(8,128)S(1)}, f32[3,8,128]{2,1,0:T(8,128)S(1)}, u32[]{:S(2)}, u32[]{:S(2)}) %collective-permute-start.19) | collective-permute-done | bytes 12320 | tf_op jit(solution)/shard_map/ppermute | solution.py:33
  88.8 2.8 %collective-permute-start.20 = (f32[3,8,128]{2,1,0:T(8,128)S(1)}, f32[3,8,128]{2,1,0:T(8,128)S(1)}, u32[]{:S(2)}, u32[]{:S(2)}) collective-permute-start(f32[3,8,128]{2,1,0:T(8,128)S(1)} %pad_maximum_fusion.13.mine_ref), channel_id=1, source_target_pairs={{0,3},{1,2},{2,1},{3,0},{4,7},{5,6},{6,5},{7,4},{8,11},{9,10},{10,... | collective-permute-start | bytes 36872 | tf_op jit(solution)/shard_map/ppermute | solution.py:33
  91.6 2.2 %collective-permute-done.20.got_ref = f32[3,8,128]{2,1,0:T(8,128)S(1)} collective-permute-done((f32[3,8,128]{2,1,0:T(8,128)S(1)}, f32[3,8,128]{2,1,0:T(8,128)S(1)}, u32[]{:S(2)}, u32[]{:S(2)}) %collective-permute-start.20) | collective-permute-done | bytes 12320 | tf_op jit(solution)/shard_map/ppermute | solution.py:33
  (52 shorter events, 12.3 us)
Async XLA Ops:
  0.6 0.9 copy-start.1
  1.5 0.7 copy-start.2
  2.2 0.7 copy-start.3
  2.8 0.7 copy-start.4
  3.5 0.7 copy-start.5
  4.5 6.4 %collective-permute-start = (bf16[8,4224]{1,0:T(8,128)(2,1)S(1)}, bf16[8,4224]{1,0:T(8,128)(2,1)S(1)}, u32[]{:S(2)}, u32[]{:S(2)}) collective-permute-start(bf16[8,4224]{1,0:T(8,128)(2,1)S(1)} %get-tuple-element.23), channel_id=1, source_target_pairs={{0,96},{1,97},{2,98},{3,99},{4,100},{5,101},{6,102},{7,103},{8,104... | collective-permute-start | bytes 202760 | tf_op jit(solution)/shard_map/ppermute | solution.py:33
  10.9 6.3 %collective-permute-start.1 = (bf16[16,4224]{1,0:T(8,128)(2,1)S(1)}, bf16[16,4224]{1,0:T(8,128)(2,1)S(1)}, u32[]{:S(2)}, u32[]{:S(2)}) collective-permute-start(bf16[16,4224]{1,0:T(8,128)(2,1)S(1)} %maximum_select_fusion.2), channel_id=1, source_target_pairs={{0,12},{1,13},{2,14},{3,15},{4,8},{5,9},{6,10},{7,11},{8,4},{9,5},... | collective-permute-start | bytes 405512 | tf_op jit(solution)/shard_map/ppermute | solution.py:33
  17.3 8.4 %collective-permute-start.2 = (bf16[32,4224]{1,0:T(8,128)(2,1)S(1)}, bf16[32,4224]{1,0:T(8,128)(2,1)S(1)}, u32[]{:S(2)}, u32[]{:S(2)}) collective-permute-start(bf16[32,4224]{1,0:T(8,128)(2,1)S(1)} %maximum_select_fusion.1), channel_id=1, source_target_pairs={{0,3},{1,2},{2,1},{3,0},{4,7},{5,6},{6,5},{7,4},{8,11},{9,10},{10,... | collective-permute-start | bytes 811016 | tf_op jit(solution)/shard_map/ppermute | solution.py:33
  25.9 5.1 %collective-permute-start.5 = (bf16[16,4224]{1,0:T(8,128)(2,1)S(1)}, bf16[16,4224]{1,0:T(8,128)(2,1)S(1)}, u32[]{:S(2)}, u32[]{:S(2)}) collective-permute-start(bf16[16,4224]{1,0:T(8,128)(2,1)S(1)} %slice.105), channel_id=1, source_target_pairs={{0,1},{1,0},{2,3},{3,2},{4,5},{5,4},{6,7},{7,6},{8,9},{9,8},{10,11... | collective-permute-start | bytes 405512 | tf_op jit(solution)/shard_map/ppermute | solution.py:33
  26.3 5.7 %collective-permute-start.4 = (bf16[24,4224]{1,0:T(8,128)(2,1)S(1)}, bf16[24,4224]{1,0:T(8,128)(2,1)S(1)}, u32[]{:S(2)}, u32[]{:S(2)}) collective-permute-start(bf16[24,4224]{1,0:T(8,128)(2,1)S(1)} %get-tuple-element.25), channel_id=1, source_target_pairs={{0,4},{1,5},{2,6},{3,7},{4,0},{5,1},{6,2},{7,3},{8,12},{9,13},{10,... | collective-permute-start | bytes 608264 | tf_op jit(solution)/shard_map/ppermute | solution.py:33
  27.4 5.7 %collective-permute-start.3 = (bf16[24,4224]{1,0:T(8,128)(2,1)S(1)}, bf16[24,4224]{1,0:T(8,128)(2,1)S(1)}, u32[]{:S(2)}, u32[]{:S(2)}) collective-permute-start(bf16[24,4224]{1,0:T(8,128)(2,1)S(1)} %get-tuple-element.24), channel_id=1, source_target_pairs={{0,32},{1,33},{2,34},{3,35},{4,36},{5,37},{6,38},{7,39},{8,40},{9,... | collective-permute-start | bytes 608264 | tf_op jit(solution)/shard_map/ppermute | solution.py:33
  33.1 6.5 %collective-permute-start.8 = (bf16[32,4224]{1,0:T(8,128)(2,1)S(1)}, bf16[32,4224]{1,0:T(8,128)(2,1)S(1)}, u32[]{:S(2)}, u32[]{:S(2)}) collective-permute-start(bf16[32,4224]{1,0:T(8,128)(2,1)S(1)} %pad_maximum_fusion.7), channel_id=1, source_target_pairs={{0,32},{1,33},{2,34},{3,35},{4,36},{5,37},{6,38},{7,39},{8,40},{9,... | collective-permute-start | bytes 811016 | tf_op jit(solution)/shard_map/ppermute | solution.py:33
  33.2 8.0 %collective-permute-start.7 = (bf16[48,4224]{1,0:T(8,128)(2,1)S(1)}, bf16[48,4224]{1,0:T(8,128)(2,1)S(1)}, u32[]{:S(2)}, u32[]{:S(2)}) collective-permute-start(bf16[48,4224]{1,0:T(8,128)(2,1)S(1)} %pad_maximum_fusion.6), channel_id=1, source_target_pairs={{0,1},{1,0},{2,3},{3,2},{4,5},{5,4},{6,7},{7,6},{8,9},{9,8},{10,11... | collective-permute-start | bytes 1216520 | tf_op jit(solution)/shard_map/ppermute | solution.py:33
  35.1 7.9 %collective-permute-start.6 = (bf16[48,4224]{1,0:T(8,128)(2,1)S(1)}, bf16[48,4224]{1,0:T(8,128)(2,1)S(1)}, u32[]{:S(2)}, u32[]{:S(2)}) collective-permute-start(bf16[48,4224]{1,0:T(8,128)(2,1)S(1)} %pad_maximum_fusion.5), channel_id=1, source_target_pairs={{0,4},{1,5},{2,6},{3,7},{4,0},{5,1},{6,2},{7,3},{8,12},{9,13},{10,... | collective-permute-start | bytes 1216520 | tf_op jit(solution)/shard_map/ppermute | solution.py:33
  39.7 7.8 %copy-start = (bf16[4096,1002]{0,1:T(8,128)(2,1)S(1)}, bf16[4096,1002]{0,1:T(8,128)(2,1)}, u32[]{:S(2)}) copy-start(bf16[4096,1002]{0,1:T(8,128)(2,1)} %param.7) | copy-start | bytes 24625156
  43.2 4.3 %collective-permute-start.12 = (bf16[256,4224]{1,0:T(8,128)(2,1)S(1)}, bf16[256,4224]{1,0:T(8,128)(2,1)S(1)}, u32[]{:S(2)}, u32[]{:S(2)}) collective-permute-start(bf16[256,4224]{1,0:T(8,128)(2,1)S(1)} %pad_maximum_fusion), channel_id=1, source_target_pairs={{0,16},{1,17},{2,18},{3,19},{4,20},{5,21},{6,22},{7,23},{8,24},{9,... | collective-permute-start | bytes 6488072 | tf_op jit(solution)/shard_map/ppermute | solution.py:37
  43.3 12.3 %collective-permute-start.10 = (bf16[96,4224]{1,0:T(8,128)(2,1)S(1)}, bf16[96,4224]{1,0:T(8,128)(2,1)S(1)}, u32[]{:S(2)}, u32[]{:S(2)}) collective-permute-start(bf16[96,4224]{1,0:T(8,128)(2,1)S(1)} %pad_maximum_fusion.3.refs_1_), channel_id=1, source_target_pairs={{0,32},{1,33},{2,34},{3,35},{4,36},{5,37},{6,38},{7,39},{8,40},{9,... | collective-permute-start | bytes 2433032 | tf_op jit(solution)/shard_map/ppermute | solution.py:33
  45.3 12.3 %collective-permute-start.9 = (bf16[96,4224]{1,0:T(8,128)(2,1)S(1)}, bf16[96,4224]{1,0:T(8,128)(2,1)S(1)}, u32[]{:S(2)}, u32[]{:S(2)}) collective-permute-start(bf16[96,4224]{1,0:T(8,128)(2,1)S(1)} %pad_maximum_fusion.2.refs_0_), channel_id=1, source_target_pairs={{0,1},{1,0},{2,3},{3,2},{4,5},{5,4},{6,7},{7,6},{8,9},{9,8},{10,11... | collective-permute-start | bytes 2433032 | tf_op jit(solution)/shard_map/ppermute | solution.py:33
  45.6 9.4 %collective-permute-start.11 = (bf16[64,4224]{1,0:T(8,128)(2,1)S(1)}, bf16[64,4224]{1,0:T(8,128)(2,1)S(1)}, u32[]{:S(2)}, u32[]{:S(2)}) collective-permute-start(bf16[64,4224]{1,0:T(8,128)(2,1)S(1)} %pad_maximum_fusion.4.refs_2_), channel_id=1, source_target_pairs={{0,4},{1,5},{2,6},{3,7},{4,0},{5,1},{6,2},{7,3},{8,12},{9,13},{10,... | collective-permute-start | bytes 1622024 | tf_op jit(solution)/shard_map/ppermute | solution.py:33
  57.7 5.6 %collective-permute-start.13 = (bf16[256,4224]{1,0:T(8,128)(2,1)S(1)}, bf16[256,4224]{1,0:T(8,128)(2,1)S(1)}, u32[]{:S(2)}, u32[]{:S(2)}) collective-permute-start(bf16[256,4224]{1,0:T(8,128)(2,1)S(1)} %pad_maximum_fusion.1), channel_id=1, source_target_pairs={{0,16},{1,17},{2,18},{3,19},{4,20},{5,21},{6,22},{7,23},{8,24},{9,... | collective-permute-start | bytes 6488072 | tf_op jit(solution)/shard_map/ppermute | solution.py:37
  66.0 1.3 %collective-permute-start.14 = (f32[3,8,128]{2,1,0:T(8,128)S(1)}, f32[3,8,128]{2,1,0:T(8,128)S(1)}, u32[]{:S(2)}, u32[]{:S(2)}) collective-permute-start(f32[3,8,128]{2,1,0:T(8,128)S(1)} %get-tuple-element.37), channel_id=1, source_target_pairs={{0,16},{1,17},{2,18},{3,19},{4,20},{5,21},{6,22},{7,23},{8,24},{9,... | collective-permute-start | bytes 36872 | tf_op jit(solution)/shard_map/ppermute | solution.py:37
  67.3 3.8 %collective-permute-start.15 = (f32[3,8,128]{2,1,0:T(8,128)S(1)}, f32[3,8,128]{2,1,0:T(8,128)S(1)}, u32[]{:S(2)}, u32[]{:S(2)}) collective-permute-start(f32[3,8,128]{2,1,0:T(8,128)S(1)} %pad_maximum_fusion.8), channel_id=1, source_target_pairs={{0,32},{1,33},{2,34},{3,35},{4,36},{5,37},{6,38},{7,39},{8,40},{9,... | collective-permute-start | bytes 36872 | tf_op jit(solution)/shard_map/ppermute | solution.py:33
  71.1 5.0 %collective-permute-start.16 = (f32[3,8,128]{2,1,0:T(8,128)S(1)}, f32[3,8,128]{2,1,0:T(8,128)S(1)}, u32[]{:S(2)}, u32[]{:S(2)}) collective-permute-start(f32[3,8,128]{2,1,0:T(8,128)S(1)} %pad_maximum_fusion.9), channel_id=1, source_target_pairs={{0,96},{1,97},{2,98},{3,99},{4,100},{5,101},{6,102},{7,103},{8,104... | collective-permute-start | bytes 36872 | tf_op jit(solution)/shard_map/ppermute | solution.py:33
  76.2 3.8 %collective-permute-start.17 = (f32[3,8,128]{2,1,0:T(8,128)S(1)}, f32[3,8,128]{2,1,0:T(8,128)S(1)}, u32[]{:S(2)}, u32[]{:S(2)}) collective-permute-start(f32[3,8,128]{2,1,0:T(8,128)S(1)} %pad_maximum_fusion.10), channel_id=1, source_target_pairs={{0,4},{1,5},{2,6},{3,7},{4,0},{5,1},{6,2},{7,3},{8,12},{9,13},{10,... | collective-permute-start | bytes 36872 | tf_op jit(solution)/shard_map/ppermute | solution.py:33
  80.0 5.0 %collective-permute-start.18 = (f32[3,8,128]{2,1,0:T(8,128)S(1)}, f32[3,8,128]{2,1,0:T(8,128)S(1)}, u32[]{:S(2)}, u32[]{:S(2)}) collective-permute-start(f32[3,8,128]{2,1,0:T(8,128)S(1)} %pad_maximum_fusion.11), channel_id=1, source_target_pairs={{0,12},{1,13},{2,14},{3,15},{4,8},{5,9},{6,10},{7,11},{8,4},{9,5},... | collective-permute-start | bytes 36872 | tf_op jit(solution)/shard_map/ppermute | solution.py:33
  85.0 3.8 %collective-permute-start.19 = (f32[3,8,128]{2,1,0:T(8,128)S(1)}, f32[3,8,128]{2,1,0:T(8,128)S(1)}, u32[]{:S(2)}, u32[]{:S(2)}) collective-permute-start(f32[3,8,128]{2,1,0:T(8,128)S(1)} %pad_maximum_fusion.12), channel_id=1, source_target_pairs={{0,1},{1,0},{2,3},{3,2},{4,5},{5,4},{6,7},{7,6},{8,9},{9,8},{10,11... | collective-permute-start | bytes 36872 | tf_op jit(solution)/shard_map/ppermute | solution.py:33
  88.8 5.0 %collective-permute-start.20 = (f32[3,8,128]{2,1,0:T(8,128)S(1)}, f32[3,8,128]{2,1,0:T(8,128)S(1)}, u32[]{:S(2)}, u32[]{:S(2)}) collective-permute-start(f32[3,8,128]{2,1,0:T(8,128)S(1)} %pad_maximum_fusion.13.mine_ref), channel_id=1, source_target_pairs={{0,3},{1,2},{2,1},{3,0},{4,7},{5,6},{6,5},{7,4},{8,11},{9,10},{10,... | collective-permute-start | bytes 36872 | tf_op jit(solution)/shard_map/ppermute | solution.py:33

commit v3 on v2

--- a/solution.py
+++ b/solution.py
@@ -15,30 +15,44 @@
 F32 = jnp.float32
 CHUNK = 256
 LIMIT = 12 << 20
+EARLY = (((2, 0), (2, 1), (1, 0)), ((0, 0), (0, 1), (1, 1)))
+LATE = (((1, 1), (0, 0), (0, 1)), ((2, 0), (2, 1), (1, 0)))
 
 
 def coords(d):
     return (d // 32, (d // 4) % 4, d % 4), (d // 16) % 2
 
 
-def flipped(d, axis, bit):
-    (z, y, x), core = coords(d)
-    p = [z, y, x]
-    p[axis] = 3 - p[axis] if bit else p[axis] ^ 1
+def cube_bits(p):
+    return (p ^ (p >> 1)) & 1, p >> 1
+
+
+def cube_index(place_of, dims):
+    return sum(cube_bits(place_of[axis])[bit] << k for k, (axis, bit) in enumerate(dims))
+
+
+def flipped(d, dims):
+    p, core = coords(d)
+    p = list(p)
+    for axis, bit in dims:
+        p[axis] = 3 - p[axis] if bit else p[axis] ^ 1
     return ((p[0] * 2 + core) * 4 + p[1]) * 4 + p[2]
 
 
-def exchange(v, axis, bits):
-    pairs = [(d, flipped(d, axis, bits[coords(d)[1]])) for d in range(N_DEV)]
-    return lax.ppermute(v, "d", pairs)
+def exchange(v, by_core):
+    return lax.ppermute(v, "d", [(d, flipped(d, by_core[coords(d)[1]])) for d in range(N_DEV)])
+
+
+def late_exchange(v, k):
+    return exchange(v, [(dims[k % 3],) for dims in LATE])
+
+
+def cross_exchange(v, dims):
+    return lax.ppermute(v, "d", [(d, flipped(d, dims) ^ 16) for d in range(N_DEV)])
 
 
 def core_swap(v):
     return lax.ppermute(v, "d", [(d, d ^ 16) for d in range(N_DEV)])
-
-
-def cube_bits(p):
-    return (p ^ (p >> 1)) & 1, p >> 1
 
 
 NT = (((1,), (1,)), ((), ()))
@@ -65,23 +79,25 @@
     return jnp.dot(wide, upto, preferred_element_type=F32)[0:1]
 
 
-def pack_kernel(hidden_ref, target_ref, bench_ref, valid_ref, length_ref, x_ref, aux_ref):
+def pack_kernel(hidden_ref, ints_ref, x_ref, aux_ref):
     rows, depth = hidden_ref.shape
     kept = rows // 2
-    seqs = length_ref.shape[1]
+    ints = ints_ref[...]
+    target, bench, valid = (ints[:, k * rows : (k + 1) * rows] for k in range(3))
+    lengths = ints[:, 3 * rows :]
+    seqs = lengths.shape[1]
     me = lax.axis_index("d")
-    ends = running_sum(length_ref[...].astype(F32), seqs).astype(jnp.int32) - 1
+    ends = running_sum(lengths.astype(F32), seqs).astype(jnp.int32) - 1
     position = me * rows + iota((rows, seqs), 0)
     is_end = jnp.max(jnp.where(ends == position, 1.0, 0.0), axis=1, keepdims=True)
-    valid = valid_ref[...].astype(F32)
+    valid = valid.astype(F32)
     rank = running_sum(valid, rows) - 1.0
     token = iota((1, rows), 1).astype(F32)
     count = jnp.sum(valid, axis=1, keepdims=True)
     slot = jnp.where(valid > 0.5, rank, count + token - rank - 1.0)
     selector = jnp.where(iota((kept, rows), 0).astype(F32) == slot, 1.0, 0.0).astype(jnp.bfloat16)
     scored = as_column(valid, rows) * (1.0 - is_end)
-    target = target_ref[...]
-    digits = [target >> 16, (target >> 8) & 255, target & 255, bench_ref[...]]
+    digits = [target >> 16, (target >> 8) & 255, target & 255, bench]
     lane = iota((rows, LAB), 1)
     labels = jnp.where(lane == 4, scored, 0.0)
     for k, digit in enumerate(digits):
@@ -103,11 +119,11 @@
             jax.ShapeDtypeStruct((rows // 2, depth + LAB), jnp.bfloat16),
             jax.ShapeDtypeStruct((rows, LAB), F32),
         ),
-        in_specs=[VMEM] * 5,
+        in_specs=[VMEM, VMEM],
         out_specs=(VMEM, VMEM),
         compiler_params=pltpu.CompilerParams(vmem_limit_bytes=4 << 20),
         name="pack",
-    )(hidden, *(v.reshape(1, -1) for v in ints))
+    )(hidden, jnp.concatenate(ints).reshape(1, -1))
 
 
 def scores(x_ref, at, w_ref, acc_ref):
@@ -168,8 +184,7 @@
     gather_rows(pieces, x_ref)
     sib = scores(x_ref, 0, w_ref, acc_ref)
     place_of, core = coords(lax.axis_index("d"))
-    bits = [cube_bits(p) for p in place_of]
-    blocks = [sum(b[k] << axis for axis, b in enumerate(bits)) for k in range(2)]
+    blocks = [cube_index(place_of, LATE[k]) for k in range(2)]
     is_first = core == 0
     halves = ((first_ref[:, :CHUNK], first_ref[:, CHUNK:]), (own_ref[...], sib))
     for half, (a, b) in enumerate(halves):
@@ -209,22 +224,23 @@
     )(w, first, own, *pieces)
 
 
-def merged(a, b):
-    best = jnp.maximum(a[0], b[0])
-    total = a[1] * jnp.exp(a[0] - best) + b[1] * jnp.exp(b[0] - best)
-    return best, total, a[2] + b[2]
-
-
-def final_kernel(mine_ref, got_ref, labels_ref, aux_ref, loss_ref, mean_ref, count_ref, all_ref):
-    best, total, target = merged(mine_ref, got_ref)
+def merged(parts):
+    best = parts[0][0]
+    for p in parts[1:]:
+        best = jnp.maximum(best, p[0])
+    total = sum(p[1] * jnp.exp(p[0] - best) for p in parts)
+    return best, total, sum(p[2] for p in parts)
+
+
+def final_kernel(*refs):
+    *parts, labels_ref, aux_ref, loss_ref, mean_ref, count_ref, all_ref = refs
+    best, total, target = merged(parts)
     losses = best + jnp.log(total) - target
     all_ref[...] = losses
     rows = aux_ref.shape[0]
     place_of, core = coords(lax.axis_index("d"))
-    bits = [cube_bits(p) for p in place_of]
-    is_first = core == 0
-    block = sum(jnp.where(is_first, b[0], b[1]) << axis for axis, b in enumerate(bits))
-    base = core * 64 + 8 * sum(jnp.where(is_first, b[1], b[0]) << axis for axis, b in enumerate(bits))
+    block = jnp.where(core == 0, *(cube_index(place_of, dims) for dims in LATE))
+    base = core * 64 + 8 * jnp.where(core == 0, *(cube_index(place_of, dims) for dims in EARLY))
     mine = all_ref[pl.ds(block, 1), :]
     hit = iota((rows, LAB), 1) == base + aux_ref[:, 0:1].astype(jnp.int32)
     column = jnp.sum(jnp.where(hit, mine, 0.0), axis=1, keepdims=True)
@@ -243,17 +259,17 @@
     count_ref[...] = counts
 
 
-def final(mine, got, labels, aux):
+def final(parts, labels, aux):
     rows = aux.shape[0]
     outs = pl.pallas_call(
         final_kernel,
         out_shape=tuple(jax.ShapeDtypeStruct((1, n), F32) for n in (rows, BENCH, BENCH)),
-        in_specs=[VMEM] * 4,
+        in_specs=[VMEM] * (len(parts) + 2),
         out_specs=(VMEM,) * 3,
         scratch_shapes=[pltpu.VMEM((8, LAB), F32)],
         compiler_params=pltpu.CompilerParams(vmem_limit_bytes=4 << 20),
         name="final",
-    )(mine, got, labels, aux)
+    )(*parts, labels, aux)
     return tuple(v.reshape(-1) for v in outs)
 
 
@@ -261,34 +277,35 @@
     return lax.optimization_barrier(arrays)
 
 
+def ordered(low, a, b):
+    return jnp.where(low, jnp.concatenate([a, b], 0), jnp.concatenate([b, a], 0))
+
+
 def body(hidden, head_weight, targets, bench_ids, valid, seq_lengths):
-    me = lax.axis_index("d")
-    place_of, core = coords(me)
-    early = [jnp.where(core == 0, b[1], b[0]) for b in map(cube_bits, place_of)]
+    place_of, core = coords(lax.axis_index("d"))
+    early = jnp.where(core == 0, *(cube_index(place_of, dims) for dims in EARLY))
+    low = [(early >> k) & 1 == 0 for k in range(3)]
     x, aux = pack(hidden, targets, bench_ids, valid, seq_lengths)
-    for axis in range(3):
-        got = exchange(x, axis, (1, 0))
-        x = jnp.where(
-            early[axis] == 0, jnp.concatenate([x, got], 0), jnp.concatenate([got, x], 0)
-        )
-    held = [x[s : s + n] for s, n in zip(STARTS, ROWS)]
+    both, first, second = (exchange(x, [d[s] for d in EARLY]) for s in (slice(0, 2), slice(0, 1), slice(1, 2)))
+    x = ordered(low[1], ordered(low[0], x, first), ordered(low[0], second, both))
+    x = ordered(low[2], x, exchange(x, [d[2:] for d in EARLY]))
+    held = tied(*(x[s : s + n] for s, n in zip(STARTS, ROWS)))
     for k in range(2):
-        held = tied(*held)
-        got = [exchange(held[g], (g + k) % 3, (0, 1)) for g in range(3)]
+        got = [late_exchange(held[g], g + k) for g in range(3)]
         held = [jnp.concatenate([a, b], 0) for a, b in zip(held, got)]
-    held = tied(*held)
     w = head_weight.T
-    last = [exchange(held[g], (g + 2) % 3, (0, 1)) for g in range(3)]
+    last = [late_exchange(held[g], g + 2) for g in range(3)]
     first = score(w, [*held, core_swap(jnp.concatenate(held, 0))])
     *last, first = tied(*last, first)
     other = core_swap(jnp.concatenate(last, 0))
     own = score(w, last)
     stats, labels = score_place(w, first, own, [other])
-    for axis, bits in [(0, None), *((a, (b, b)) for a in range(3) for b in range(2))]:
-        got = core_swap(stats) if bits is None else exchange(stats, axis, bits)
-        if (axis, bits) != (2, (1, 1)):
-            stats = jnp.stack(merged(stats, got))
-    return final(stats, got, labels, aux)
+    parts = [stats, core_swap(stats)]
+    for axis in range(3):
+        stats = jnp.stack(merged(parts))
+        steps = [(axis, 0), (axis, 1)]
+        parts = [stats, *(cross_exchange(stats, d) for d in (steps[:1], steps[1:], steps))]
+    return final(parts, labels, aux)
 
 
 def solution(mesh):

time: 94.7 us -> 85.7 us (0.905); the launches traced: 94.5 us -> 84.3 us
  waiting for transfers between devices: 47.3 us -> 37.1 us
  local copies, waits for them, and re-layouts: 3.56 us -> 1.34 us
  starting transfers between devices: 30.8 us -> 32.3 us
    ppermute x18 -> x22, waiting for transfers between devices: 44.1 us -> 32.4 us  [the longest x13 26.7 us: exchange(): lax.ppermute(v, 'd', [(d, flipped(d, by_core[coords(d)[1]])) for d in ran...]
    ppermute x18 -> x22, starting transfers between devices: 28.5 us -> 31.7 us  [the longest x13 20.6 us: exchange(): lax.ppermute(v, 'd', [(d, flipped(d, by_core[coords(d)[1]])) for d in ran...]
    unnamed x12, local copies, waits for them, and re-layouts: 3.52 us -> 1.25 us
    ppermute x3, starting transfers between devices: 2.3 us -> 0.56 us  [core_swap(): return lax.ppermute(v, 'd', [(d, d ^ 16) for d in range(N_DEV)])]
    ppermute x3, waiting for transfers between devices: 3.17 us -> 4.72 us  [core_swap(): return lax.ppermute(v, 'd', [(d, d ^ 16) for d in range(N_DEV)])]
  transfers between devices with their start and end apart: 21 -> 25, of which waited for: 21 -> 19; matrix products, arithmetic and copies ran while one was open for 0% -> 1% of each run, Pallas kernels for 8% -> 9%
where the time goes in v3:
time: 85.7 us; the launch traced here: 84.3 us
  waiting for transfers between devices  37.1 us (43%)
  starting transfers between devices  32.3 us (38%)
  Pallas kernels  11.4 us (13%)
  local copies, waits for them, and re-layouts  1.34 us (2%)
  other arithmetic  1.26 us (1%)
    ppermute x13, waiting for transfers between devices, exchange(): lax.ppermute(v, 'd', [(d, flipped(d, by_core[coords(d)[1]])) for d in ran...  26.7 us
    ppermute x13, starting transfers between devices, exchange(): lax.ppermute(v, 'd', [(d, flipped(d, by_core[coords(d)[1]])) for d in ran...  20.6 us
    ppermute x9, starting transfers between devices, cross_exchange(): lax.ppermute(v, 'd', [(d, flipped(d, dims) ^ 16) for d in range(N_DEV)])  11.1 us
    pallas_call x2, Pallas kernels, score(): pl.pallas_call(score_kernel, out_shape=jax.ShapeDtypeStruct((8, rows), F3...  7.51 us
    ppermute x9, waiting for transfers between devices, cross_exchange(): lax.ppermute(v, 'd', [(d, flipped(d, dims) ^ 16) for d in range(N_DEV)])  5.74 us
    ppermute x3, waiting for transfers between devices, core_swap(): return lax.ppermute(v, 'd', [(d, d ^ 16) for d in range(N_DEV)])  4.72 us
    pallas_call x1, Pallas kernels, score_place(): pl.pallas_call(score_place_kernel, out_shape=(jax.ShapeDtypeStruct((3, 8,...  2.69 us
  transfers between devices with their start and end apart: 25, of which 19 were waited for; matrix products, arithmetic and copies ran while one was open for 1% of the time, Pallas kernels for 9%

profile of v3, /device:TPU:0, one launch (start us, length us, event | category | flops | bytes accessed | tf_op | source)
XLA Modules:
  0.0 84.3 jit_solution(5394597586160750634)
XLA Ops:
  0.6 0.8 add_bitcast_fusion.ints_ref
  1.4 0.9 %copy-done.1 = bf16[16,4096]{1,0:T(8,128)(2,1)S(1)} copy-done((bf16[16,4096]{1,0:T(8,128)(2,1)S(1)}, bf16[16,4096]{1,0:T(8,128)(2,1)}, u32[]{:S(2)}) %copy-start.1) | copy-done | bytes 131096
  2.8 1.7 %collective-permute-start = (bf16[8,4224]{1,0:T(8,128)(2,1)S(1)}, bf16[8,4224]{1,0:T(8,128)(2,1)S(1)}, u32[]{:S(2)}, u32[]{:S(2)}) collective-permute-start(bf16[8,4224]{1,0:T(8,128)(2,1)S(1)} %get-tuple-element.17), channel_id=1, source_target_pairs={{0,1},{1,0},{2,3},{3,2},{4,5},{5,4},{6,7},{7,6},{8,9},{9,8},{10,11... | collective-permute-start | bytes 202760 | tf_op jit(solution)/shard_map/ppermute | solution.py:43
  4.5 2.1 %collective-permute-start.1 = (bf16[8,4224]{1,0:T(8,128)(2,1)S(1)}, bf16[8,4224]{1,0:T(8,128)(2,1)S(1)}, u32[]{:S(2)}, u32[]{:S(2)}) collective-permute-start(bf16[8,4224]{1,0:T(8,128)(2,1)S(1)} %get-tuple-element.17), channel_id=1, source_target_pairs={{0,3},{1,2},{2,1},{3,0},{4,7},{5,6},{6,5},{7,4},{8,11},{9,10},{10,... | collective-permute-start | bytes 202760 | tf_op jit(solution)/shard_map/ppermute | solution.py:43
  7.2 2.7 %collective-permute-done.1 = bf16[8,4224]{1,0:T(8,128)(2,1)S(1)} collective-permute-done((bf16[8,4224]{1,0:T(8,128)(2,1)S(1)}, bf16[8,4224]{1,0:T(8,128)(2,1)S(1)}, u32[]{:S(2)}, u32[]{:S(2)}) %collective-permute-start.1) | collective-permute-done | bytes 67616 | tf_op jit(solution)/shard_map/ppermute | solution.py:43
  10.0 2.4 %collective-permute-done.2 = bf16[8,4224]{1,0:T(8,128)(2,1)S(1)} collective-permute-done((bf16[8,4224]{1,0:T(8,128)(2,1)S(1)}, bf16[8,4224]{1,0:T(8,128)(2,1)S(1)}, u32[]{:S(2)}, u32[]{:S(2)}) %collective-permute-start.2) | collective-permute-done | bytes 67616 | tf_op jit(solution)/shard_map/ppermute | solution.py:43
  12.4 1.7 %collective-permute-start.3 = (bf16[32,4224]{1,0:T(8,128)(2,1)S(1)}, bf16[32,4224]{1,0:T(8,128)(2,1)S(1)}, u32[]{:S(2)}, u32[]{:S(2)}) collective-permute-start(bf16[32,4224]{1,0:T(8,128)(2,1)S(1)} %maximum_select_fusion.1), channel_id=1, source_target_pairs={{0,4},{1,5},{2,6},{3,7},{4,0},{5,1},{6,2},{7,3},{8,12},{9,13},{10,... | collective-permute-start | bytes 811016 | tf_op jit(solution)/shard_map/ppermute | solution.py:43
  14.1 4.9 %collective-permute-done.3 = bf16[32,4224]{1,0:T(8,128)(2,1)S(1)} collective-permute-done((bf16[32,4224]{1,0:T(8,128)(2,1)S(1)}, bf16[32,4224]{1,0:T(8,128)(2,1)S(1)}, u32[]{:S(2)}, u32[]{:S(2)}) %collective-permute-start.3) | collective-permute-done | bytes 270368 | tf_op jit(solution)/shard_map/ppermute | solution.py:43
  19.1 5.4 %collective-permute-start.10 = (bf16[16,4224]{1,0:T(8,128)(2,1)S(1)}, bf16[16,4224]{1,0:T(8,128)(2,1)S(1)}, u32[]{:S(2)}, u32[]{:S(2)}) collective-permute-start(bf16[16,4224]{1,0:T(8,128)(2,1)S(1)} %slice.118), channel_id=1, source_target_pairs={{0,96},{1,97},{2,98},{3,99},{4,100},{5,101},{6,102},{7,103},{8,104... | collective-permute-start | bytes 405512 | tf_op jit(solution)/shard_map/ppermute | solution.py:43
  24.6 3.2 %collective-permute-start.4 = (bf16[24,4224]{1,0:T(8,128)(2,1)S(1)}, bf16[24,4224]{1,0:T(8,128)(2,1)S(1)}, u32[]{:S(2)}, u32[]{:S(2)}) collective-permute-start(bf16[24,4224]{1,0:T(8,128)(2,1)S(1)} %get-tuple-element.18), channel_id=1, source_target_pairs={{0,12},{1,13},{2,14},{3,15},{4,8},{5,9},{6,10},{7,11},{8,4},{9,5},... | collective-permute-start | bytes 608264 | tf_op jit(solution)/shard_map/ppermute | solution.py:43
  27.8 3.0 %collective-permute-start.11 = (bf16[32,4224]{1,0:T(8,128)(2,1)S(1)}, bf16[32,4224]{1,0:T(8,128)(2,1)S(1)}, u32[]{:S(2)}, u32[]{:S(2)}) collective-permute-start(bf16[32,4224]{1,0:T(8,128)(2,1)S(1)} %pad_maximum_fusion.3), channel_id=1, source_target_pairs={{0,12},{1,13},{2,14},{3,15},{4,8},{5,9},{6,10},{7,11},{8,4},{9,5},... | collective-permute-start | bytes 811016 | tf_op jit(solution)/shard_map/ppermute | solution.py:43
  30.7 0.9 %collective-permute-done.4 = bf16[24,4224]{1,0:T(8,128)(2,1)S(1)} collective-permute-done((bf16[24,4224]{1,0:T(8,128)(2,1)S(1)}, bf16[24,4224]{1,0:T(8,128)(2,1)S(1)}, u32[]{:S(2)}, u32[]{:S(2)}) %collective-permute-start.4) | collective-permute-done | bytes 202784 | tf_op jit(solution)/shard_map/ppermute | solution.py:43
  31.8 1.7 %collective-permute-done.7 = bf16[24,4224]{1,0:T(8,128)(2,1)S(1)} collective-permute-done((bf16[24,4224]{1,0:T(8,128)(2,1)S(1)}, bf16[24,4224]{1,0:T(8,128)(2,1)S(1)}, u32[]{:S(2)}, u32[]{:S(2)}) %collective-permute-start.7) | collective-permute-done | bytes 202784 | tf_op jit(solution)/shard_map/ppermute | solution.py:43
  34.3 5.4 %collective-permute-done.5 = bf16[48,4224]{1,0:T(8,128)(2,1)S(1)} collective-permute-done((bf16[48,4224]{1,0:T(8,128)(2,1)S(1)}, bf16[48,4224]{1,0:T(8,128)(2,1)S(1)}, u32[]{:S(2)}, u32[]{:S(2)}) %collective-permute-start.5) | collective-permute-done | bytes 405536 | tf_op jit(solution)/shard_map/ppermute | solution.py:43
  39.8 2.9 %collective-permute-done.8 = bf16[48,4224]{1,0:T(8,128)(2,1)S(1)} collective-permute-done((bf16[48,4224]{1,0:T(8,128)(2,1)S(1)}, bf16[48,4224]{1,0:T(8,128)(2,1)S(1)}, u32[]{:S(2)}, u32[]{:S(2)}) %collective-permute-start.8) | collective-permute-done | bytes 405536 | tf_op jit(solution)/shard_map/ppermute | solution.py:43
  43.0 1.4 %collective-permute-start.9 = (bf16[96,4224]{1,0:T(8,128)(2,1)S(1)}, bf16[96,4224]{1,0:T(8,128)(2,1)S(1)}, u32[]{:S(2)}, u32[]{:S(2)}) collective-permute-start(bf16[96,4224]{1,0:T(8,128)(2,1)S(1)} %get-tuple-element.40.refs_1_), channel_id=1, source_target_pairs={{0,12},{1,13},{2,14},{3,15},{4,8},{5,9},{6,10},{7,11},{8,4},{9,5},... | collective-permute-start | bytes 2433032 | tf_op jit(solution)/shard_map/ppermute | solution.py:43
  45.3 2.0 %collective-permute-done.13.refs_3_ = bf16[256,4224]{1,0:T(8,128)(2,1)S(1)} collective-permute-done((bf16[256,4224]{1,0:T(8,128)(2,1)S(1)}, bf16[256,4224]{1,0:T(8,128)(2,1)S(1)}, u32[]{:S(2)}, u32[]{:S(2)}) %collective-permute-start.13) | collective-permute-done | bytes 2162720 | tf_op jit(solution)/shard_map/ppermute | solution.py:55
  47.3 4.9 %score.2.first_ref = f32[8,512]{1,0:T(8,128)S(1)} custom-call(bf16[1002,4096]{1,0:T(8,128)(2,1)S(1)} %bitcast.6, bf16[96,4224]{1,0:T(8,128)(2,1)S(1)} %get-tuple-element.42.refs_0_, bf16[96,4224]{1,0:T(8,128)(2,1)S(1)} %get-tuple-element.40.refs_1_, bf16[64,4224]{1,0:T(8,128)(2,1)S(1)} %get-tuple-element.44.refs_2_, ...), custom_call_target="tpu_custom_call" | custom-call | flops 4202692608 | bytes 8208384 | tf_op jit(solution)/shard_map/score/pallas_call | solution.py:165
  52.2 1.6 %collective-permute-done.12.refs_2_ = bf16[64,4224]{1,0:T(8,128)(2,1)S(1)} collective-permute-done((bf16[64,4224]{1,0:T(8,128)(2,1)S(1)}, bf16[64,4224]{1,0:T(8,128)(2,1)S(1)}, u32[]{:S(2)}, u32[]{:S(2)}) %collective-permute-start.12) | collective-permute-done | bytes 540704 | tf_op jit(solution)/shard_map/ppermute | solution.py:43
  53.9 2.7 %collective-permute-done.9.refs_1_ = bf16[96,4224]{1,0:T(8,128)(2,1)S(1)} collective-permute-done((bf16[96,4224]{1,0:T(8,128)(2,1)S(1)}, bf16[96,4224]{1,0:T(8,128)(2,1)S(1)}, u32[]{:S(2)}, u32[]{:S(2)}) %collective-permute-start.9) | collective-permute-done | bytes 811040 | tf_op jit(solution)/shard_map/ppermute | solution.py:43
  56.6 1.4 %collective-permute-done.6.refs_0_ = bf16[96,4224]{1,0:T(8,128)(2,1)S(1)} collective-permute-done((bf16[96,4224]{1,0:T(8,128)(2,1)S(1)}, bf16[96,4224]{1,0:T(8,128)(2,1)S(1)}, u32[]{:S(2)}, u32[]{:S(2)}) %collective-permute-start.6) | collective-permute-done | bytes 811040 | tf_op jit(solution)/shard_map/ppermute | solution.py:43
  58.4 2.6 %score.3.own_ref = f32[8,256]{1,0:T(8,128)S(1)} custom-call(bf16[1002,4096]{1,0:T(8,128)(2,1)S(1)} %bitcast.7, bf16[96,4224]{1,0:T(8,128)(2,1)S(1)} %collective-permute-done.6.refs_0_, bf16[96,4224]{1,0:T(8,128)(2,1)S(1)} %collective-permute-done.9.refs_1_, bf16[64,4224]{1,0:T(8,128)(2,1)S(1)} %collective-permute-done.12.refs_2_), custom_call_target="tpu_custom_call" | custom-call | flops 2101346304 | bytes 8208384 | tf_op jit(solution)/shard_map/score/pallas_call | solution.py:165
  60.9 1.7 %collective-permute-done.14.refs_0_ = bf16[256,4224]{1,0:T(8,128)(2,1)S(1)} collective-permute-done((bf16[256,4224]{1,0:T(8,128)(2,1)S(1)}, bf16[256,4224]{1,0:T(8,128)(2,1)S(1)}, u32[]{:S(2)}, u32[]{:S(2)}) %collective-permute-start.14) | collective-permute-done | bytes 2162720 | tf_op jit(solution)/shard_map/ppermute | solution.py:55
  62.6 2.7 %score_place.1 = (f32[3,8,128]{2,1,0:T(8,128)S(1)}, f32[2,8,128]{2,1,0:T(8,128)S(1)}) custom-call(bf16[1002,4096]{1,0:T(8,128)(2,1)S(1)} %bitcast.8, f32[8,512]{1,0:T(8,128)S(1)} %score.2.first_ref, f32[8,256]{1,0:T(8,128)S(1)} %score.3.own_ref, bf16[256,4224]{1,0:T(8,128)(2,1)S(1)} %collective-permute-done.14.refs_0_), custom_call_target="tpu_custom_call" | custom-call | flops 2101346304 | bytes 8208384 | tf_op jit(solution)/shard_map/score_place/pallas_call | solution.py:209
  65.5 1.0 %collective-permute-done.15 = f32[3,8,128]{2,1,0:T(8,128)S(1)} collective-permute-done((f32[3,8,128]{2,1,0:T(8,128)S(1)}, f32[3,8,128]{2,1,0:T(8,128)S(1)}, u32[]{:S(2)}, u32[]{:S(2)}) %collective-permute-start.15) | collective-permute-done | bytes 12320 | tf_op jit(solution)/shard_map/ppermute | solution.py:55
  66.8 3.5 %collective-permute-start.18 = (f32[3,8,128]{2,1,0:T(8,128)S(1)}, f32[3,8,128]{2,1,0:T(8,128)S(1)}, u32[]{:S(2)}, u32[]{:S(2)}) collective-permute-start(f32[3,8,128]{2,1,0:T(8,128)S(1)} %pad_maximum_fusion.4), channel_id=1, source_target_pairs={{0,80},{1,81},{2,82},{3,83},{4,84},{5,85},{6,86},{7,87},{8,88},{9,... | collective-permute-start | bytes 36872 | tf_op jit(solution)/shard_map/ppermute | solution.py:51
  70.2 0.8 collective-permute-done.17
  71.8 2.0 %collective-permute-start.20 = (f32[3,8,128]{2,1,0:T(8,128)S(1)}, f32[3,8,128]{2,1,0:T(8,128)S(1)}, u32[]{:S(2)}, u32[]{:S(2)}) collective-permute-start(f32[3,8,128]{2,1,0:T(8,128)S(1)} %pad_maximum_fusion.5), channel_id=1, source_target_pairs={{0,28},{1,29},{2,30},{3,31},{4,24},{5,25},{6,26},{7,27},{8,20},{9,... | collective-permute-start | bytes 36872 | tf_op jit(solution)/shard_map/ppermute | solution.py:51
  73.8 1.7 %collective-permute-start.21 = (f32[3,8,128]{2,1,0:T(8,128)S(1)}, f32[3,8,128]{2,1,0:T(8,128)S(1)}, u32[]{:S(2)}, u32[]{:S(2)}) collective-permute-start(f32[3,8,128]{2,1,0:T(8,128)S(1)} %pad_maximum_fusion.5), channel_id=1, source_target_pairs={{0,24},{1,25},{2,26},{3,27},{4,28},{5,29},{6,30},{7,31},{8,16},{9,... | collective-permute-start | bytes 36872 | tf_op jit(solution)/shard_map/ppermute | solution.py:51
  76.2 2.2 %collective-permute-done.21 = f32[3,8,128]{2,1,0:T(8,128)S(1)} collective-permute-done((f32[3,8,128]{2,1,0:T(8,128)S(1)}, f32[3,8,128]{2,1,0:T(8,128)S(1)}, u32[]{:S(2)}, u32[]{:S(2)}) %collective-permute-start.21) | collective-permute-done | bytes 12320 | tf_op jit(solution)/shard_map/ppermute | solution.py:51
  78.6 3.5 %collective-permute-start.24 = (f32[3,8,128]{2,1,0:T(8,128)S(1)}, f32[3,8,128]{2,1,0:T(8,128)S(1)}, u32[]{:S(2)}, u32[]{:S(2)}) collective-permute-start(f32[3,8,128]{2,1,0:T(8,128)S(1)} %pad_maximum_fusion.6.refs_0_), channel_id=1, source_target_pairs={{0,18},{1,19},{2,16},{3,17},{4,22},{5,23},{6,20},{7,21},{8,26},{9,... | collective-permute-start | bytes 36872 | tf_op jit(solution)/shard_map/ppermute | solution.py:51
  82.1 0.8 collective-permute-done.23.refs_2_
  (53 shorter events, 7.2 us)
Async XLA Ops:
  1.4 0.9 %copy-start.1 = (bf16[16,4096]{1,0:T(8,128)(2,1)S(1)}, bf16[16,4096]{1,0:T(8,128)(2,1)}, u32[]{:S(2)}) copy-start(bf16[16,4096]{1,0:T(8,128)(2,1)} %hidden_ref.1) | copy-start | bytes 393220
  2.8 4.4 %collective-permute-start = (bf16[8,4224]{1,0:T(8,128)(2,1)S(1)}, bf16[8,4224]{1,0:T(8,128)(2,1)S(1)}, u32[]{:S(2)}, u32[]{:S(2)}) collective-permute-start(bf16[8,4224]{1,0:T(8,128)(2,1)S(1)} %get-tuple-element.17), channel_id=1, source_target_pairs={{0,1},{1,0},{2,3},{3,2},{4,5},{5,4},{6,7},{7,6},{8,9},{9,8},{10,11... | collective-permute-start | bytes 202760 | tf_op jit(solution)/shard_map/ppermute | solution.py:43
  4.5 5.5 %collective-permute-start.1 = (bf16[8,4224]{1,0:T(8,128)(2,1)S(1)}, bf16[8,4224]{1,0:T(8,128)(2,1)S(1)}, u32[]{:S(2)}, u32[]{:S(2)}) collective-permute-start(bf16[8,4224]{1,0:T(8,128)(2,1)S(1)} %get-tuple-element.17), channel_id=1, source_target_pairs={{0,3},{1,2},{2,1},{3,0},{4,7},{5,6},{6,5},{7,4},{8,11},{9,10},{10,... | collective-permute-start | bytes 202760 | tf_op jit(solution)/shard_map/ppermute | solution.py:43
  6.6 5.8 %collective-permute-start.2 = (bf16[8,4224]{1,0:T(8,128)(2,1)S(1)}, bf16[8,4224]{1,0:T(8,128)(2,1)S(1)}, u32[]{:S(2)}, u32[]{:S(2)}) collective-permute-start(bf16[8,4224]{1,0:T(8,128)(2,1)S(1)} %get-tuple-element.17), channel_id=1, source_target_pairs={{0,2},{1,3},{2,0},{3,1},{4,6},{5,7},{6,4},{7,5},{8,10},{9,11},{10,... | collective-permute-start | bytes 202760 | tf_op jit(solution)/shard_map/ppermute | solution.py:43
  12.4 6.5 %collective-permute-start.3 = (bf16[32,4224]{1,0:T(8,128)(2,1)S(1)}, bf16[32,4224]{1,0:T(8,128)(2,1)S(1)}, u32[]{:S(2)}, u32[]{:S(2)}) collective-permute-start(bf16[32,4224]{1,0:T(8,128)(2,1)S(1)} %maximum_select_fusion.1), channel_id=1, source_target_pairs={{0,4},{1,5},{2,6},{3,7},{4,0},{5,1},{6,2},{7,3},{8,12},{9,13},{10,... | collective-permute-start | bytes 811016 | tf_op jit(solution)/shard_map/ppermute | solution.py:43
  19.1 8.6 %collective-permute-start.10 = (bf16[16,4224]{1,0:T(8,128)(2,1)S(1)}, bf16[16,4224]{1,0:T(8,128)(2,1)S(1)}, u32[]{:S(2)}, u32[]{:S(2)}) collective-permute-start(bf16[16,4224]{1,0:T(8,128)(2,1)S(1)} %slice.118), channel_id=1, source_target_pairs={{0,96},{1,97},{2,98},{3,99},{4,100},{5,101},{6,102},{7,103},{8,104... | collective-permute-start | bytes 405512 | tf_op jit(solution)/shard_map/ppermute | solution.py:43
  24.6 22.7 %copy-start = (bf16[4096,1002]{0,1:T(8,128)(2,1)S(1)}, bf16[4096,1002]{0,1:T(8,128)(2,1)}, u32[]{:S(2)}) copy-start(bf16[4096,1002]{0,1:T(8,128)(2,1)} %param.7) | copy-start | bytes 24625156
  24.6 7.0 %collective-permute-start.4 = (bf16[24,4224]{1,0:T(8,128)(2,1)S(1)}, bf16[24,4224]{1,0:T(8,128)(2,1)S(1)}, u32[]{:S(2)}, u32[]{:S(2)}) collective-permute-start(bf16[24,4224]{1,0:T(8,128)(2,1)S(1)} %get-tuple-element.18), channel_id=1, source_target_pairs={{0,12},{1,13},{2,14},{3,15},{4,8},{5,9},{6,10},{7,11},{8,4},{9,5},... | collective-permute-start | bytes 608264 | tf_op jit(solution)/shard_map/ppermute | solution.py:43
  27.8 5.7 %collective-permute-start.7 = (bf16[24,4224]{1,0:T(8,128)(2,1)S(1)}, bf16[24,4224]{1,0:T(8,128)(2,1)S(1)}, u32[]{:S(2)}, u32[]{:S(2)}) collective-permute-start(bf16[24,4224]{1,0:T(8,128)(2,1)S(1)} %get-tuple-element.19), channel_id=1, source_target_pairs={{0,32},{1,33},{2,34},{3,35},{4,36},{5,37},{6,38},{7,39},{8,40},{9,... | collective-permute-start | bytes 608264 | tf_op jit(solution)/shard_map/ppermute | solution.py:43
  27.8 15.1 %collective-permute-start.11 = (bf16[32,4224]{1,0:T(8,128)(2,1)S(1)}, bf16[32,4224]{1,0:T(8,128)(2,1)S(1)}, u32[]{:S(2)}, u32[]{:S(2)}) collective-permute-start(bf16[32,4224]{1,0:T(8,128)(2,1)S(1)} %pad_maximum_fusion.3), channel_id=1, source_target_pairs={{0,12},{1,13},{2,14},{3,15},{4,8},{5,9},{6,10},{7,11},{8,4},{9,5},... | collective-permute-start | bytes 811016 | tf_op jit(solution)/shard_map/ppermute | solution.py:43
  31.7 8.0 %collective-permute-start.5 = (bf16[48,4224]{1,0:T(8,128)(2,1)S(1)}, bf16[48,4224]{1,0:T(8,128)(2,1)S(1)}, u32[]{:S(2)}, u32[]{:S(2)}) collective-permute-start(bf16[48,4224]{1,0:T(8,128)(2,1)S(1)} %pad_maximum_fusion.1), channel_id=1, source_target_pairs={{0,32},{1,33},{2,34},{3,35},{4,36},{5,37},{6,38},{7,39},{8,40},{9,... | collective-permute-start | bytes 1216520 | tf_op jit(solution)/shard_map/ppermute | solution.py:43
  33.5 9.2 %collective-permute-start.8 = (bf16[48,4224]{1,0:T(8,128)(2,1)S(1)}, bf16[48,4224]{1,0:T(8,128)(2,1)S(1)}, u32[]{:S(2)}, u32[]{:S(2)}) collective-permute-start(bf16[48,4224]{1,0:T(8,128)(2,1)S(1)} %pad_maximum_fusion.2), channel_id=1, source_target_pairs={{0,96},{1,97},{2,98},{3,99},{4,100},{5,101},{6,102},{7,103},{8,104... | collective-permute-start | bytes 1216520 | tf_op jit(solution)/shard_map/ppermute | solution.py:43
  42.9 4.3 %collective-permute-start.13 = (bf16[256,4224]{1,0:T(8,128)(2,1)S(1)}, bf16[256,4224]{1,0:T(8,128)(2,1)S(1)}, u32[]{:S(2)}, u32[]{:S(2)}) collective-permute-start(bf16[256,4224]{1,0:T(8,128)(2,1)S(1)} %get-tuple-element.43), channel_id=1, source_target_pairs={{0,16},{1,17},{2,18},{3,19},{4,20},{5,21},{6,22},{7,23},{8,24},{9,... | collective-permute-start | bytes 6488072 | tf_op jit(solution)/shard_map/ppermute | solution.py:55
  43.0 13.5 %collective-permute-start.9 = (bf16[96,4224]{1,0:T(8,128)(2,1)S(1)}, bf16[96,4224]{1,0:T(8,128)(2,1)S(1)}, u32[]{:S(2)}, u32[]{:S(2)}) collective-permute-start(bf16[96,4224]{1,0:T(8,128)(2,1)S(1)} %get-tuple-element.40.refs_1_), channel_id=1, source_target_pairs={{0,12},{1,13},{2,14},{3,15},{4,8},{5,9},{6,10},{7,11},{8,4},{9,5},... | collective-permute-start | bytes 2433032 | tf_op jit(solution)/shard_map/ppermute | solution.py:43
  44.5 13.5 %collective-permute-start.6 = (bf16[96,4224]{1,0:T(8,128)(2,1)S(1)}, bf16[96,4224]{1,0:T(8,128)(2,1)S(1)}, u32[]{:S(2)}, u32[]{:S(2)}) collective-permute-start(bf16[96,4224]{1,0:T(8,128)(2,1)S(1)} %get-tuple-element.42.refs_0_), channel_id=1, source_target_pairs={{0,96},{1,97},{2,98},{3,99},{4,100},{5,101},{6,102},{7,103},{8,104... | collective-permute-start | bytes 2433032 | tf_op jit(solution)/shard_map/ppermute | solution.py:43
  44.5 9.4 %collective-permute-start.12 = (bf16[64,4224]{1,0:T(8,128)(2,1)S(1)}, bf16[64,4224]{1,0:T(8,128)(2,1)S(1)}, u32[]{:S(2)}, u32[]{:S(2)}) collective-permute-start(bf16[64,4224]{1,0:T(8,128)(2,1)S(1)} %get-tuple-element.44.refs_2_), channel_id=1, source_target_pairs={{0,32},{1,33},{2,34},{3,35},{4,36},{5,37},{6,38},{7,39},{8,40},{9,... | collective-permute-start | bytes 1622024 | tf_op jit(solution)/shard_map/ppermute | solution.py:43
  58.1 4.5 %collective-permute-start.14 = (bf16[256,4224]{1,0:T(8,128)(2,1)S(1)}, bf16[256,4224]{1,0:T(8,128)(2,1)S(1)}, u32[]{:S(2)}, u32[]{:S(2)}) collective-permute-start(bf16[256,4224]{1,0:T(8,128)(2,1)S(1)} %pad_maximum_fusion), channel_id=1, source_target_pairs={{0,16},{1,17},{2,18},{3,19},{4,20},{5,21},{6,22},{7,23},{8,24},{9,... | collective-permute-start | bytes 6488072 | tf_op jit(solution)/shard_map/ppermute | solution.py:55
  65.3 1.3 %collective-permute-start.15 = (f32[3,8,128]{2,1,0:T(8,128)S(1)}, f32[3,8,128]{2,1,0:T(8,128)S(1)}, u32[]{:S(2)}, u32[]{:S(2)}) collective-permute-start(f32[3,8,128]{2,1,0:T(8,128)S(1)} %get-tuple-element.25), channel_id=1, source_target_pairs={{0,16},{1,17},{2,18},{3,19},{4,20},{5,21},{6,22},{7,23},{8,24},{9,... | collective-permute-start | bytes 36872 | tf_op jit(solution)/shard_map/ppermute | solution.py:55
  66.6 3.7 %collective-permute-start.16 = (f32[3,8,128]{2,1,0:T(8,128)S(1)}, f32[3,8,128]{2,1,0:T(8,128)S(1)}, u32[]{:S(2)}, u32[]{:S(2)}) collective-permute-start(f32[3,8,128]{2,1,0:T(8,128)S(1)} %pad_maximum_fusion.4), channel_id=1, source_target_pairs={{0,48},{1,49},{2,50},{3,51},{4,52},{5,53},{6,54},{7,55},{8,56},{9,... | collective-permute-start | bytes 36872 | tf_op jit(solution)/shard_map/ppermute | solution.py:51
  66.7 4.4 %collective-permute-start.17 = (f32[3,8,128]{2,1,0:T(8,128)S(1)}, f32[3,8,128]{2,1,0:T(8,128)S(1)}, u32[]{:S(2)}, u32[]{:S(2)}) collective-permute-start(f32[3,8,128]{2,1,0:T(8,128)S(1)} %pad_maximum_fusion.4), channel_id=1, source_target_pairs={{0,112},{1,113},{2,114},{3,115},{4,116},{5,117},{6,118},{7,119},{8... | collective-permute-start | bytes 36872 | tf_op jit(solution)/shard_map/ppermute | solution.py:51
  66.8 4.9 %collective-permute-start.18 = (f32[3,8,128]{2,1,0:T(8,128)S(1)}, f32[3,8,128]{2,1,0:T(8,128)S(1)}, u32[]{:S(2)}, u32[]{:S(2)}) collective-permute-start(f32[3,8,128]{2,1,0:T(8,128)S(1)} %pad_maximum_fusion.4), channel_id=1, source_target_pairs={{0,80},{1,81},{2,82},{3,83},{4,84},{5,85},{6,86},{7,87},{8,88},{9,... | collective-permute-start | bytes 36872 | tf_op jit(solution)/shard_map/ppermute | solution.py:51
  71.7 3.8 %collective-permute-start.19 = (f32[3,8,128]{2,1,0:T(8,128)S(1)}, f32[3,8,128]{2,1,0:T(8,128)S(1)}, u32[]{:S(2)}, u32[]{:S(2)}) collective-permute-start(f32[3,8,128]{2,1,0:T(8,128)S(1)} %pad_maximum_fusion.5), channel_id=1, source_target_pairs={{0,20},{1,21},{2,22},{3,23},{4,16},{5,17},{6,18},{7,19},{8,28},{9,... | collective-permute-start | bytes 36872 | tf_op jit(solution)/shard_map/ppermute | solution.py:51
  71.8 4.4 %collective-permute-start.20 = (f32[3,8,128]{2,1,0:T(8,128)S(1)}, f32[3,8,128]{2,1,0:T(8,128)S(1)}, u32[]{:S(2)}, u32[]{:S(2)}) collective-permute-start(f32[3,8,128]{2,1,0:T(8,128)S(1)} %pad_maximum_fusion.5), channel_id=1, source_target_pairs={{0,28},{1,29},{2,30},{3,31},{4,24},{5,25},{6,26},{7,27},{8,20},{9,... | collective-permute-start | bytes 36872 | tf_op jit(solution)/shard_map/ppermute | solution.py:51
  73.8 4.6 %collective-permute-start.21 = (f32[3,8,128]{2,1,0:T(8,128)S(1)}, f32[3,8,128]{2,1,0:T(8,128)S(1)}, u32[]{:S(2)}, u32[]{:S(2)}) collective-permute-start(f32[3,8,128]{2,1,0:T(8,128)S(1)} %pad_maximum_fusion.5), channel_id=1, source_target_pairs={{0,24},{1,25},{2,26},{3,27},{4,28},{5,29},{6,30},{7,31},{8,16},{9,... | collective-permute-start | bytes 36872 | tf_op jit(solution)/shard_map/ppermute | solution.py:51
  78.5 3.7 %collective-permute-start.22 = (f32[3,8,128]{2,1,0:T(8,128)S(1)}, f32[3,8,128]{2,1,0:T(8,128)S(1)}, u32[]{:S(2)}, u32[]{:S(2)}) collective-permute-start(f32[3,8,128]{2,1,0:T(8,128)S(1)} %pad_maximum_fusion.6.refs_0_), channel_id=1, source_target_pairs={{0,17},{1,16},{2,19},{3,18},{4,21},{5,20},{6,23},{7,22},{8,25},{9,... | collective-permute-start | bytes 36872 | tf_op jit(solution)/shard_map/ppermute | solution.py:51
  78.5 4.4 %collective-permute-start.23 = (f32[3,8,128]{2,1,0:T(8,128)S(1)}, f32[3,8,128]{2,1,0:T(8,128)S(1)}, u32[]{:S(2)}, u32[]{:S(2)}) collective-permute-start(f32[3,8,128]{2,1,0:T(8,128)S(1)} %pad_maximum_fusion.6.refs_0_), channel_id=1, source_target_pairs={{0,19},{1,18},{2,17},{3,16},{4,23},{5,22},{6,21},{7,20},{8,27},{9,... | collective-permute-start | bytes 36872 | tf_op jit(solution)/shard_map/ppermute | solution.py:51
  78.6 4.9 %collective-permute-start.24 = (f32[3,8,128]{2,1,0:T(8,128)S(1)}, f32[3,8,128]{2,1,0:T(8,128)S(1)}, u32[]{:S(2)}, u32[]{:S(2)}) collective-permute-start(f32[3,8,128]{2,1,0:T(8,128)S(1)} %pad_maximum_fusion.6.refs_0_), channel_id=1, source_target_pairs={{0,18},{1,19},{2,16},{3,17},{4,22},{5,23},{6,20},{7,21},{8,26},{9,... | collective-permute-start | bytes 36872 | tf_op jit(solution)/shard_map/ppermute | solution.py:51

commit v4 on v3

--- a/solution.py
+++ b/solution.py
@@ -9,12 +9,11 @@
 BENCH = 40
 N_DEV = 128
 LAB = 128
-ROWS = (24, 24, 16)
-STARTS = (0, 24, 48)
-HALF_STARTS = (0, 96, 192)
+CUTS = (0, 32, 64)
+SETS = ((0, 1, 2, 4), (3, 6, 5), (7,))
 F32 = jnp.float32
-CHUNK = 256
 LIMIT = 12 << 20
+BLOCK = 64
 EARLY = (((2, 0), (2, 1), (1, 0)), ((0, 0), (0, 1), (1, 1)))
 LATE = (((1, 1), (0, 0), (0, 1)), ((2, 0), (2, 1), (1, 0)))
 
@@ -126,22 +125,21 @@
     )(hidden, jnp.concatenate(ints).reshape(1, -1))
 
 
-def scores(x_ref, at, w_ref, acc_ref):
+def scores(x_ref, w_ref, acc_ref):
     vocab, depth = w_ref.shape
     r, c = iota((8, LAB), 0), iota((8, LAB), 1)
     digit = jnp.where(c == 0, 65536.0, jnp.where(c == 1, 256.0, 1.0))
     sel = jnp.where((r == 5) & (c < 3), digit, jnp.where(((r == 3) | (r == 4)) & (r == c), 1.0, 0.0))
-    rows = pl.ds(at, CHUNK)
     labels = lax.dot_general(
-        sel.astype(jnp.bfloat16), x_ref[rows, depth:], NT, preferred_element_type=F32
+        sel.astype(jnp.bfloat16), x_ref[:, depth:], NT, preferred_element_type=F32
     )
-    acc_ref[...] = lax.dot_general(w_ref[...], x_ref[rows, :depth], NT, preferred_element_type=F32)
+    acc_ref[...] = lax.dot_general(w_ref[...], x_ref[:, :depth], NT, preferred_element_type=F32)
     logits = acc_ref[...]
     top = jnp.max(logits, axis=0, keepdims=True)
     total = jnp.sum(jnp.exp(logits - top), axis=0, keepdims=True)
     local = labels[5:6].astype(jnp.int32) - lax.axis_index("d") * vocab
     target = jnp.sum(jnp.where(iota(logits.shape, 0) == local, logits, 0.0), axis=0, keepdims=True)
-    k = iota((8, CHUNK), 0)
+    k = iota((8, x_ref.shape[0]), 0)
     return jnp.where(k == 0, top, jnp.where(k == 1, total, jnp.where(k == 2, target, labels)))
 
 
@@ -155,8 +153,7 @@
 def score_kernel(w_ref, *refs):
     *pieces, out_ref, x_ref, acc_ref = refs
     gather_rows(pieces, x_ref)
-    for at in range(0, x_ref.shape[0], CHUNK):
-        out_ref[:, at : at + CHUNK] = scores(x_ref, at, w_ref, acc_ref)
+    out_ref[...] = scores(x_ref, w_ref, acc_ref)
 
 
 def score(w, pieces):
@@ -169,7 +166,7 @@
         out_specs=VMEM,
         scratch_shapes=[
             pltpu.VMEM((rows, depth + LAB), jnp.bfloat16),
-            pltpu.VMEM((vocab, CHUNK), F32),
+            pltpu.VMEM((vocab, rows), F32),
         ],
         compiler_params=pltpu.CompilerParams(vmem_limit_bytes=LIMIT),
         cost_estimate=pl.CostEstimate(
@@ -179,41 +176,38 @@
     )(w, *pieces)
 
 
-def score_place_kernel(w_ref, first_ref, own_ref, *refs):
-    *pieces, stats_ref, labels_ref, x_ref, acc_ref, all_ref = refs
+def score_place_kernel(w_ref, *refs):
+    *refs, stats_ref, labels_ref, x_ref, acc_ref, all_ref = refs
+    done, pieces = refs[:4], refs[4:]
     gather_rows(pieces, x_ref)
-    sib = scores(x_ref, 0, w_ref, acc_ref)
+    last = scores(x_ref, w_ref, acc_ref)
     place_of, core = coords(lax.axis_index("d"))
     blocks = [cube_index(place_of, LATE[k]) for k in range(2)]
     is_first = core == 0
-    halves = ((first_ref[:, :CHUNK], first_ref[:, CHUNK:]), (own_ref[...], sib))
-    for half, (a, b) in enumerate(halves):
-        by_core = (jnp.where(is_first, a, b), jnp.where(is_first, b, a))
-        for g in range(3):
-            for i in range(4):
-                r = 4 * half + i
-                rel = sum(((r >> k) & 1) << ((g + k) % 3) for k in range(3))
-                at = HALF_STARTS[g] + i * ROWS[g]
-                for side in range(2):
-                    to = side * 64 + STARTS[g]
-                    all_ref[blocks[side] ^ rel, :, to : to + ROWS[g]] = by_core[side][:, at : at + ROWS[g]]
+    pairs = [(done[0][...], done[1][...]), (done[2][...], done[3][...]), (last[:, :BLOCK], last[:, BLOCK:])]
+    for rels, (own, sib) in zip(SETS, pairs):
+        by_core = (jnp.where(is_first, own, sib), jnp.where(is_first, sib, own))
+        for i, rel in enumerate(rels):
+            for side in range(2):
+                to = side * BLOCK
+                all_ref[blocks[side] ^ rel, :, to : to + BLOCK] = by_core[side][:, i * BLOCK : (i + 1) * BLOCK]
     for kind in range(3):
         stats_ref[kind] = all_ref[:, kind, :]
     for kind in range(2):
         labels_ref[kind] = all_ref[:, 3 + kind, :]
 
 
-def score_place(w, first, own, pieces):
+def score_place(w, done, pieces):
     vocab, depth = w.shape
     rows = sum(p.shape[0] for p in pieces)
     return pl.pallas_call(
         score_place_kernel,
         out_shape=(jax.ShapeDtypeStruct((3, 8, 128), F32), jax.ShapeDtypeStruct((2, 8, 128), F32)),
-        in_specs=[VMEM] * (3 + len(pieces)),
+        in_specs=[VMEM] * (1 + len(done) + len(pieces)),
         out_specs=(VMEM, VMEM),
         scratch_shapes=[
             pltpu.VMEM((rows, depth + LAB), jnp.bfloat16),
-            pltpu.VMEM((vocab, CHUNK), F32),
+            pltpu.VMEM((vocab, rows), F32),
             pltpu.VMEM((8, 8, 128), F32),
         ],
         compiler_params=pltpu.CompilerParams(vmem_limit_bytes=LIMIT),
@@ -221,7 +215,7 @@
             flops=2 * rows * vocab * depth, bytes_accessed=2 * vocab * depth, transcendentals=rows * vocab
         ),
         name="score_place",
-    )(w, first, own, *pieces)
+    )(w, *done, *pieces)
 
 
 def merged(parts):
@@ -277,6 +271,25 @@
     return lax.optimization_barrier(arrays)
 
 
+def fetch_kernel(w_ref, out_ref, sem):
+    move = pltpu.make_async_copy(w_ref, out_ref, sem)
+    move.start()
+    move.wait()
+
+
+def fetch(w):
+    return pl.pallas_call(
+        fetch_kernel,
+        out_shape=jax.ShapeDtypeStruct(w.shape, w.dtype),
+        in_specs=[pl.BlockSpec(memory_space=pl.ANY)],
+        out_specs=VMEM,
+        scratch_shapes=[pltpu.SemaphoreType.DMA],
+        compiler_params=pltpu.CompilerParams(vmem_limit_bytes=LIMIT),
+        cost_estimate=pl.CostEstimate(flops=0, bytes_accessed=2 * w.size, transcendentals=0),
+        name="fetch",
+    )(w)
+
+
 def ordered(low, a, b):
     return jnp.where(low, jnp.concatenate([a, b], 0), jnp.concatenate([b, a], 0))
 
@@ -289,17 +302,21 @@
     both, first, second = (exchange(x, [d[s] for d in EARLY]) for s in (slice(0, 2), slice(0, 1), slice(1, 2)))
     x = ordered(low[1], ordered(low[0], x, first), ordered(low[0], second, both))
     x = ordered(low[2], x, exchange(x, [d[2:] for d in EARLY]))
-    held = tied(*(x[s : s + n] for s, n in zip(STARTS, ROWS)))
-    for k in range(2):
-        got = [late_exchange(held[g], g + k) for g in range(3)]
-        held = [jnp.concatenate([a, b], 0) for a, b in zip(held, got)]
-    w = head_weight.T
-    last = [late_exchange(held[g], g + 2) for g in range(3)]
-    first = score(w, [*held, core_swap(jnp.concatenate(held, 0))])
-    *last, first = tied(*last, first)
-    other = core_swap(jnp.concatenate(last, 0))
-    own = score(w, last)
-    stats, labels = score_place(w, first, own, [other])
+    x, w = tied(x, fetch(head_weight.T))
+    near = [late_exchange(x, k) for k in range(3)]
+    near_rows = [x, *near]
+    own1 = score(w, near_rows)
+    sib1 = score(w, [core_swap(jnp.concatenate(near_rows, 0))])
+    far = [late_exchange(near[(k + 1) % 3], k) for k in range(3)]
+    *far, own1, sib1 = tied(*far, own1, sib1)
+    own2 = score(w, far)
+    sib2 = score(w, [core_swap(jnp.concatenate(far, 0))])
+    spans = zip(CUTS, CUTS[1:])
+    last = jnp.concatenate(
+        [late_exchange(far[(k + 1) % 3][i:j], k) for k, (i, j) in enumerate(spans)], 0
+    )
+    last, own2 = tied(last, own2)
+    stats, labels = score_place(w, (own1, sib1, own2, sib2), [last, core_swap(last)])
     parts = [stats, core_swap(stats)]
     for axis in range(3):
         stats = jnp.stack(merged(parts))

time: 85.7 us -> 83.9 us (0.979)
  starting transfers between devices: 32.3 us -> 27.8 us
  waiting for transfers between devices: 37.1 us -> 33.4 us
  Pallas kernels: 11.4 us -> 15 us
  local copies, waits for them, and re-layouts: 1.34 us -> 4.29 us
    ppermute x3 -> x4, waiting for transfers between devices: 4.72 us -> 0.9 us  [core_swap(): return lax.ppermute(v, 'd', [(d, d ^ 16) for d in range(N_DEV)])]
    ppermute x13 -> x12, starting transfers between devices: 20.6 us -> 17.4 us  [exchange(): lax.ppermute(v, 'd', [(d, flipped(d, by_core[coords(d)[1]])) for d in ran...]
    unnamed x12 -> x4, local copies, waits for them, and re-layouts: 1.25 us -> 4.25 us
    pallas_call x2 -> x4, Pallas kernels: 7.51 us -> 10.5 us  [score(): pl.pallas_call(score_kernel, out_shape=jax.ShapeDtypeStruct((8, rows), F3...]
    ppermute x9, waiting for transfers between devices: 5.74 us -> 7.45 us  [cross_exchange(): lax.ppermute(v, 'd', [(d, flipped(d, dims) ^ 16) for d in range(N_DEV)])]
    ppermute x9, starting transfers between devices: 11.1 us -> 9.41 us  [cross_exchange(): lax.ppermute(v, 'd', [(d, flipped(d, dims) ^ 16) for d in range(N_DEV)])]
    ppermute x13 -> x12, waiting for transfers between devices: 26.7 us -> 25 us  [exchange(): lax.ppermute(v, 'd', [(d, flipped(d, by_core[coords(d)[1]])) for d in ran...]
  transfers between devices with their start and end apart: 25 -> 25, of which waited for: 19 -> 18; matrix products, arithmetic and copies ran while one was open for 1% -> 0% of each run, Pallas kernels for 9% -> 14%
where the time goes in v4:
time: 83.9 us; the launch traced here: 82.6 us
  waiting for transfers between devices  33.4 us (40%)
  starting transfers between devices  27.8 us (33%)
  Pallas kernels  15 us (18%)
  local copies, waits for them, and re-layouts  4.29 us (5%)
  other arithmetic  1.32 us (2%)
    ppermute x12, waiting for transfers between devices, exchange(): lax.ppermute(v, 'd', [(d, flipped(d, by_core[coords(d)[1]])) for d in ran...  25 us
    ppermute x12, starting transfers between devices, exchange(): lax.ppermute(v, 'd', [(d, flipped(d, by_core[coords(d)[1]])) for d in ran...  17.4 us
    pallas_call x4, Pallas kernels, score(): pl.pallas_call(score_kernel, out_shape=jax.ShapeDtypeStruct((8, rows), F3...  10.5 us
    ppermute x9, starting transfers between devices, cross_exchange(): lax.ppermute(v, 'd', [(d, flipped(d, dims) ^ 16) for d in range(N_DEV)])  9.41 us
    ppermute x9, waiting for transfers between devices, cross_exchange(): lax.ppermute(v, 'd', [(d, flipped(d, dims) ^ 16) for d in range(N_DEV)])  7.45 us
    unnamed x4, local copies, waits for them, and re-layouts  4.25 us
    pallas_call x1, Pallas kernels, score_place(): pl.pallas_call(score_place_kernel, out_shape=(jax.ShapeDtypeStruct((3, 8,...  2.55 us
  transfers between devices with their start and end apart: 25, of which 18 were waited for; matrix products, arithmetic and copies ran while one was open for 0% of the time, Pallas kernels for 14%

profile of v4, /device:TPU:0, one launch (start us, length us, event | category | flops | bytes accessed | tf_op | source)
XLA Modules:
  0.0 82.6 jit_solution(16654468072311243526)
XLA Ops:
  1.4 0.9 %copy-done.1 = bf16[16,4096]{1,0:T(8,128)(2,1)S(1)} copy-done((bf16[16,4096]{1,0:T(8,128)(2,1)S(1)}, bf16[16,4096]{1,0:T(8,128)(2,1)}, u32[]{:S(2)}) %copy-start.1) | copy-done | bytes 131096
  2.8 1.7 %collective-permute-start = (bf16[8,4224]{1,0:T(8,128)(2,1)S(1)}, bf16[8,4224]{1,0:T(8,128)(2,1)S(1)}, u32[]{:S(2)}, u32[]{:S(2)}) collective-permute-start(bf16[8,4224]{1,0:T(8,128)(2,1)S(1)} %get-tuple-element.19), channel_id=1, source_target_pairs={{0,1},{1,0},{2,3},{3,2},{4,5},{5,4},{6,7},{7,6},{8,9},{9,8},{10,11... | collective-permute-start | bytes 202760 | tf_op jit(solution)/shard_map/ppermute | solution.py:42
  4.5 2.1 %collective-permute-start.1 = (bf16[8,4224]{1,0:T(8,128)(2,1)S(1)}, bf16[8,4224]{1,0:T(8,128)(2,1)S(1)}, u32[]{:S(2)}, u32[]{:S(2)}) collective-permute-start(bf16[8,4224]{1,0:T(8,128)(2,1)S(1)} %get-tuple-element.19), channel_id=1, source_target_pairs={{0,3},{1,2},{2,1},{3,0},{4,7},{5,6},{6,5},{7,4},{8,11},{9,10},{10,... | collective-permute-start | bytes 202760 | tf_op jit(solution)/shard_map/ppermute | solution.py:42
  7.2 2.7 %collective-permute-done.1 = bf16[8,4224]{1,0:T(8,128)(2,1)S(1)} collective-permute-done((bf16[8,4224]{1,0:T(8,128)(2,1)S(1)}, bf16[8,4224]{1,0:T(8,128)(2,1)S(1)}, u32[]{:S(2)}, u32[]{:S(2)}) %collective-permute-start.1) | collective-permute-done | bytes 67616 | tf_op jit(solution)/shard_map/ppermute | solution.py:42
  10.0 2.4 %collective-permute-done.2 = bf16[8,4224]{1,0:T(8,128)(2,1)S(1)} collective-permute-done((bf16[8,4224]{1,0:T(8,128)(2,1)S(1)}, bf16[8,4224]{1,0:T(8,128)(2,1)S(1)}, u32[]{:S(2)}, u32[]{:S(2)}) %collective-permute-start.2) | collective-permute-done | bytes 67616 | tf_op jit(solution)/shard_map/ppermute | solution.py:42
  12.4 1.7 %collective-permute-start.3 = (bf16[32,4224]{1,0:T(8,128)(2,1)S(1)}, bf16[32,4224]{1,0:T(8,128)(2,1)S(1)}, u32[]{:S(2)}, u32[]{:S(2)}) collective-permute-start(bf16[32,4224]{1,0:T(8,128)(2,1)S(1)} %maximum_select_fusion.1), channel_id=1, source_target_pairs={{0,4},{1,5},{2,6},{3,7},{4,0},{5,1},{6,2},{7,3},{8,12},{9,13},{10,... | collective-permute-start | bytes 811016 | tf_op jit(solution)/shard_map/ppermute | solution.py:42
  14.1 3.3 %copy-done = bf16[4096,1002]{0,1:T(8,128)(2,1)S(1)} copy-done((bf16[4096,1002]{0,1:T(8,128)(2,1)S(1)}, bf16[4096,1002]{0,1:T(8,128)(2,1)}, u32[]{:S(2)}) %copy-start) | copy-done | bytes 8208408
  19.1 3.1 %collective-permute-start.8 = (bf16[64,4224]{1,0:T(8,128)(2,1)S(1)}, bf16[64,4224]{1,0:T(8,128)(2,1)S(1)}, u32[]{:S(2)}, u32[]{:S(2)}) collective-permute-start(bf16[64,4224]{1,0:T(8,128)(2,1)S(1)} %maximum_select_fusion.refs_0_), channel_id=1, source_target_pairs={{0,12},{1,13},{2,14},{3,15},{4,8},{5,9},{6,10},{7,11},{8,4},{9,5},... | collective-permute-start | bytes 1622024 | tf_op jit(solution)/shard_map/ppermute | solution.py:42
  22.2 4.3 %collective-permute-start.6 = (bf16[64,4224]{1,0:T(8,128)(2,1)S(1)}, bf16[64,4224]{1,0:T(8,128)(2,1)S(1)}, u32[]{:S(2)}, u32[]{:S(2)}) collective-permute-start(bf16[64,4224]{1,0:T(8,128)(2,1)S(1)} %maximum_select_fusion.refs_0_), channel_id=1, source_target_pairs={{0,96},{1,97},{2,98},{3,99},{4,100},{5,101},{6,102},{7,103},{8,104... | collective-permute-start | bytes 1622024 | tf_op jit(solution)/shard_map/ppermute | solution.py:42
  26.4 3.3 %collective-permute-done.8.refs_1_ = bf16[64,4224]{1,0:T(8,128)(2,1)S(1)} collective-permute-done((bf16[64,4224]{1,0:T(8,128)(2,1)S(1)}, bf16[64,4224]{1,0:T(8,128)(2,1)S(1)}, u32[]{:S(2)}, u32[]{:S(2)}) %collective-permute-start.8) | collective-permute-done | bytes 540704 | tf_op jit(solution)/shard_map/ppermute | solution.py:42
  29.7 4.1 %collective-permute-done.6.refs_3_ = bf16[64,4224]{1,0:T(8,128)(2,1)S(1)} collective-permute-done((bf16[64,4224]{1,0:T(8,128)(2,1)S(1)}, bf16[64,4224]{1,0:T(8,128)(2,1)S(1)}, u32[]{:S(2)}, u32[]{:S(2)}) %collective-permute-start.6) | collective-permute-done | bytes 540704 | tf_op jit(solution)/shard_map/ppermute | solution.py:42
  33.8 2.0 %collective-permute-done.4.refs_2_ = bf16[64,4224]{1,0:T(8,128)(2,1)S(1)} collective-permute-done((bf16[64,4224]{1,0:T(8,128)(2,1)S(1)}, bf16[64,4224]{1,0:T(8,128)(2,1)S(1)}, u32[]{:S(2)}, u32[]{:S(2)}) %collective-permute-start.4) | collective-permute-done | bytes 540704 | tf_op jit(solution)/shard_map/ppermute | solution.py:42
  36.0 1.3 %collective-permute-start.9 = (bf16[64,4224]{1,0:T(8,128)(2,1)S(1)}, bf16[64,4224]{1,0:T(8,128)(2,1)S(1)}, u32[]{:S(2)}, u32[]{:S(2)}) collective-permute-start(bf16[64,4224]{1,0:T(8,128)(2,1)S(1)} %collective-permute-done.8.refs_1_), channel_id=1, source_target_pairs={{0,96},{1,97},{2,98},{3,99},{4,100},{5,101},{6,102},{7,103},{8,104... | collective-permute-start | bytes 1622024 | tf_op jit(solution)/shard_map/ppermute | solution.py:42
  37.6 2.6 %score.4.refs_0_ = f32[8,256]{1,0:T(8,128)S(1)} custom-call(bf16[1002,4096]{1,0:T(8,128)(2,1)S(1)} %fetch.1.w_ref, bf16[64,4224]{1,0:T(8,128)(2,1)S(1)} %maximum_select_fusion.refs_0_, bf16[64,4224]{1,0:T(8,128)(2,1)S(1)} %collective-permute-done.8.refs_1_, bf16[64,4224]{1,0:T(8,128)(2,1)S(1)} %collective-permute-done.4.refs_2_, ...), custom_call_target="tpu_custom_call" | custom-call | flops 2101346304 | bytes 8208384 | tf_op jit(solution)/shard_map/score/pallas_call | solution.py:162
  40.3 2.6 %score.5.refs_1_ = f32[8,256]{1,0:T(8,128)S(1)} custom-call(bf16[1002,4096]{1,0:T(8,128)(2,1)S(1)} %fetch.1.w_ref, bf16[256,4224]{1,0:T(8,128)(2,1)S(1)} %collective-permute-done.10.refs_0_), custom_call_target="tpu_custom_call" | custom-call | flops 2101346304 | bytes 8208384 | tf_op jit(solution)/shard_map/score/pallas_call | solution.py:162
  42.9 3.8 %collective-permute-done.9.refs_2_ = bf16[64,4224]{1,0:T(8,128)(2,1)S(1)} collective-permute-done((bf16[64,4224]{1,0:T(8,128)(2,1)S(1)}, bf16[64,4224]{1,0:T(8,128)(2,1)S(1)}, u32[]{:S(2)}, u32[]{:S(2)}) %collective-permute-start.9) | collective-permute-done | bytes 540704 | tf_op jit(solution)/shard_map/ppermute | solution.py:42
  46.7 1.2 %collective-permute-done.5.refs_0_ = bf16[64,4224]{1,0:T(8,128)(2,1)S(1)} collective-permute-done((bf16[64,4224]{1,0:T(8,128)(2,1)S(1)}, bf16[64,4224]{1,0:T(8,128)(2,1)S(1)}, u32[]{:S(2)}, u32[]{:S(2)}) %collective-permute-start.5) | collective-permute-done | bytes 540704 | tf_op jit(solution)/shard_map/ppermute | solution.py:42
  48.2 2.1 %collective-permute-start.12 = (bf16[32,4224]{1,0:T(8,128)(2,1)S(1)}, bf16[32,4224]{1,0:T(8,128)(2,1)S(1)}, u32[]{:S(2)}, u32[]{:S(2)}) collective-permute-start(bf16[32,4224]{1,0:T(8,128)(2,1)S(1)} %slice.87), channel_id=1, source_target_pairs={{0,32},{1,33},{2,34},{3,35},{4,36},{5,37},{6,38},{7,39},{8,40},{9,... | collective-permute-start | bytes 811016 | tf_op jit(solution)/shard_map/ppermute | solution.py:42
  50.6 2.7 %score.6.refs_2_ = f32[8,192]{1,0:T(8,128)S(1)} custom-call(bf16[1002,4096]{1,0:T(8,128)(2,1)S(1)} %fetch.1.w_ref, bf16[64,4224]{1,0:T(8,128)(2,1)S(1)} %collective-permute-done.5.refs_0_, bf16[64,4224]{1,0:T(8,128)(2,1)S(1)} %collective-permute-done.7.refs_1_, bf16[64,4224]{1,0:T(8,128)(2,1)S(1)} %collective-permute-done.9.refs_2_), custom_call_target="tpu_custom_call" | custom-call | flops 1576009728 | bytes 8208384 | tf_op jit(solution)/shard_map/score/pallas_call | solution.py:162
  53.2 1.5 %collective-permute-done.12 = bf16[32,4224]{1,0:T(8,128)(2,1)S(1)} collective-permute-done((bf16[32,4224]{1,0:T(8,128)(2,1)S(1)}, bf16[32,4224]{1,0:T(8,128)(2,1)S(1)}, u32[]{:S(2)}, u32[]{:S(2)}) %collective-permute-start.12) | collective-permute-done | bytes 270368 | tf_op jit(solution)/shard_map/ppermute | solution.py:42
  54.7 3.2 %collective-permute-done.11 = bf16[32,4224]{1,0:T(8,128)(2,1)S(1)} collective-permute-done((bf16[32,4224]{1,0:T(8,128)(2,1)S(1)}, bf16[32,4224]{1,0:T(8,128)(2,1)S(1)}, u32[]{:S(2)}, u32[]{:S(2)}) %collective-permute-start.11) | collective-permute-done | bytes 270368 | tf_op jit(solution)/shard_map/ppermute | solution.py:42
  58.3 2.7 %score.7.refs_3_ = f32[8,192]{1,0:T(8,128)S(1)} custom-call(bf16[1002,4096]{1,0:T(8,128)(2,1)S(1)} %fetch.1.w_ref, bf16[192,4224]{1,0:T(8,128)(2,1)S(1)} %collective-permute-done.13.refs_0_), custom_call_target="tpu_custom_call" | custom-call | flops 1576009728 | bytes 8208384 | tf_op jit(solution)/shard_map/score/pallas_call | solution.py:162
  60.9 2.6 %score_place.1 = (f32[3,8,128]{2,1,0:T(8,128)S(1)}, f32[2,8,128]{2,1,0:T(8,128)S(1)}) custom-call(bf16[1002,4096]{1,0:T(8,128)(2,1)S(1)} %fetch.1.w_ref, f32[8,256]{1,0:T(8,128)S(1)} %score.4.refs_0_, f32[8,256]{1,0:T(8,128)S(1)} %score.5.refs_1_, f32[8,192]{1,0:T(8,128)S(1)} %score.6.refs_2_, f32[8,192]{1,0:T(8,128)S(1)} %score.7.refs_3_, ...), custom_call_target="tpu_custom_call" | custom-call | flops 1050673152 | bytes 8208384 | tf_op jit(solution)/shard_map/score_place/pallas_call | solution.py:203
  64.9 1.6 %collective-permute-start.18 = (f32[3,8,128]{2,1,0:T(8,128)S(1)}, f32[3,8,128]{2,1,0:T(8,128)S(1)}, u32[]{:S(2)}, u32[]{:S(2)}) collective-permute-start(f32[3,8,128]{2,1,0:T(8,128)S(1)} %pad_maximum_fusion.3), channel_id=1, source_target_pairs={{0,80},{1,81},{2,82},{3,83},{4,84},{5,85},{6,86},{7,87},{8,88},{9,... | collective-permute-start | bytes 36872 | tf_op jit(solution)/shard_map/ppermute | solution.py:50
  66.5 1.0 %collective-permute-start.17 = (f32[3,8,128]{2,1,0:T(8,128)S(1)}, f32[3,8,128]{2,1,0:T(8,128)S(1)}, u32[]{:S(2)}, u32[]{:S(2)}) collective-permute-start(f32[3,8,128]{2,1,0:T(8,128)S(1)} %pad_maximum_fusion.3), channel_id=1, source_target_pairs={{0,112},{1,113},{2,114},{3,115},{4,116},{5,117},{6,118},{7,119},{8... | collective-permute-start | bytes 36872 | tf_op jit(solution)/shard_map/ppermute | solution.py:50
  68.2 1.5 %collective-permute-done.18 = f32[3,8,128]{2,1,0:T(8,128)S(1)} collective-permute-done((f32[3,8,128]{2,1,0:T(8,128)S(1)}, f32[3,8,128]{2,1,0:T(8,128)S(1)}, u32[]{:S(2)}, u32[]{:S(2)}) %collective-permute-start.18) | collective-permute-done | bytes 12320 | tf_op jit(solution)/shard_map/ppermute | solution.py:50
  69.6 1.2 %collective-permute-done.17 = f32[3,8,128]{2,1,0:T(8,128)S(1)} collective-permute-done((f32[3,8,128]{2,1,0:T(8,128)S(1)}, f32[3,8,128]{2,1,0:T(8,128)S(1)}, u32[]{:S(2)}, u32[]{:S(2)}) %collective-permute-start.17) | collective-permute-done | bytes 12320 | tf_op jit(solution)/shard_map/ppermute | solution.py:50
  71.6 2.3 %collective-permute-start.19 = (f32[3,8,128]{2,1,0:T(8,128)S(1)}, f32[3,8,128]{2,1,0:T(8,128)S(1)}, u32[]{:S(2)}, u32[]{:S(2)}) collective-permute-start(f32[3,8,128]{2,1,0:T(8,128)S(1)} %pad_maximum_fusion.4), channel_id=1, source_target_pairs={{0,20},{1,21},{2,22},{3,23},{4,16},{5,17},{6,18},{7,19},{8,28},{9,... | collective-permute-start | bytes 36872 | tf_op jit(solution)/shard_map/ppermute | solution.py:50
  73.9 1.6 %collective-permute-done.21 = f32[3,8,128]{2,1,0:T(8,128)S(1)} collective-permute-done((f32[3,8,128]{2,1,0:T(8,128)S(1)}, f32[3,8,128]{2,1,0:T(8,128)S(1)}, u32[]{:S(2)}, u32[]{:S(2)}) %collective-permute-start.21) | collective-permute-done | bytes 12320 | tf_op jit(solution)/shard_map/ppermute | solution.py:50
  76.3 2.5 %collective-permute-start.23 = (f32[3,8,128]{2,1,0:T(8,128)S(1)}, f32[3,8,128]{2,1,0:T(8,128)S(1)}, u32[]{:S(2)}, u32[]{:S(2)}) collective-permute-start(f32[3,8,128]{2,1,0:T(8,128)S(1)} %pad_maximum_fusion.5.refs_0_), channel_id=1, source_target_pairs={{0,19},{1,18},{2,17},{3,16},{4,23},{5,22},{6,21},{7,20},{8,27},{9,... | collective-permute-start | bytes 36872 | tf_op jit(solution)/shard_map/ppermute | solution.py:50
  78.7 1.6 %collective-permute-done.24.refs_3_ = f32[3,8,128]{2,1,0:T(8,128)S(1)} collective-permute-done((f32[3,8,128]{2,1,0:T(8,128)S(1)}, f32[3,8,128]{2,1,0:T(8,128)S(1)}, u32[]{:S(2)}, u32[]{:S(2)}) %collective-permute-start.24) | collective-permute-done | bytes 12320 | tf_op jit(solution)/shard_map/ppermute | solution.py:50
  80.6 1.2 %collective-permute-done.22.refs_1_ = f32[3,8,128]{2,1,0:T(8,128)S(1)} collective-permute-done((f32[3,8,128]{2,1,0:T(8,128)S(1)}, f32[3,8,128]{2,1,0:T(8,128)S(1)}, u32[]{:S(2)}, u32[]{:S(2)}) %collective-permute-start.22) | collective-permute-done | bytes 12320 | tf_op jit(solution)/shard_map/ppermute | solution.py:50
  (46 shorter events, 9.7 us)
Async XLA Ops:
  1.4 0.9 %copy-start.1 = (bf16[16,4096]{1,0:T(8,128)(2,1)S(1)}, bf16[16,4096]{1,0:T(8,128)(2,1)}, u32[]{:S(2)}) copy-start(bf16[16,4096]{1,0:T(8,128)(2,1)} %hidden_ref.1) | copy-start | bytes 393220
  2.8 4.4 %collective-permute-start = (bf16[8,4224]{1,0:T(8,128)(2,1)S(1)}, bf16[8,4224]{1,0:T(8,128)(2,1)S(1)}, u32[]{:S(2)}, u32[]{:S(2)}) collective-permute-start(bf16[8,4224]{1,0:T(8,128)(2,1)S(1)} %get-tuple-element.19), channel_id=1, source_target_pairs={{0,1},{1,0},{2,3},{3,2},{4,5},{5,4},{6,7},{7,6},{8,9},{9,8},{10,11... | collective-permute-start | bytes 202760 | tf_op jit(solution)/shard_map/ppermute | solution.py:42
  4.5 5.5 %collective-permute-start.1 = (bf16[8,4224]{1,0:T(8,128)(2,1)S(1)}, bf16[8,4224]{1,0:T(8,128)(2,1)S(1)}, u32[]{:S(2)}, u32[]{:S(2)}) collective-permute-start(bf16[8,4224]{1,0:T(8,128)(2,1)S(1)} %get-tuple-element.19), channel_id=1, source_target_pairs={{0,3},{1,2},{2,1},{3,0},{4,7},{5,6},{6,5},{7,4},{8,11},{9,10},{10,... | collective-permute-start | bytes 202760 | tf_op jit(solution)/shard_map/ppermute | solution.py:42
  6.6 5.8 %collective-permute-start.2 = (bf16[8,4224]{1,0:T(8,128)(2,1)S(1)}, bf16[8,4224]{1,0:T(8,128)(2,1)S(1)}, u32[]{:S(2)}, u32[]{:S(2)}) collective-permute-start(bf16[8,4224]{1,0:T(8,128)(2,1)S(1)} %get-tuple-element.19), channel_id=1, source_target_pairs={{0,2},{1,3},{2,0},{3,1},{4,6},{5,7},{6,4},{7,5},{8,10},{9,11},{10,... | collective-permute-start | bytes 202760 | tf_op jit(solution)/shard_map/ppermute | solution.py:42
  12.4 6.5 %collective-permute-start.3 = (bf16[32,4224]{1,0:T(8,128)(2,1)S(1)}, bf16[32,4224]{1,0:T(8,128)(2,1)S(1)}, u32[]{:S(2)}, u32[]{:S(2)}) collective-permute-start(bf16[32,4224]{1,0:T(8,128)(2,1)S(1)} %maximum_select_fusion.1), channel_id=1, source_target_pairs={{0,4},{1,5},{2,6},{3,7},{4,0},{5,1},{6,2},{7,3},{8,12},{9,13},{10,... | collective-permute-start | bytes 811016 | tf_op jit(solution)/shard_map/ppermute | solution.py:42
  14.1 3.3 %copy-start = (bf16[4096,1002]{0,1:T(8,128)(2,1)S(1)}, bf16[4096,1002]{0,1:T(8,128)(2,1)}, u32[]{:S(2)}) copy-start(bf16[4096,1002]{0,1:T(8,128)(2,1)} %param.7) | copy-start | bytes 24625156
  19.1 10.6 %collective-permute-start.8 = (bf16[64,4224]{1,0:T(8,128)(2,1)S(1)}, bf16[64,4224]{1,0:T(8,128)(2,1)S(1)}, u32[]{:S(2)}, u32[]{:S(2)}) collective-permute-start(bf16[64,4224]{1,0:T(8,128)(2,1)S(1)} %maximum_select_fusion.refs_0_), channel_id=1, source_target_pairs={{0,12},{1,13},{2,14},{3,15},{4,8},{5,9},{6,10},{7,11},{8,4},{9,5},... | collective-permute-start | bytes 1622024 | tf_op jit(solution)/shard_map/ppermute | solution.py:42
  22.2 11.6 %collective-permute-start.6 = (bf16[64,4224]{1,0:T(8,128)(2,1)S(1)}, bf16[64,4224]{1,0:T(8,128)(2,1)S(1)}, u32[]{:S(2)}, u32[]{:S(2)}) collective-permute-start(bf16[64,4224]{1,0:T(8,128)(2,1)S(1)} %maximum_select_fusion.refs_0_), channel_id=1, source_target_pairs={{0,96},{1,97},{2,98},{3,99},{4,100},{5,101},{6,102},{7,103},{8,104... | collective-permute-start | bytes 1622024 | tf_op jit(solution)/shard_map/ppermute | solution.py:42
  26.4 9.4 %collective-permute-start.4 = (bf16[64,4224]{1,0:T(8,128)(2,1)S(1)}, bf16[64,4224]{1,0:T(8,128)(2,1)S(1)}, u32[]{:S(2)}, u32[]{:S(2)}) collective-permute-start(bf16[64,4224]{1,0:T(8,128)(2,1)S(1)} %maximum_select_fusion.refs_0_), channel_id=1, source_target_pairs={{0,32},{1,33},{2,34},{3,35},{4,36},{5,37},{6,38},{7,39},{8,40},{9,... | collective-permute-start | bytes 1622024 | tf_op jit(solution)/shard_map/ppermute | solution.py:42
  35.9 4.3 %collective-permute-start.10 = (bf16[256,4224]{1,0:T(8,128)(2,1)S(1)}, bf16[256,4224]{1,0:T(8,128)(2,1)S(1)}, u32[]{:S(2)}, u32[]{:S(2)}) collective-permute-start(bf16[256,4224]{1,0:T(8,128)(2,1)S(1)} %pad_maximum_fusion), channel_id=1, source_target_pairs={{0,16},{1,17},{2,18},{3,19},{4,20},{5,21},{6,22},{7,23},{8,24},{9,... | collective-permute-start | bytes 6488072 | tf_op jit(solution)/shard_map/ppermute | solution.py:54
  36.0 10.6 %collective-permute-start.9 = (bf16[64,4224]{1,0:T(8,128)(2,1)S(1)}, bf16[64,4224]{1,0:T(8,128)(2,1)S(1)}, u32[]{:S(2)}, u32[]{:S(2)}) collective-permute-start(bf16[64,4224]{1,0:T(8,128)(2,1)S(1)} %collective-permute-done.8.refs_1_), channel_id=1, source_target_pairs={{0,96},{1,97},{2,98},{3,99},{4,100},{5,101},{6,102},{7,103},{8,104... | collective-permute-start | bytes 1622024 | tf_op jit(solution)/shard_map/ppermute | solution.py:42
  37.3 9.4 %collective-permute-start.7 = (bf16[64,4224]{1,0:T(8,128)(2,1)S(1)}, bf16[64,4224]{1,0:T(8,128)(2,1)S(1)}, u32[]{:S(2)}, u32[]{:S(2)}) collective-permute-start(bf16[64,4224]{1,0:T(8,128)(2,1)S(1)} %collective-permute-done.6.refs_3_), channel_id=1, source_target_pairs={{0,32},{1,33},{2,34},{3,35},{4,36},{5,37},{6,38},{7,39},{8,40},{9,... | collective-permute-start | bytes 1622024 | tf_op jit(solution)/shard_map/ppermute | solution.py:42
  37.3 10.6 %collective-permute-start.5 = (bf16[64,4224]{1,0:T(8,128)(2,1)S(1)}, bf16[64,4224]{1,0:T(8,128)(2,1)S(1)}, u32[]{:S(2)}, u32[]{:S(2)}) collective-permute-start(bf16[64,4224]{1,0:T(8,128)(2,1)S(1)} %collective-permute-done.4.refs_2_), channel_id=1, source_target_pairs={{0,12},{1,13},{2,14},{3,15},{4,8},{5,9},{6,10},{7,11},{8,4},{9,5},... | collective-permute-start | bytes 1622024 | tf_op jit(solution)/shard_map/ppermute | solution.py:42
  48.0 10.2 %collective-permute-start.13 = (bf16[192,4224]{1,0:T(8,128)(2,1)S(1)}, bf16[192,4224]{1,0:T(8,128)(2,1)S(1)}, u32[]{:S(2)}, u32[]{:S(2)}) collective-permute-start(bf16[192,4224]{1,0:T(8,128)(2,1)S(1)} %pad_maximum_fusion.1), channel_id=1, source_target_pairs={{0,16},{1,17},{2,18},{3,19},{4,20},{5,21},{6,22},{7,23},{8,24},{9,... | collective-permute-start | bytes 4866056 | tf_op jit(solution)/shard_map/ppermute | solution.py:54
  48.2 6.5 %collective-permute-start.12 = (bf16[32,4224]{1,0:T(8,128)(2,1)S(1)}, bf16[32,4224]{1,0:T(8,128)(2,1)S(1)}, u32[]{:S(2)}, u32[]{:S(2)}) collective-permute-start(bf16[32,4224]{1,0:T(8,128)(2,1)S(1)} %slice.87), channel_id=1, source_target_pairs={{0,32},{1,33},{2,34},{3,35},{4,36},{5,37},{6,38},{7,39},{8,40},{9,... | collective-permute-start | bytes 811016 | tf_op jit(solution)/shard_map/ppermute | solution.py:42
  50.3 7.7 %collective-permute-start.11 = (bf16[32,4224]{1,0:T(8,128)(2,1)S(1)}, bf16[32,4224]{1,0:T(8,128)(2,1)S(1)}, u32[]{:S(2)}, u32[]{:S(2)}) collective-permute-start(bf16[32,4224]{1,0:T(8,128)(2,1)S(1)} %slice.86), channel_id=1, source_target_pairs={{0,12},{1,13},{2,14},{3,15},{4,8},{5,9},{6,10},{7,11},{8,4},{9,5},... | collective-permute-start | bytes 811016 | tf_op jit(solution)/shard_map/ppermute | solution.py:42
  58.0 2.9 %collective-permute-start.14 = (bf16[64,4224]{1,0:T(8,128)(2,1)S(1)}, bf16[64,4224]{1,0:T(8,128)(2,1)S(1)}, u32[]{:S(2)}, u32[]{:S(2)}) collective-permute-start(bf16[64,4224]{1,0:T(8,128)(2,1)S(1)} %pad_maximum_fusion.2.refs_4_), channel_id=1, source_target_pairs={{0,16},{1,17},{2,18},{3,19},{4,20},{5,21},{6,22},{7,23},{8,24},{9,... | collective-permute-start | bytes 1622024 | tf_op jit(solution)/shard_map/ppermute | solution.py:54
  63.5 1.4 %collective-permute-start.15 = (f32[3,8,128]{2,1,0:T(8,128)S(1)}, f32[3,8,128]{2,1,0:T(8,128)S(1)}, u32[]{:S(2)}, u32[]{:S(2)}) collective-permute-start(f32[3,8,128]{2,1,0:T(8,128)S(1)} %get-tuple-element.29), channel_id=1, source_target_pairs={{0,16},{1,17},{2,18},{3,19},{4,20},{5,21},{6,22},{7,23},{8,24},{9,... | collective-permute-start | bytes 36872 | tf_op jit(solution)/shard_map/ppermute | solution.py:54
  64.9 4.7 %collective-permute-start.18 = (f32[3,8,128]{2,1,0:T(8,128)S(1)}, f32[3,8,128]{2,1,0:T(8,128)S(1)}, u32[]{:S(2)}, u32[]{:S(2)}) collective-permute-start(f32[3,8,128]{2,1,0:T(8,128)S(1)} %pad_maximum_fusion.3), channel_id=1, source_target_pairs={{0,80},{1,81},{2,82},{3,83},{4,84},{5,85},{6,86},{7,87},{8,88},{9,... | collective-permute-start | bytes 36872 | tf_op jit(solution)/shard_map/ppermute | solution.py:50
  66.5 4.3 %collective-permute-start.17 = (f32[3,8,128]{2,1,0:T(8,128)S(1)}, f32[3,8,128]{2,1,0:T(8,128)S(1)}, u32[]{:S(2)}, u32[]{:S(2)}) collective-permute-start(f32[3,8,128]{2,1,0:T(8,128)S(1)} %pad_maximum_fusion.3), channel_id=1, source_target_pairs={{0,112},{1,113},{2,114},{3,115},{4,116},{5,117},{6,118},{7,119},{8... | collective-permute-start | bytes 36872 | tf_op jit(solution)/shard_map/ppermute | solution.py:50
  67.5 3.4 %collective-permute-start.16 = (f32[3,8,128]{2,1,0:T(8,128)S(1)}, f32[3,8,128]{2,1,0:T(8,128)S(1)}, u32[]{:S(2)}, u32[]{:S(2)}) collective-permute-start(f32[3,8,128]{2,1,0:T(8,128)S(1)} %pad_maximum_fusion.3), channel_id=1, source_target_pairs={{0,48},{1,49},{2,50},{3,51},{4,52},{5,53},{6,54},{7,55},{8,56},{9,... | collective-permute-start | bytes 36872 | tf_op jit(solution)/shard_map/ppermute | solution.py:50
  70.9 4.7 %collective-permute-start.21 = (f32[3,8,128]{2,1,0:T(8,128)S(1)}, f32[3,8,128]{2,1,0:T(8,128)S(1)}, u32[]{:S(2)}, u32[]{:S(2)}) collective-permute-start(f32[3,8,128]{2,1,0:T(8,128)S(1)} %pad_maximum_fusion.4), channel_id=1, source_target_pairs={{0,24},{1,25},{2,26},{3,27},{4,28},{5,29},{6,30},{7,31},{8,16},{9,... | collective-permute-start | bytes 36872 | tf_op jit(solution)/shard_map/ppermute | solution.py:50
  71.0 4.6 %collective-permute-start.20 = (f32[3,8,128]{2,1,0:T(8,128)S(1)}, f32[3,8,128]{2,1,0:T(8,128)S(1)}, u32[]{:S(2)}, u32[]{:S(2)}) collective-permute-start(f32[3,8,128]{2,1,0:T(8,128)S(1)} %pad_maximum_fusion.4), channel_id=1, source_target_pairs={{0,28},{1,29},{2,30},{3,31},{4,24},{5,25},{6,26},{7,27},{8,20},{9,... | collective-permute-start | bytes 36872 | tf_op jit(solution)/shard_map/ppermute | solution.py:50
  71.6 3.9 %collective-permute-start.19 = (f32[3,8,128]{2,1,0:T(8,128)S(1)}, f32[3,8,128]{2,1,0:T(8,128)S(1)}, u32[]{:S(2)}, u32[]{:S(2)}) collective-permute-start(f32[3,8,128]{2,1,0:T(8,128)S(1)} %pad_maximum_fusion.4), channel_id=1, source_target_pairs={{0,20},{1,21},{2,22},{3,23},{4,16},{5,17},{6,18},{7,19},{8,28},{9,... | collective-permute-start | bytes 36872 | tf_op jit(solution)/shard_map/ppermute | solution.py:50
  75.6 4.7 %collective-permute-start.24 = (f32[3,8,128]{2,1,0:T(8,128)S(1)}, f32[3,8,128]{2,1,0:T(8,128)S(1)}, u32[]{:S(2)}, u32[]{:S(2)}) collective-permute-start(f32[3,8,128]{2,1,0:T(8,128)S(1)} %pad_maximum_fusion.5.refs_0_), channel_id=1, source_target_pairs={{0,18},{1,19},{2,16},{3,17},{4,22},{5,23},{6,20},{7,21},{8,26},{9,... | collective-permute-start | bytes 36872 | tf_op jit(solution)/shard_map/ppermute | solution.py:50
  76.3 4.3 %collective-permute-start.23 = (f32[3,8,128]{2,1,0:T(8,128)S(1)}, f32[3,8,128]{2,1,0:T(8,128)S(1)}, u32[]{:S(2)}, u32[]{:S(2)}) collective-permute-start(f32[3,8,128]{2,1,0:T(8,128)S(1)} %pad_maximum_fusion.5.refs_0_), channel_id=1, source_target_pairs={{0,19},{1,18},{2,17},{3,16},{4,23},{5,22},{6,21},{7,20},{8,27},{9,... | collective-permute-start | bytes 36872 | tf_op jit(solution)/shard_map/ppermute | solution.py:50
  78.7 3.1 %collective-permute-start.22 = (f32[3,8,128]{2,1,0:T(8,128)S(1)}, f32[3,8,128]{2,1,0:T(8,128)S(1)}, u32[]{:S(2)}, u32[]{:S(2)}) collective-permute-start(f32[3,8,128]{2,1,0:T(8,128)S(1)} %pad_maximum_fusion.5.refs_0_), channel_id=1, source_target_pairs={{0,17},{1,16},{2,19},{3,18},{4,21},{5,20},{6,23},{7,22},{8,25},{9,... | collective-permute-start | bytes 36872 | tf_op jit(solution)/shard_map/ppermute | solution.py:50

commit v5 on v4

--- a/solution.py
+++ b/solution.py
@@ -14,8 +14,8 @@
 F32 = jnp.float32
 LIMIT = 12 << 20
 BLOCK = 64
-EARLY = (((2, 0), (2, 1), (1, 0)), ((0, 0), (0, 1), (1, 1)))
-LATE = (((1, 1), (0, 0), (0, 1)), ((2, 0), (2, 1), (1, 0)))
+EARLY = (((2, 0), (1, 0), (0, 0)), ((2, 1), (1, 1), (0, 1)))
+LATE = (EARLY[1], EARLY[0])
 
 
 def coords(d):
@@ -48,6 +48,14 @@
 
 def cross_exchange(v, dims):
     return lax.ppermute(v, "d", [(d, flipped(d, dims) ^ 16) for d in range(N_DEV)])
+
+
+def early_groups():
+    groups = {}
+    for d in range(N_DEV):
+        p, core = coords(d)
+        groups.setdefault((core, cube_index(p, LATE[core])), []).append((cube_index(p, EARLY[core]), d))
+    return [[d for _, d in sorted(group)] for group in groups.values()]
 
 
 def core_swap(v):
@@ -101,12 +109,11 @@
     labels = jnp.where(lane == 4, scored, 0.0)
     for k, digit in enumerate(digits):
         labels = jnp.where(lane == k, as_column(digit.astype(F32), rows), labels)
-    x_ref[:, :depth] = jnp.dot(
-        selector, hidden_ref[...], preferred_element_type=F32
-    ).astype(jnp.bfloat16)
-    x_ref[:, depth:] = jnp.dot(
-        selector, labels.astype(jnp.bfloat16), preferred_element_type=F32
-    ).astype(jnp.bfloat16)
+    picked = jnp.dot(selector, hidden_ref[...], preferred_element_type=F32).astype(jnp.bfloat16)
+    tags = jnp.dot(selector, labels.astype(jnp.bfloat16), preferred_element_type=F32).astype(jnp.bfloat16)
+    for k in range(x_ref.shape[0]):
+        x_ref[k, :, :depth] = picked
+        x_ref[k, :, depth:] = tags
     aux_ref[...] = jnp.where(lane == 0, as_column(slot, rows), jnp.where(lane == 1, scored, 0.0))
 
 
@@ -115,7 +122,7 @@
     return pl.pallas_call(
         pack_kernel,
         out_shape=(
-            jax.ShapeDtypeStruct((rows // 2, depth + LAB), jnp.bfloat16),
+            jax.ShapeDtypeStruct((8, rows // 2, depth + LAB), jnp.bfloat16),
             jax.ShapeDtypeStruct((rows, LAB), F32),
         ),
         in_specs=[VMEM, VMEM],
@@ -290,20 +297,11 @@
     )(w)
 
 
-def ordered(low, a, b):
-    return jnp.where(low, jnp.concatenate([a, b], 0), jnp.concatenate([b, a], 0))
-
-
 def body(hidden, head_weight, targets, bench_ids, valid, seq_lengths):
-    place_of, core = coords(lax.axis_index("d"))
-    early = jnp.where(core == 0, *(cube_index(place_of, dims) for dims in EARLY))
-    low = [(early >> k) & 1 == 0 for k in range(3)]
     x, aux = pack(hidden, targets, bench_ids, valid, seq_lengths)
-    both, first, second = (exchange(x, [d[s] for d in EARLY]) for s in (slice(0, 2), slice(0, 1), slice(1, 2)))
-    x = ordered(low[1], ordered(low[0], x, first), ordered(low[0], second, both))
-    x = ordered(low[2], x, exchange(x, [d[2:] for d in EARLY]))
-    x, w = tied(x, fetch(head_weight.T))
+    x = lax.all_to_all(x, "d", 0, 0, axis_index_groups=early_groups()).reshape(-1, x.shape[-1])
     near = [late_exchange(x, k) for k in range(3)]
+    *near, w = tied(*near, fetch(head_weight.T))
     near_rows = [x, *near]
     own1 = score(w, near_rows)
     sib1 = score(w, [core_swap(jnp.concatenate(near_rows, 0))])

time: 83.9 us -> 81.2 us (0.968)
  blocking collectives: 0 us -> 13.5 us
  waiting for transfers between devices: 33.4 us -> 20 us
  starting transfers between devices: 27.8 us -> 25.3 us
    all_to_all x0 -> x1, blocking collectives: none -> 13.5 us  [body(): lax.all_to_all(x, 'd', 0, 0, axis_index_groups=early_groups())]
    ppermute x12 -> x8, waiting for transfers between devices: 25 us -> 13.1 us  [exchange(): lax.ppermute(v, 'd', [(d, flipped(d, by_core[coords(d)[1]])) for d in ran...]
    ppermute x12 -> x8, starting transfers between devices: 17.4 us -> 14.5 us  [exchange(): lax.ppermute(v, 'd', [(d, flipped(d, by_core[coords(d)[1]])) for d in ran...]
    ppermute x9, waiting for transfers between devices: 7.45 us -> 6.03 us  [cross_exchange(): lax.ppermute(v, 'd', [(d, flipped(d, dims) ^ 16) for d in range(N_DEV)])]
  transfers between devices with their start and end apart: 25 -> 21, of which waited for: 18 -> 14; matrix products, arithmetic and copies ran while one was open for 0% -> 0% of each run, Pallas kernels for 14% -> 14%
where the time goes in v5:
time: 81.2 us; the launch traced here: 80 us
  starting transfers between devices  25.3 us (31%)
  waiting for transfers between devices  20 us (25%)
  Pallas kernels  15 us (18%)
  blocking collectives  13.5 us (17%)
  local copies, waits for them, and re-layouts  4.29 us (5%)
  other arithmetic  1.13 us (1%)
    ppermute x8, starting transfers between devices, exchange(): lax.ppermute(v, 'd', [(d, flipped(d, by_core[coords(d)[1]])) for d in ran...  14.5 us
    all_to_all x1, blocking collectives, body(): lax.all_to_all(x, 'd', 0, 0, axis_index_groups=early_groups())  13.5 us
    ppermute x8, waiting for transfers between devices, exchange(): lax.ppermute(v, 'd', [(d, flipped(d, by_core[coords(d)[1]])) for d in ran...  13.1 us
    pallas_call x4, Pallas kernels, score(): pl.pallas_call(score_kernel, out_shape=jax.ShapeDtypeStruct((8, rows), F3...  10.5 us
    ppermute x9, starting transfers between devices, cross_exchange(): lax.ppermute(v, 'd', [(d, flipped(d, dims) ^ 16) for d in range(N_DEV)])  9.8 us
    ppermute x9, waiting for transfers between devices, cross_exchange(): lax.ppermute(v, 'd', [(d, flipped(d, dims) ^ 16) for d in range(N_DEV)])  6.03 us
    unnamed x4, local copies, waits for them, and re-layouts  4.25 us
    pallas_call x1, Pallas kernels, score_place(): pl.pallas_call(score_place_kernel, out_shape=(jax.ShapeDtypeStruct((3, 8,...  2.55 us
  transfers between devices with their start and end apart: 21, of which 14 were waited for; matrix products, arithmetic and copies ran while one was open for 0% of the time, Pallas kernels for 14%

profile of v5, /device:TPU:0, one launch (start us, length us, event | category | flops | bytes accessed | tf_op | source)
XLA Modules:
  0.0 80.0 jit_solution(2242551929125724463)
XLA Ops:
  0.6 0.8 add_bitcast_fusion.ints_ref
  1.4 0.9 %copy-done.1 = bf16[16,4096]{1,0:T(8,128)(2,1)S(1)} copy-done((bf16[16,4096]{1,0:T(8,128)(2,1)S(1)}, bf16[16,4096]{1,0:T(8,128)(2,1)}, u32[]{:S(2)}) %copy-start.1) | copy-done | bytes 131096
  2.8 13.5 %all_to_all.5 = bf16[8,8,4224]{2,1,0:T(8,128)(2,1)S(1)} all-to-all(bf16[8,8,4224]{2,1,0:T(8,128)(2,1)S(1)} %get-tuple-element.21), channel_id=1, replica_groups={{0,1,4,5,32,33,36,37},{3,2,7,6,35,34,39,38},{12,13,8,9,44,45,40,41},{15..., dimensions={0} | all-to-all | bytes 1081344 | tf_op jit(solution)/shard_map/all_to_all | solution.py:302
  16.3 2.7 %collective-permute-start.2 = (bf16[64,4224]{1,0:T(8,128)(2,1)S(1)}, bf16[64,4224]{1,0:T(8,128)(2,1)S(1)}, u32[]{:S(2)}, u32[]{:S(2)}) collective-permute-start(bf16[64,4224]{1,0:T(8,128)(2,1)S(1)} %bitcast.8), channel_id=1, source_target_pairs={{0,96},{1,97},{2,98},{3,99},{4,100},{5,101},{6,102},{7,103},{8,104... | collective-permute-start | bytes 1622024 | tf_op jit(solution)/shard_map/ppermute | solution.py:42
  19.0 2.2 %collective-permute-start.1 = (bf16[64,4224]{1,0:T(8,128)(2,1)S(1)}, bf16[64,4224]{1,0:T(8,128)(2,1)S(1)}, u32[]{:S(2)}, u32[]{:S(2)}) collective-permute-start(bf16[64,4224]{1,0:T(8,128)(2,1)S(1)} %bitcast.9), channel_id=1, source_target_pairs={{0,12},{1,13},{2,14},{3,15},{4,8},{5,9},{6,10},{7,11},{8,4},{9,5},... | collective-permute-start | bytes 1622024 | tf_op jit(solution)/shard_map/ppermute | solution.py:42
  21.2 2.4 %collective-permute-start = (bf16[64,4224]{1,0:T(8,128)(2,1)S(1)}, bf16[64,4224]{1,0:T(8,128)(2,1)S(1)}, u32[]{:S(2)}, u32[]{:S(2)}) collective-permute-start(bf16[64,4224]{1,0:T(8,128)(2,1)S(1)} %bitcast.10), channel_id=1, source_target_pairs={{0,3},{1,2},{2,1},{3,0},{4,7},{5,6},{6,5},{7,4},{8,11},{9,10},{10,... | collective-permute-start | bytes 1622024 | tf_op jit(solution)/shard_map/ppermute | solution.py:42
  23.6 3.3 %copy-done = bf16[4096,1002]{0,1:T(8,128)(2,1)S(1)} copy-done((bf16[4096,1002]{0,1:T(8,128)(2,1)S(1)}, bf16[4096,1002]{0,1:T(8,128)(2,1)}, u32[]{:S(2)}) %copy-start) | copy-done | bytes 8208408
  27.7 1.9 %collective-permute-done.1.refs_2_ = bf16[64,4224]{1,0:T(8,128)(2,1)S(1)} collective-permute-done((bf16[64,4224]{1,0:T(8,128)(2,1)S(1)}, bf16[64,4224]{1,0:T(8,128)(2,1)S(1)}, u32[]{:S(2)}, u32[]{:S(2)}) %collective-permute-start.1) | collective-permute-done | bytes 540704 | tf_op jit(solution)/shard_map/ppermute | solution.py:42
  29.5 2.2 %collective-permute-done.refs_1_ = bf16[64,4224]{1,0:T(8,128)(2,1)S(1)} collective-permute-done((bf16[64,4224]{1,0:T(8,128)(2,1)S(1)}, bf16[64,4224]{1,0:T(8,128)(2,1)S(1)}, u32[]{:S(2)}, u32[]{:S(2)}) %collective-permute-start) | collective-permute-done | bytes 540704 | tf_op jit(solution)/shard_map/ppermute | solution.py:42
  32.0 2.5 %collective-permute-start.3 = (bf16[64,4224]{1,0:T(8,128)(2,1)S(1)}, bf16[64,4224]{1,0:T(8,128)(2,1)S(1)}, u32[]{:S(2)}, u32[]{:S(2)}) collective-permute-start(bf16[64,4224]{1,0:T(8,128)(2,1)S(1)} %collective-permute-done.1.refs_2_), channel_id=1, source_target_pairs={{0,3},{1,2},{2,1},{3,0},{4,7},{5,6},{6,5},{7,4},{8,11},{9,10},{10,... | collective-permute-start | bytes 1622024 | tf_op jit(solution)/shard_map/ppermute | solution.py:42
  35.8 2.6 %score.4.refs_0_ = f32[8,256]{1,0:T(8,128)S(1)} custom-call(bf16[1002,4096]{1,0:T(8,128)(2,1)S(1)} %fetch.1.w_ref, bf16[64,4224]{1,0:T(8,128)(2,1)S(1)} %bitcast.12, bf16[64,4224]{1,0:T(8,128)(2,1)S(1)} %collective-permute-done.refs_1_, bf16[64,4224]{1,0:T(8,128)(2,1)S(1)} %collective-permute-done.1.refs_2_, bf16[64,4224]{1,0:T(8,128)(2,1)S(1)} %collective-permute-done.2.refs_3_), custom_call_target="tpu_custom_call" | custom-call | flops 2101346304 | bytes 8208384 | tf_op jit(solution)/shard_map/score/pallas_call | solution.py:169
  38.3 2.6 %score.5.refs_1_ = f32[8,256]{1,0:T(8,128)S(1)} custom-call(bf16[1002,4096]{1,0:T(8,128)(2,1)S(1)} %fetch.1.w_ref, bf16[256,4224]{1,0:T(8,128)(2,1)S(1)} %collective-permute-done.6.refs_0_), custom_call_target="tpu_custom_call" | custom-call | flops 2101346304 | bytes 8208384 | tf_op jit(solution)/shard_map/score/pallas_call | solution.py:169
  40.9 1.7 %collective-permute-done.3.refs_0_ = bf16[64,4224]{1,0:T(8,128)(2,1)S(1)} collective-permute-done((bf16[64,4224]{1,0:T(8,128)(2,1)S(1)}, bf16[64,4224]{1,0:T(8,128)(2,1)S(1)}, u32[]{:S(2)}, u32[]{:S(2)}) %collective-permute-start.3) | collective-permute-done | bytes 540704 | tf_op jit(solution)/shard_map/ppermute | solution.py:42
  42.6 2.4 %collective-permute-done.4.refs_1_ = bf16[64,4224]{1,0:T(8,128)(2,1)S(1)} collective-permute-done((bf16[64,4224]{1,0:T(8,128)(2,1)S(1)}, bf16[64,4224]{1,0:T(8,128)(2,1)S(1)}, u32[]{:S(2)}, u32[]{:S(2)}) %collective-permute-start.4) | collective-permute-done | bytes 540704 | tf_op jit(solution)/shard_map/ppermute | solution.py:42
  46.0 2.6 %collective-permute-start.8 = (bf16[32,4224]{1,0:T(8,128)(2,1)S(1)}, bf16[32,4224]{1,0:T(8,128)(2,1)S(1)}, u32[]{:S(2)}, u32[]{:S(2)}) collective-permute-start(bf16[32,4224]{1,0:T(8,128)(2,1)S(1)} %slice.87), channel_id=1, source_target_pairs={{0,12},{1,13},{2,14},{3,15},{4,8},{5,9},{6,10},{7,11},{8,4},{9,5},... | collective-permute-start | bytes 811016 | tf_op jit(solution)/shard_map/ppermute | solution.py:42
  48.6 0.8 %collective-permute-start.7 = (bf16[32,4224]{1,0:T(8,128)(2,1)S(1)}, bf16[32,4224]{1,0:T(8,128)(2,1)S(1)}, u32[]{:S(2)}, u32[]{:S(2)}) collective-permute-start(bf16[32,4224]{1,0:T(8,128)(2,1)S(1)} %slice.86), channel_id=1, source_target_pairs={{0,3},{1,2},{2,1},{3,0},{4,7},{5,6},{6,5},{7,4},{8,11},{9,10},{10,... | collective-permute-start | bytes 811016 | tf_op jit(solution)/shard_map/ppermute | solution.py:42
  49.4 2.7 %score.6.refs_2_ = f32[8,192]{1,0:T(8,128)S(1)} custom-call(bf16[1002,4096]{1,0:T(8,128)(2,1)S(1)} %fetch.1.w_ref, bf16[64,4224]{1,0:T(8,128)(2,1)S(1)} %collective-permute-done.3.refs_0_, bf16[64,4224]{1,0:T(8,128)(2,1)S(1)} %collective-permute-done.4.refs_1_, bf16[64,4224]{1,0:T(8,128)(2,1)S(1)} %collective-permute-done.5.refs_2_), custom_call_target="tpu_custom_call" | custom-call | flops 1576009728 | bytes 8208384 | tf_op jit(solution)/shard_map/score/pallas_call | solution.py:169
  52.1 1.7 %collective-permute-done.8 = bf16[32,4224]{1,0:T(8,128)(2,1)S(1)} collective-permute-done((bf16[32,4224]{1,0:T(8,128)(2,1)S(1)}, bf16[32,4224]{1,0:T(8,128)(2,1)S(1)}, u32[]{:S(2)}, u32[]{:S(2)}) %collective-permute-start.8) | collective-permute-done | bytes 270368 | tf_op jit(solution)/shard_map/ppermute | solution.py:42
  53.8 2.5 %collective-permute-done.7 = bf16[32,4224]{1,0:T(8,128)(2,1)S(1)} collective-permute-done((bf16[32,4224]{1,0:T(8,128)(2,1)S(1)}, bf16[32,4224]{1,0:T(8,128)(2,1)S(1)}, u32[]{:S(2)}, u32[]{:S(2)}) %collective-permute-start.7) | collective-permute-done | bytes 270368 | tf_op jit(solution)/shard_map/ppermute | solution.py:42
  56.6 2.7 %score.7.refs_3_ = f32[8,192]{1,0:T(8,128)S(1)} custom-call(bf16[1002,4096]{1,0:T(8,128)(2,1)S(1)} %fetch.1.w_ref, bf16[192,4224]{1,0:T(8,128)(2,1)S(1)} %collective-permute-done.9.refs_0_), custom_call_target="tpu_custom_call" | custom-call | flops 1576009728 | bytes 8208384 | tf_op jit(solution)/shard_map/score/pallas_call | solution.py:169
  59.3 2.6 %score_place.1 = (f32[3,8,128]{2,1,0:T(8,128)S(1)}, f32[2,8,128]{2,1,0:T(8,128)S(1)}) custom-call(bf16[1002,4096]{1,0:T(8,128)(2,1)S(1)} %fetch.1.w_ref, f32[8,256]{1,0:T(8,128)S(1)} %score.4.refs_0_, f32[8,256]{1,0:T(8,128)S(1)} %score.5.refs_1_, f32[8,192]{1,0:T(8,128)S(1)} %score.6.refs_2_, f32[8,192]{1,0:T(8,128)S(1)} %score.7.refs_3_, ...), custom_call_target="tpu_custom_call" | custom-call | flops 1050673152 | bytes 8208384 | tf_op jit(solution)/shard_map/score_place/pallas_call | solution.py:210
  62.4 0.8 %collective-permute-done.11 = f32[3,8,128]{2,1,0:T(8,128)S(1)} collective-permute-done((f32[3,8,128]{2,1,0:T(8,128)S(1)}, f32[3,8,128]{2,1,0:T(8,128)S(1)}, u32[]{:S(2)}, u32[]{:S(2)}) %collective-permute-start.11) | collective-permute-done | bytes 12320 | tf_op jit(solution)/shard_map/ppermute | solution.py:62
  63.4 1.1 %collective-permute-start.13 = (f32[3,8,128]{2,1,0:T(8,128)S(1)}, f32[3,8,128]{2,1,0:T(8,128)S(1)}, u32[]{:S(2)}, u32[]{:S(2)}) collective-permute-start(f32[3,8,128]{2,1,0:T(8,128)S(1)} %pad_maximum_fusion.3), channel_id=1, source_target_pairs={{0,112},{1,113},{2,114},{3,115},{4,116},{5,117},{6,118},{7,119},{8... | collective-permute-start | bytes 36872 | tf_op jit(solution)/shard_map/ppermute | solution.py:50
  64.5 2.0 %collective-permute-start.12 = (f32[3,8,128]{2,1,0:T(8,128)S(1)}, f32[3,8,128]{2,1,0:T(8,128)S(1)}, u32[]{:S(2)}, u32[]{:S(2)}) collective-permute-start(f32[3,8,128]{2,1,0:T(8,128)S(1)} %pad_maximum_fusion.3), channel_id=1, source_target_pairs={{0,48},{1,49},{2,50},{3,51},{4,52},{5,53},{6,54},{7,55},{8,56},{9,... | collective-permute-start | bytes 36872 | tf_op jit(solution)/shard_map/ppermute | solution.py:50
  66.5 1.5 %collective-permute-done.14 = f32[3,8,128]{2,1,0:T(8,128)S(1)} collective-permute-done((f32[3,8,128]{2,1,0:T(8,128)S(1)}, f32[3,8,128]{2,1,0:T(8,128)S(1)}, u32[]{:S(2)}, u32[]{:S(2)}) %collective-permute-start.14) | collective-permute-done | bytes 12320 | tf_op jit(solution)/shard_map/ppermute | solution.py:50
  68.4 1.7 %collective-permute-start.16 = (f32[3,8,128]{2,1,0:T(8,128)S(1)}, f32[3,8,128]{2,1,0:T(8,128)S(1)}, u32[]{:S(2)}, u32[]{:S(2)}) collective-permute-start(f32[3,8,128]{2,1,0:T(8,128)S(1)} %pad_maximum_fusion.4), channel_id=1, source_target_pairs={{0,28},{1,29},{2,30},{3,31},{4,24},{5,25},{6,26},{7,27},{8,20},{9,... | collective-permute-start | bytes 36872 | tf_op jit(solution)/shard_map/ppermute | solution.py:50
  70.1 1.1 %collective-permute-start.15 = (f32[3,8,128]{2,1,0:T(8,128)S(1)}, f32[3,8,128]{2,1,0:T(8,128)S(1)}, u32[]{:S(2)}, u32[]{:S(2)}) collective-permute-start(f32[3,8,128]{2,1,0:T(8,128)S(1)} %pad_maximum_fusion.4), channel_id=1, source_target_pairs={{0,20},{1,21},{2,22},{3,23},{4,16},{5,17},{6,18},{7,19},{8,28},{9,... | collective-permute-start | bytes 36872 | tf_op jit(solution)/shard_map/ppermute | solution.py:50
  71.3 1.6 %collective-permute-done.17 = f32[3,8,128]{2,1,0:T(8,128)S(1)} collective-permute-done((f32[3,8,128]{2,1,0:T(8,128)S(1)}, f32[3,8,128]{2,1,0:T(8,128)S(1)}, u32[]{:S(2)}, u32[]{:S(2)}) %collective-permute-start.17) | collective-permute-done | bytes 12320 | tf_op jit(solution)/shard_map/ppermute | solution.py:50
  73.9 2.2 %collective-permute-start.19 = (f32[3,8,128]{2,1,0:T(8,128)S(1)}, f32[3,8,128]{2,1,0:T(8,128)S(1)}, u32[]{:S(2)}, u32[]{:S(2)}) collective-permute-start(f32[3,8,128]{2,1,0:T(8,128)S(1)} %pad_maximum_fusion.5.refs_0_), channel_id=1, source_target_pairs={{0,19},{1,18},{2,17},{3,16},{4,23},{5,22},{6,21},{7,20},{8,27},{9,... | collective-permute-start | bytes 36872 | tf_op jit(solution)/shard_map/ppermute | solution.py:50
  76.6 1.4 %collective-permute-done.20.refs_3_ = f32[3,8,128]{2,1,0:T(8,128)S(1)} collective-permute-done((f32[3,8,128]{2,1,0:T(8,128)S(1)}, f32[3,8,128]{2,1,0:T(8,128)S(1)}, u32[]{:S(2)}, u32[]{:S(2)}) %collective-permute-start.20) | collective-permute-done | bytes 12320 | tf_op jit(solution)/shard_map/ppermute | solution.py:50
  78.2 1.0 %collective-permute-done.18.refs_1_ = f32[3,8,128]{2,1,0:T(8,128)S(1)} collective-permute-done((f32[3,8,128]{2,1,0:T(8,128)S(1)}, f32[3,8,128]{2,1,0:T(8,128)S(1)}, u32[]{:S(2)}, u32[]{:S(2)}) %collective-permute-start.18) | collective-permute-done | bytes 12320 | tf_op jit(solution)/shard_map/ppermute | solution.py:50
  79.2 0.8 final.1
  (35 shorter events, 6.9 us)
Async XLA Ops:
  1.4 0.9 %copy-start.1 = (bf16[16,4096]{1,0:T(8,128)(2,1)S(1)}, bf16[16,4096]{1,0:T(8,128)(2,1)}, u32[]{:S(2)}) copy-start(bf16[16,4096]{1,0:T(8,128)(2,1)} %hidden_ref.1) | copy-start | bytes 393220
  16.3 11.4 %collective-permute-start.2 = (bf16[64,4224]{1,0:T(8,128)(2,1)S(1)}, bf16[64,4224]{1,0:T(8,128)(2,1)S(1)}, u32[]{:S(2)}, u32[]{:S(2)}) collective-permute-start(bf16[64,4224]{1,0:T(8,128)(2,1)S(1)} %bitcast.8), channel_id=1, source_target_pairs={{0,96},{1,97},{2,98},{3,99},{4,100},{5,101},{6,102},{7,103},{8,104... | collective-permute-start | bytes 1622024 | tf_op jit(solution)/shard_map/ppermute | solution.py:42
  19.0 10.6 %collective-permute-start.1 = (bf16[64,4224]{1,0:T(8,128)(2,1)S(1)}, bf16[64,4224]{1,0:T(8,128)(2,1)S(1)}, u32[]{:S(2)}, u32[]{:S(2)}) collective-permute-start(bf16[64,4224]{1,0:T(8,128)(2,1)S(1)} %bitcast.9), channel_id=1, source_target_pairs={{0,12},{1,13},{2,14},{3,15},{4,8},{5,9},{6,10},{7,11},{8,4},{9,5},... | collective-permute-start | bytes 1622024 | tf_op jit(solution)/shard_map/ppermute | solution.py:42
  21.2 10.6 %collective-permute-start = (bf16[64,4224]{1,0:T(8,128)(2,1)S(1)}, bf16[64,4224]{1,0:T(8,128)(2,1)S(1)}, u32[]{:S(2)}, u32[]{:S(2)}) collective-permute-start(bf16[64,4224]{1,0:T(8,128)(2,1)S(1)} %bitcast.10), channel_id=1, source_target_pairs={{0,3},{1,2},{2,1},{3,0},{4,7},{5,6},{6,5},{7,4},{8,11},{9,10},{10,... | collective-permute-start | bytes 1622024 | tf_op jit(solution)/shard_map/ppermute | solution.py:42
  23.6 3.3 %copy-start = (bf16[4096,1002]{0,1:T(8,128)(2,1)S(1)}, bf16[4096,1002]{0,1:T(8,128)(2,1)}, u32[]{:S(2)}) copy-start(bf16[4096,1002]{0,1:T(8,128)(2,1)} %param.7) | copy-start | bytes 24625156
  31.9 6.5 %collective-permute-start.6 = (bf16[256,4224]{1,0:T(8,128)(2,1)S(1)}, bf16[256,4224]{1,0:T(8,128)(2,1)S(1)}, u32[]{:S(2)}, u32[]{:S(2)}) collective-permute-start(bf16[256,4224]{1,0:T(8,128)(2,1)S(1)} %pad_maximum_fusion), channel_id=1, source_target_pairs={{0,16},{1,17},{2,18},{3,19},{4,20},{5,21},{6,22},{7,23},{8,24},{9,... | collective-permute-start | bytes 6488072 | tf_op jit(solution)/shard_map/ppermute | solution.py:62
  32.0 10.6 %collective-permute-start.3 = (bf16[64,4224]{1,0:T(8,128)(2,1)S(1)}, bf16[64,4224]{1,0:T(8,128)(2,1)S(1)}, u32[]{:S(2)}, u32[]{:S(2)}) collective-permute-start(bf16[64,4224]{1,0:T(8,128)(2,1)S(1)} %collective-permute-done.1.refs_2_), channel_id=1, source_target_pairs={{0,3},{1,2},{2,1},{3,0},{4,7},{5,6},{6,5},{7,4},{8,11},{9,10},{10,... | collective-permute-start | bytes 1622024 | tf_op jit(solution)/shard_map/ppermute | solution.py:42
  34.5 10.6 %collective-permute-start.4 = (bf16[64,4224]{1,0:T(8,128)(2,1)S(1)}, bf16[64,4224]{1,0:T(8,128)(2,1)S(1)}, u32[]{:S(2)}, u32[]{:S(2)}) collective-permute-start(bf16[64,4224]{1,0:T(8,128)(2,1)S(1)} %collective-permute-done.2.refs_3_), channel_id=1, source_target_pairs={{0,12},{1,13},{2,14},{3,15},{4,8},{5,9},{6,10},{7,11},{8,4},{9,5},... | collective-permute-start | bytes 1622024 | tf_op jit(solution)/shard_map/ppermute | solution.py:42
  35.2 10.6 %collective-permute-start.5 = (bf16[64,4224]{1,0:T(8,128)(2,1)S(1)}, bf16[64,4224]{1,0:T(8,128)(2,1)S(1)}, u32[]{:S(2)}, u32[]{:S(2)}) collective-permute-start(bf16[64,4224]{1,0:T(8,128)(2,1)S(1)} %collective-permute-done.refs_1_), channel_id=1, source_target_pairs={{0,96},{1,97},{2,98},{3,99},{4,100},{5,101},{6,102},{7,103},{8,104... | collective-permute-start | bytes 1622024 | tf_op jit(solution)/shard_map/ppermute | solution.py:42
  45.9 10.7 %collective-permute-start.9 = (bf16[192,4224]{1,0:T(8,128)(2,1)S(1)}, bf16[192,4224]{1,0:T(8,128)(2,1)S(1)}, u32[]{:S(2)}, u32[]{:S(2)}) collective-permute-start(bf16[192,4224]{1,0:T(8,128)(2,1)S(1)} %pad_maximum_fusion.1), channel_id=1, source_target_pairs={{0,16},{1,17},{2,18},{3,19},{4,20},{5,21},{6,22},{7,23},{8,24},{9,... | collective-permute-start | bytes 4866056 | tf_op jit(solution)/shard_map/ppermute | solution.py:62
  46.0 7.8 %collective-permute-start.8 = (bf16[32,4224]{1,0:T(8,128)(2,1)S(1)}, bf16[32,4224]{1,0:T(8,128)(2,1)S(1)}, u32[]{:S(2)}, u32[]{:S(2)}) collective-permute-start(bf16[32,4224]{1,0:T(8,128)(2,1)S(1)} %slice.87), channel_id=1, source_target_pairs={{0,12},{1,13},{2,14},{3,15},{4,8},{5,9},{6,10},{7,11},{8,4},{9,5},... | collective-permute-start | bytes 811016 | tf_op jit(solution)/shard_map/ppermute | solution.py:42
  48.6 7.7 %collective-permute-start.7 = (bf16[32,4224]{1,0:T(8,128)(2,1)S(1)}, bf16[32,4224]{1,0:T(8,128)(2,1)S(1)}, u32[]{:S(2)}, u32[]{:S(2)}) collective-permute-start(bf16[32,4224]{1,0:T(8,128)(2,1)S(1)} %slice.86), channel_id=1, source_target_pairs={{0,3},{1,2},{2,1},{3,0},{4,7},{5,6},{6,5},{7,4},{8,11},{9,10},{10,... | collective-permute-start | bytes 811016 | tf_op jit(solution)/shard_map/ppermute | solution.py:42
  56.3 2.9 %collective-permute-start.10 = (bf16[64,4224]{1,0:T(8,128)(2,1)S(1)}, bf16[64,4224]{1,0:T(8,128)(2,1)S(1)}, u32[]{:S(2)}, u32[]{:S(2)}) collective-permute-start(bf16[64,4224]{1,0:T(8,128)(2,1)S(1)} %pad_maximum_fusion.2.refs_4_), channel_id=1, source_target_pairs={{0,16},{1,17},{2,18},{3,19},{4,20},{5,21},{6,22},{7,23},{8,24},{9,... | collective-permute-start | bytes 1622024 | tf_op jit(solution)/shard_map/ppermute | solution.py:62
  61.9 1.4 %collective-permute-start.11 = (f32[3,8,128]{2,1,0:T(8,128)S(1)}, f32[3,8,128]{2,1,0:T(8,128)S(1)}, u32[]{:S(2)}, u32[]{:S(2)}) collective-permute-start(f32[3,8,128]{2,1,0:T(8,128)S(1)} %get-tuple-element.33), channel_id=1, source_target_pairs={{0,16},{1,17},{2,18},{3,19},{4,20},{5,21},{6,22},{7,23},{8,24},{9,... | collective-permute-start | bytes 36872 | tf_op jit(solution)/shard_map/ppermute | solution.py:62
  63.3 4.7 %collective-permute-start.14 = (f32[3,8,128]{2,1,0:T(8,128)S(1)}, f32[3,8,128]{2,1,0:T(8,128)S(1)}, u32[]{:S(2)}, u32[]{:S(2)}) collective-permute-start(f32[3,8,128]{2,1,0:T(8,128)S(1)} %pad_maximum_fusion.3), channel_id=1, source_target_pairs={{0,80},{1,81},{2,82},{3,83},{4,84},{5,85},{6,86},{7,87},{8,88},{9,... | collective-permute-start | bytes 36872 | tf_op jit(solution)/shard_map/ppermute | solution.py:50
  63.4 4.6 %collective-permute-start.13 = (f32[3,8,128]{2,1,0:T(8,128)S(1)}, f32[3,8,128]{2,1,0:T(8,128)S(1)}, u32[]{:S(2)}, u32[]{:S(2)}) collective-permute-start(f32[3,8,128]{2,1,0:T(8,128)S(1)} %pad_maximum_fusion.3), channel_id=1, source_target_pairs={{0,112},{1,113},{2,114},{3,115},{4,116},{5,117},{6,118},{7,119},{8... | collective-permute-start | bytes 36872 | tf_op jit(solution)/shard_map/ppermute | solution.py:50
  64.5 3.5 %collective-permute-start.12 = (f32[3,8,128]{2,1,0:T(8,128)S(1)}, f32[3,8,128]{2,1,0:T(8,128)S(1)}, u32[]{:S(2)}, u32[]{:S(2)}) collective-permute-start(f32[3,8,128]{2,1,0:T(8,128)S(1)} %pad_maximum_fusion.3), channel_id=1, source_target_pairs={{0,48},{1,49},{2,50},{3,51},{4,52},{5,53},{6,54},{7,55},{8,56},{9,... | collective-permute-start | bytes 36872 | tf_op jit(solution)/shard_map/ppermute | solution.py:50
  68.0 4.8 %collective-permute-start.17 = (f32[3,8,128]{2,1,0:T(8,128)S(1)}, f32[3,8,128]{2,1,0:T(8,128)S(1)}, u32[]{:S(2)}, u32[]{:S(2)}) collective-permute-start(f32[3,8,128]{2,1,0:T(8,128)S(1)} %pad_maximum_fusion.4), channel_id=1, source_target_pairs={{0,24},{1,25},{2,26},{3,27},{4,28},{5,29},{6,30},{7,31},{8,16},{9,... | collective-permute-start | bytes 36872 | tf_op jit(solution)/shard_map/ppermute | solution.py:50
  68.4 4.5 %collective-permute-start.16 = (f32[3,8,128]{2,1,0:T(8,128)S(1)}, f32[3,8,128]{2,1,0:T(8,128)S(1)}, u32[]{:S(2)}, u32[]{:S(2)}) collective-permute-start(f32[3,8,128]{2,1,0:T(8,128)S(1)} %pad_maximum_fusion.4), channel_id=1, source_target_pairs={{0,28},{1,29},{2,30},{3,31},{4,24},{5,25},{6,26},{7,27},{8,20},{9,... | collective-permute-start | bytes 36872 | tf_op jit(solution)/shard_map/ppermute | solution.py:50
  70.1 3.1 %collective-permute-start.15 = (f32[3,8,128]{2,1,0:T(8,128)S(1)}, f32[3,8,128]{2,1,0:T(8,128)S(1)}, u32[]{:S(2)}, u32[]{:S(2)}) collective-permute-start(f32[3,8,128]{2,1,0:T(8,128)S(1)} %pad_maximum_fusion.4), channel_id=1, source_target_pairs={{0,20},{1,21},{2,22},{3,23},{4,16},{5,17},{6,18},{7,19},{8,28},{9,... | collective-permute-start | bytes 36872 | tf_op jit(solution)/shard_map/ppermute | solution.py:50
  73.3 4.7 %collective-permute-start.20 = (f32[3,8,128]{2,1,0:T(8,128)S(1)}, f32[3,8,128]{2,1,0:T(8,128)S(1)}, u32[]{:S(2)}, u32[]{:S(2)}) collective-permute-start(f32[3,8,128]{2,1,0:T(8,128)S(1)} %pad_maximum_fusion.5.refs_0_), channel_id=1, source_target_pairs={{0,18},{1,19},{2,16},{3,17},{4,22},{5,23},{6,20},{7,21},{8,26},{9,... | collective-permute-start | bytes 36872 | tf_op jit(solution)/shard_map/ppermute | solution.py:50
  73.9 4.3 %collective-permute-start.19 = (f32[3,8,128]{2,1,0:T(8,128)S(1)}, f32[3,8,128]{2,1,0:T(8,128)S(1)}, u32[]{:S(2)}, u32[]{:S(2)}) collective-permute-start(f32[3,8,128]{2,1,0:T(8,128)S(1)} %pad_maximum_fusion.5.refs_0_), channel_id=1, source_target_pairs={{0,19},{1,18},{2,17},{3,16},{4,23},{5,22},{6,21},{7,20},{8,27},{9,... | collective-permute-start | bytes 36872 | tf_op jit(solution)/shard_map/ppermute | solution.py:50
  76.1 3.1 %collective-permute-start.18 = (f32[3,8,128]{2,1,0:T(8,128)S(1)}, f32[3,8,128]{2,1,0:T(8,128)S(1)}, u32[]{:S(2)}, u32[]{:S(2)}) collective-permute-start(f32[3,8,128]{2,1,0:T(8,128)S(1)} %pad_maximum_fusion.5.refs_0_), channel_id=1, source_target_pairs={{0,17},{1,16},{2,19},{3,18},{4,21},{5,20},{6,23},{7,22},{8,25},{9,... | collective-permute-start | bytes 36872 | tf_op jit(solution)/shard_map/ppermute | solution.py:50

commit v6 on v5

--- a/solution.py
+++ b/solution.py
@@ -301,7 +301,7 @@
     x, aux = pack(hidden, targets, bench_ids, valid, seq_lengths)
     x = lax.all_to_all(x, "d", 0, 0, axis_index_groups=early_groups()).reshape(-1, x.shape[-1])
     near = [late_exchange(x, k) for k in range(3)]
-    *near, w = tied(*near, fetch(head_weight.T))
+    near[0], w = tied(near[0], fetch(head_weight.T))
     near_rows = [x, *near]
     own1 = score(w, near_rows)
     sib1 = score(w, [core_swap(jnp.concatenate(near_rows, 0))])

time: 81.2 us -> 80.3 us (0.989)
  waiting for transfers between devices: 20 us -> 19.1 us
    ppermute x8, waiting for transfers between devices: 13.1 us -> 11.7 us  [exchange(): lax.ppermute(v, 'd', [(d, flipped(d, by_core[coords(d)[1]])) for d in ran...]
  transfers between devices with their start and end apart: 21 -> 21, of which waited for: 14 -> 13; matrix products, arithmetic and copies ran while one was open for 0% -> 0% of each run, Pallas kernels for 14% -> 14%
where the time goes in v6:
time: 80.3 us; the launch traced here: 79 us
  starting transfers between devices  25.2 us (31%)
  waiting for transfers between devices  19.1 us (24%)
  Pallas kernels  15 us (19%)
  blocking collectives  13.5 us (17%)
  local copies, waits for them, and re-layouts  4.29 us (5%)
  other arithmetic  1.13 us (1%)
    ppermute x8, starting transfers between devices, exchange(): lax.ppermute(v, 'd', [(d, flipped(d, by_core[coords(d)[1]])) for d in ran...  14.5 us
    all_to_all x1, blocking collectives, body(): lax.all_to_all(x, 'd', 0, 0, axis_index_groups=early_groups())  13.5 us
    ppermute x8, waiting for transfers between devices, exchange(): lax.ppermute(v, 'd', [(d, flipped(d, by_core[coords(d)[1]])) for d in ran...  11.7 us
    pallas_call x4, Pallas kernels, score(): pl.pallas_call(score_kernel, out_shape=jax.ShapeDtypeStruct((8, rows), F3...  10.5 us
    ppermute x9, starting transfers between devices, cross_exchange(): lax.ppermute(v, 'd', [(d, flipped(d, dims) ^ 16) for d in range(N_DEV)])  9.71 us
    ppermute x9, waiting for transfers between devices, cross_exchange(): lax.ppermute(v, 'd', [(d, flipped(d, dims) ^ 16) for d in range(N_DEV)])  6.58 us
    unnamed x4, local copies, waits for them, and re-layouts  4.25 us
    pallas_call x1, Pallas kernels, score_place(): pl.pallas_call(score_place_kernel, out_shape=(jax.ShapeDtypeStruct((3, 8,...  2.55 us
  transfers between devices with their start and end apart: 21, of which 13 were waited for; matrix products, arithmetic and copies ran while one was open for 0% of the time, Pallas kernels for 14%

profile of v6, /device:TPU:0, one launch (start us, length us, event | category | flops | bytes accessed | tf_op | source)
XLA Modules:
  0.0 79.0 jit_solution(10259150308069833537)
XLA Ops:
  1.4 0.9 %copy-done.1 = bf16[16,4096]{1,0:T(8,128)(2,1)S(1)} copy-done((bf16[16,4096]{1,0:T(8,128)(2,1)S(1)}, bf16[16,4096]{1,0:T(8,128)(2,1)}, u32[]{:S(2)}) %copy-start.1) | copy-done | bytes 131096
  2.8 13.5 %all_to_all.5 = bf16[8,8,4224]{2,1,0:T(8,128)(2,1)S(1)} all-to-all(bf16[8,8,4224]{2,1,0:T(8,128)(2,1)S(1)} %get-tuple-element.19), channel_id=1, replica_groups={{0,1,4,5,32,33,36,37},{3,2,7,6,35,34,39,38},{12,13,8,9,44,45,40,41},{15..., dimensions={0} | all-to-all | bytes 1081344 | tf_op jit(solution)/shard_map/all_to_all | solution.py:302
  16.3 2.1 %collective-permute-start = (bf16[64,4224]{1,0:T(8,128)(2,1)S(1)}, bf16[64,4224]{1,0:T(8,128)(2,1)S(1)}, u32[]{:S(2)}, u32[]{:S(2)}) collective-permute-start(bf16[64,4224]{1,0:T(8,128)(2,1)S(1)} %bitcast.8), channel_id=1, source_target_pairs={{0,3},{1,2},{2,1},{3,0},{4,7},{5,6},{6,5},{7,4},{8,11},{9,10},{10,... | collective-permute-start | bytes 1622024 | tf_op jit(solution)/shard_map/ppermute | solution.py:42
  18.4 2.7 %collective-permute-start.3 = (bf16[64,4224]{1,0:T(8,128)(2,1)S(1)}, bf16[64,4224]{1,0:T(8,128)(2,1)S(1)}, u32[]{:S(2)}, u32[]{:S(2)}) collective-permute-start(bf16[64,4224]{1,0:T(8,128)(2,1)S(1)} %bitcast.9), channel_id=1, source_target_pairs={{0,96},{1,97},{2,98},{3,99},{4,100},{5,101},{6,102},{7,103},{8,104... | collective-permute-start | bytes 1622024 | tf_op jit(solution)/shard_map/ppermute | solution.py:42
  21.1 2.5 %collective-permute-start.1 = (bf16[64,4224]{1,0:T(8,128)(2,1)S(1)}, bf16[64,4224]{1,0:T(8,128)(2,1)S(1)}, u32[]{:S(2)}, u32[]{:S(2)}) collective-permute-start(bf16[64,4224]{1,0:T(8,128)(2,1)S(1)} %bitcast.10), channel_id=1, source_target_pairs={{0,12},{1,13},{2,14},{3,15},{4,8},{5,9},{6,10},{7,11},{8,4},{9,5},... | collective-permute-start | bytes 1622024 | tf_op jit(solution)/shard_map/ppermute | solution.py:42
  23.6 3.3 %copy-done = bf16[4096,1002]{0,1:T(8,128)(2,1)S(1)} copy-done((bf16[4096,1002]{0,1:T(8,128)(2,1)S(1)}, bf16[4096,1002]{0,1:T(8,128)(2,1)}, u32[]{:S(2)}) %copy-start) | copy-done | bytes 8208408
  27.7 1.4 %collective-permute-done.3.refs_3_ = bf16[64,4224]{1,0:T(8,128)(2,1)S(1)} collective-permute-done((bf16[64,4224]{1,0:T(8,128)(2,1)S(1)}, bf16[64,4224]{1,0:T(8,128)(2,1)S(1)}, u32[]{:S(2)}, u32[]{:S(2)}) %collective-permute-start.3) | collective-permute-done | bytes 540704 | tf_op jit(solution)/shard_map/ppermute | solution.py:42
  29.1 2.6 %collective-permute-done.1.refs_2_ = bf16[64,4224]{1,0:T(8,128)(2,1)S(1)} collective-permute-done((bf16[64,4224]{1,0:T(8,128)(2,1)S(1)}, bf16[64,4224]{1,0:T(8,128)(2,1)S(1)}, u32[]{:S(2)}, u32[]{:S(2)}) %collective-permute-start.1) | collective-permute-done | bytes 540704 | tf_op jit(solution)/shard_map/ppermute | solution.py:42
  31.9 2.6 %collective-permute-start.4 = (bf16[64,4224]{1,0:T(8,128)(2,1)S(1)}, bf16[64,4224]{1,0:T(8,128)(2,1)S(1)}, u32[]{:S(2)}, u32[]{:S(2)}) collective-permute-start(bf16[64,4224]{1,0:T(8,128)(2,1)S(1)} %collective-permute-done.3.refs_3_), channel_id=1, source_target_pairs={{0,12},{1,13},{2,14},{3,15},{4,8},{5,9},{6,10},{7,11},{8,4},{9,5},... | collective-permute-start | bytes 1622024 | tf_op jit(solution)/shard_map/ppermute | solution.py:42
  34.5 0.8 %collective-permute-start.2 = (bf16[64,4224]{1,0:T(8,128)(2,1)S(1)}, bf16[64,4224]{1,0:T(8,128)(2,1)S(1)}, u32[]{:S(2)}, u32[]{:S(2)}) collective-permute-start(bf16[64,4224]{1,0:T(8,128)(2,1)S(1)} %collective-permute-done.1.refs_2_), channel_id=1, source_target_pairs={{0,3},{1,2},{2,1},{3,0},{4,7},{5,6},{6,5},{7,4},{8,11},{9,10},{10,... | collective-permute-start | bytes 1622024 | tf_op jit(solution)/shard_map/ppermute | solution.py:42
  35.8 2.6 %score.4.refs_0_ = f32[8,256]{1,0:T(8,128)S(1)} custom-call(bf16[1002,4096]{1,0:T(8,128)(2,1)S(1)} %fetch.1.w_ref, bf16[64,4224]{1,0:T(8,128)(2,1)S(1)} %bitcast.12, bf16[64,4224]{1,0:T(8,128)(2,1)S(1)} %collective-permute-done.refs_1_, bf16[64,4224]{1,0:T(8,128)(2,1)S(1)} %collective-permute-done.1.refs_2_, bf16[64,4224]{1,0:T(8,128)(2,1)S(1)} %collective-permute-done.3.refs_3_), custom_call_target="tpu_custom_call" | custom-call | flops 2101346304 | bytes 8208384 | tf_op jit(solution)/shard_map/score/pallas_call | solution.py:169
  38.4 2.6 %score.5.refs_1_ = f32[8,256]{1,0:T(8,128)S(1)} custom-call(bf16[1002,4096]{1,0:T(8,128)(2,1)S(1)} %fetch.1.w_ref, bf16[256,4224]{1,0:T(8,128)(2,1)S(1)} %collective-permute-done.6.refs_0_), custom_call_target="tpu_custom_call" | custom-call | flops 2101346304 | bytes 8208384 | tf_op jit(solution)/shard_map/score/pallas_call | solution.py:169
  41.0 1.5 %collective-permute-done.4.refs_1_ = bf16[64,4224]{1,0:T(8,128)(2,1)S(1)} collective-permute-done((bf16[64,4224]{1,0:T(8,128)(2,1)S(1)}, bf16[64,4224]{1,0:T(8,128)(2,1)S(1)}, u32[]{:S(2)}, u32[]{:S(2)}) %collective-permute-start.4) | collective-permute-done | bytes 540704 | tf_op jit(solution)/shard_map/ppermute | solution.py:42
  42.5 2.5 %collective-permute-done.2.refs_0_ = bf16[64,4224]{1,0:T(8,128)(2,1)S(1)} collective-permute-done((bf16[64,4224]{1,0:T(8,128)(2,1)S(1)}, bf16[64,4224]{1,0:T(8,128)(2,1)S(1)}, u32[]{:S(2)}, u32[]{:S(2)}) %collective-permute-start.2) | collective-permute-done | bytes 540704 | tf_op jit(solution)/shard_map/ppermute | solution.py:42
  46.1 1.1 %collective-permute-start.8 = (bf16[32,4224]{1,0:T(8,128)(2,1)S(1)}, bf16[32,4224]{1,0:T(8,128)(2,1)S(1)}, u32[]{:S(2)}, u32[]{:S(2)}) collective-permute-start(bf16[32,4224]{1,0:T(8,128)(2,1)S(1)} %slice.87), channel_id=1, source_target_pairs={{0,12},{1,13},{2,14},{3,15},{4,8},{5,9},{6,10},{7,11},{8,4},{9,5},... | collective-permute-start | bytes 811016 | tf_op jit(solution)/shard_map/ppermute | solution.py:42
  47.3 2.1 %collective-permute-start.7 = (bf16[32,4224]{1,0:T(8,128)(2,1)S(1)}, bf16[32,4224]{1,0:T(8,128)(2,1)S(1)}, u32[]{:S(2)}, u32[]{:S(2)}) collective-permute-start(bf16[32,4224]{1,0:T(8,128)(2,1)S(1)} %slice.86), channel_id=1, source_target_pairs={{0,3},{1,2},{2,1},{3,0},{4,7},{5,6},{6,5},{7,4},{8,11},{9,10},{10,... | collective-permute-start | bytes 811016 | tf_op jit(solution)/shard_map/ppermute | solution.py:42
  49.4 2.7 %score.6.refs_2_ = f32[8,192]{1,0:T(8,128)S(1)} custom-call(bf16[1002,4096]{1,0:T(8,128)(2,1)S(1)} %fetch.1.w_ref, bf16[64,4224]{1,0:T(8,128)(2,1)S(1)} %collective-permute-done.2.refs_0_, bf16[64,4224]{1,0:T(8,128)(2,1)S(1)} %collective-permute-done.4.refs_1_, bf16[64,4224]{1,0:T(8,128)(2,1)S(1)} %collective-permute-done.5.refs_2_), custom_call_target="tpu_custom_call" | custom-call | flops 1576009728 | bytes 8208384 | tf_op jit(solution)/shard_map/score/pallas_call | solution.py:169
  52.0 1.9 %collective-permute-done.8 = bf16[32,4224]{1,0:T(8,128)(2,1)S(1)} collective-permute-done((bf16[32,4224]{1,0:T(8,128)(2,1)S(1)}, bf16[32,4224]{1,0:T(8,128)(2,1)S(1)}, u32[]{:S(2)}, u32[]{:S(2)}) %collective-permute-start.8) | collective-permute-done | bytes 270368 | tf_op jit(solution)/shard_map/ppermute | solution.py:42
  53.9 1.1 %collective-permute-done.7 = bf16[32,4224]{1,0:T(8,128)(2,1)S(1)} collective-permute-done((bf16[32,4224]{1,0:T(8,128)(2,1)S(1)}, bf16[32,4224]{1,0:T(8,128)(2,1)S(1)}, u32[]{:S(2)}, u32[]{:S(2)}) %collective-permute-start.7) | collective-permute-done | bytes 270368 | tf_op jit(solution)/shard_map/ppermute | solution.py:42
  55.2 2.7 %score.7.refs_3_ = f32[8,192]{1,0:T(8,128)S(1)} custom-call(bf16[1002,4096]{1,0:T(8,128)(2,1)S(1)} %fetch.1.w_ref, bf16[192,4224]{1,0:T(8,128)(2,1)S(1)} %collective-permute-done.9.refs_0_), custom_call_target="tpu_custom_call" | custom-call | flops 1576009728 | bytes 8208384 | tf_op jit(solution)/shard_map/score/pallas_call | solution.py:169
  57.9 2.6 %score_place.1 = (f32[3,8,128]{2,1,0:T(8,128)S(1)}, f32[2,8,128]{2,1,0:T(8,128)S(1)}) custom-call(bf16[1002,4096]{1,0:T(8,128)(2,1)S(1)} %fetch.1.w_ref, f32[8,256]{1,0:T(8,128)S(1)} %score.4.refs_0_, f32[8,256]{1,0:T(8,128)S(1)} %score.5.refs_1_, f32[8,192]{1,0:T(8,128)S(1)} %score.6.refs_2_, f32[8,192]{1,0:T(8,128)S(1)} %score.7.refs_3_, ...), custom_call_target="tpu_custom_call" | custom-call | flops 1050673152 | bytes 8208384 | tf_op jit(solution)/shard_map/score_place/pallas_call | solution.py:210
  61.0 0.8 %collective-permute-done.11 = f32[3,8,128]{2,1,0:T(8,128)S(1)} collective-permute-done((f32[3,8,128]{2,1,0:T(8,128)S(1)}, f32[3,8,128]{2,1,0:T(8,128)S(1)}, u32[]{:S(2)}, u32[]{:S(2)}) %collective-permute-start.11) | collective-permute-done | bytes 12320 | tf_op jit(solution)/shard_map/ppermute | solution.py:62
  62.2 2.4 %collective-permute-start.13 = (f32[3,8,128]{2,1,0:T(8,128)S(1)}, f32[3,8,128]{2,1,0:T(8,128)S(1)}, u32[]{:S(2)}, u32[]{:S(2)}) collective-permute-start(f32[3,8,128]{2,1,0:T(8,128)S(1)} %pad_maximum_fusion.3), channel_id=1, source_target_pairs={{0,112},{1,113},{2,114},{3,115},{4,116},{5,117},{6,118},{7,119},{8... | collective-permute-start | bytes 36872 | tf_op jit(solution)/shard_map/ppermute | solution.py:50
  65.1 1.5 %collective-permute-done.14 = f32[3,8,128]{2,1,0:T(8,128)S(1)} collective-permute-done((f32[3,8,128]{2,1,0:T(8,128)S(1)}, f32[3,8,128]{2,1,0:T(8,128)S(1)}, u32[]{:S(2)}, u32[]{:S(2)}) %collective-permute-start.14) | collective-permute-done | bytes 12320 | tf_op jit(solution)/shard_map/ppermute | solution.py:50
  66.6 1.1 %collective-permute-done.12 = f32[3,8,128]{2,1,0:T(8,128)S(1)} collective-permute-done((f32[3,8,128]{2,1,0:T(8,128)S(1)}, f32[3,8,128]{2,1,0:T(8,128)S(1)}, u32[]{:S(2)}, u32[]{:S(2)}) %collective-permute-start.12) | collective-permute-done | bytes 12320 | tf_op jit(solution)/shard_map/ppermute | solution.py:50
  67.9 1.5 %collective-permute-start.16 = (f32[3,8,128]{2,1,0:T(8,128)S(1)}, f32[3,8,128]{2,1,0:T(8,128)S(1)}, u32[]{:S(2)}, u32[]{:S(2)}) collective-permute-start(f32[3,8,128]{2,1,0:T(8,128)S(1)} %pad_maximum_fusion.4), channel_id=1, source_target_pairs={{0,28},{1,29},{2,30},{3,31},{4,24},{5,25},{6,26},{7,27},{8,20},{9,... | collective-permute-start | bytes 36872 | tf_op jit(solution)/shard_map/ppermute | solution.py:50
  69.3 1.7 %collective-permute-start.15 = (f32[3,8,128]{2,1,0:T(8,128)S(1)}, f32[3,8,128]{2,1,0:T(8,128)S(1)}, u32[]{:S(2)}, u32[]{:S(2)}) collective-permute-start(f32[3,8,128]{2,1,0:T(8,128)S(1)} %pad_maximum_fusion.4), channel_id=1, source_target_pairs={{0,20},{1,21},{2,22},{3,23},{4,16},{5,17},{6,18},{7,19},{8,28},{9,... | collective-permute-start | bytes 36872 | tf_op jit(solution)/shard_map/ppermute | solution.py:50
  71.0 1.5 %collective-permute-done.17 = f32[3,8,128]{2,1,0:T(8,128)S(1)} collective-permute-done((f32[3,8,128]{2,1,0:T(8,128)S(1)}, f32[3,8,128]{2,1,0:T(8,128)S(1)}, u32[]{:S(2)}, u32[]{:S(2)}) %collective-permute-start.17) | collective-permute-done | bytes 12320 | tf_op jit(solution)/shard_map/ppermute | solution.py:50
  72.5 1.4 %collective-permute-start.20 = (f32[3,8,128]{2,1,0:T(8,128)S(1)}, f32[3,8,128]{2,1,0:T(8,128)S(1)}, u32[]{:S(2)}, u32[]{:S(2)}) collective-permute-start(f32[3,8,128]{2,1,0:T(8,128)S(1)} %pad_maximum_fusion.5.refs_0_), channel_id=1, source_target_pairs={{0,18},{1,19},{2,16},{3,17},{4,22},{5,23},{6,20},{7,21},{8,26},{9,... | collective-permute-start | bytes 36872 | tf_op jit(solution)/shard_map/ppermute | solution.py:50
  74.7 1.1 %collective-permute-start.18 = (f32[3,8,128]{2,1,0:T(8,128)S(1)}, f32[3,8,128]{2,1,0:T(8,128)S(1)}, u32[]{:S(2)}, u32[]{:S(2)}) collective-permute-start(f32[3,8,128]{2,1,0:T(8,128)S(1)} %pad_maximum_fusion.5.refs_0_), channel_id=1, source_target_pairs={{0,17},{1,16},{2,19},{3,18},{4,21},{5,20},{6,23},{7,22},{8,25},{9,... | collective-permute-start | bytes 36872 | tf_op jit(solution)/shard_map/ppermute | solution.py:50
  75.8 1.5 %collective-permute-done.20.refs_3_ = f32[3,8,128]{2,1,0:T(8,128)S(1)} collective-permute-done((f32[3,8,128]{2,1,0:T(8,128)S(1)}, f32[3,8,128]{2,1,0:T(8,128)S(1)}, u32[]{:S(2)}, u32[]{:S(2)}) %collective-permute-start.20) | collective-permute-done | bytes 12320 | tf_op jit(solution)/shard_map/ppermute | solution.py:50
  77.2 1.0 %collective-permute-done.19.refs_2_ = f32[3,8,128]{2,1,0:T(8,128)S(1)} collective-permute-done((f32[3,8,128]{2,1,0:T(8,128)S(1)}, f32[3,8,128]{2,1,0:T(8,128)S(1)}, u32[]{:S(2)}, u32[]{:S(2)}) %collective-permute-start.19) | collective-permute-done | bytes 12320 | tf_op jit(solution)/shard_map/ppermute | solution.py:50
  (35 shorter events, 7.2 us)
Async XLA Ops:
  1.4 0.9 %copy-start.1 = (bf16[16,4096]{1,0:T(8,128)(2,1)S(1)}, bf16[16,4096]{1,0:T(8,128)(2,1)}, u32[]{:S(2)}) copy-start(bf16[16,4096]{1,0:T(8,128)(2,1)} %hidden_ref.1) | copy-start | bytes 393220
  16.3 11.4 %collective-permute-start = (bf16[64,4224]{1,0:T(8,128)(2,1)S(1)}, bf16[64,4224]{1,0:T(8,128)(2,1)S(1)}, u32[]{:S(2)}, u32[]{:S(2)}) collective-permute-start(bf16[64,4224]{1,0:T(8,128)(2,1)S(1)} %bitcast.8), channel_id=1, source_target_pairs={{0,3},{1,2},{2,1},{3,0},{4,7},{5,6},{6,5},{7,4},{8,11},{9,10},{10,... | collective-permute-start | bytes 1622024 | tf_op jit(solution)/shard_map/ppermute | solution.py:42
  18.4 10.7 %collective-permute-start.3 = (bf16[64,4224]{1,0:T(8,128)(2,1)S(1)}, bf16[64,4224]{1,0:T(8,128)(2,1)S(1)}, u32[]{:S(2)}, u32[]{:S(2)}) collective-permute-start(bf16[64,4224]{1,0:T(8,128)(2,1)S(1)} %bitcast.9), channel_id=1, source_target_pairs={{0,96},{1,97},{2,98},{3,99},{4,100},{5,101},{6,102},{7,103},{8,104... | collective-permute-start | bytes 1622024 | tf_op jit(solution)/shard_map/ppermute | solution.py:42
  21.1 10.6 %collective-permute-start.1 = (bf16[64,4224]{1,0:T(8,128)(2,1)S(1)}, bf16[64,4224]{1,0:T(8,128)(2,1)S(1)}, u32[]{:S(2)}, u32[]{:S(2)}) collective-permute-start(bf16[64,4224]{1,0:T(8,128)(2,1)S(1)} %bitcast.10), channel_id=1, source_target_pairs={{0,12},{1,13},{2,14},{3,15},{4,8},{5,9},{6,10},{7,11},{8,4},{9,5},... | collective-permute-start | bytes 1622024 | tf_op jit(solution)/shard_map/ppermute | solution.py:42
  23.6 3.3 %copy-start = (bf16[4096,1002]{0,1:T(8,128)(2,1)S(1)}, bf16[4096,1002]{0,1:T(8,128)(2,1)}, u32[]{:S(2)}) copy-start(bf16[4096,1002]{0,1:T(8,128)(2,1)} %param.7) | copy-start | bytes 24625156
  31.8 6.6 %collective-permute-start.6 = (bf16[256,4224]{1,0:T(8,128)(2,1)S(1)}, bf16[256,4224]{1,0:T(8,128)(2,1)S(1)}, u32[]{:S(2)}, u32[]{:S(2)}) collective-permute-start(bf16[256,4224]{1,0:T(8,128)(2,1)S(1)} %pad_maximum_fusion), channel_id=1, source_target_pairs={{0,16},{1,17},{2,18},{3,19},{4,20},{5,21},{6,22},{7,23},{8,24},{9,... | collective-permute-start | bytes 6488072 | tf_op jit(solution)/shard_map/ppermute | solution.py:62
  31.9 10.6 %collective-permute-start.4 = (bf16[64,4224]{1,0:T(8,128)(2,1)S(1)}, bf16[64,4224]{1,0:T(8,128)(2,1)S(1)}, u32[]{:S(2)}, u32[]{:S(2)}) collective-permute-start(bf16[64,4224]{1,0:T(8,128)(2,1)S(1)} %collective-permute-done.3.refs_3_), channel_id=1, source_target_pairs={{0,12},{1,13},{2,14},{3,15},{4,8},{5,9},{6,10},{7,11},{8,4},{9,5},... | collective-permute-start | bytes 1622024 | tf_op jit(solution)/shard_map/ppermute | solution.py:42
  34.5 10.6 %collective-permute-start.2 = (bf16[64,4224]{1,0:T(8,128)(2,1)S(1)}, bf16[64,4224]{1,0:T(8,128)(2,1)S(1)}, u32[]{:S(2)}, u32[]{:S(2)}) collective-permute-start(bf16[64,4224]{1,0:T(8,128)(2,1)S(1)} %collective-permute-done.1.refs_2_), channel_id=1, source_target_pairs={{0,3},{1,2},{2,1},{3,0},{4,7},{5,6},{6,5},{7,4},{8,11},{9,10},{10,... | collective-permute-start | bytes 1622024 | tf_op jit(solution)/shard_map/ppermute | solution.py:42
  35.3 10.6 %collective-permute-start.5 = (bf16[64,4224]{1,0:T(8,128)(2,1)S(1)}, bf16[64,4224]{1,0:T(8,128)(2,1)S(1)}, u32[]{:S(2)}, u32[]{:S(2)}) collective-permute-start(bf16[64,4224]{1,0:T(8,128)(2,1)S(1)} %collective-permute-done.refs_1_), channel_id=1, source_target_pairs={{0,96},{1,97},{2,98},{3,99},{4,100},{5,101},{6,102},{7,103},{8,104... | collective-permute-start | bytes 1622024 | tf_op jit(solution)/shard_map/ppermute | solution.py:42
  46.0 9.3 %collective-permute-start.9 = (bf16[192,4224]{1,0:T(8,128)(2,1)S(1)}, bf16[192,4224]{1,0:T(8,128)(2,1)S(1)}, u32[]{:S(2)}, u32[]{:S(2)}) collective-permute-start(bf16[192,4224]{1,0:T(8,128)(2,1)S(1)} %pad_maximum_fusion.1), channel_id=1, source_target_pairs={{0,16},{1,17},{2,18},{3,19},{4,20},{5,21},{6,22},{7,23},{8,24},{9,... | collective-permute-start | bytes 4866056 | tf_op jit(solution)/shard_map/ppermute | solution.py:62
  46.1 7.8 %collective-permute-start.8 = (bf16[32,4224]{1,0:T(8,128)(2,1)S(1)}, bf16[32,4224]{1,0:T(8,128)(2,1)S(1)}, u32[]{:S(2)}, u32[]{:S(2)}) collective-permute-start(bf16[32,4224]{1,0:T(8,128)(2,1)S(1)} %slice.87), channel_id=1, source_target_pairs={{0,12},{1,13},{2,14},{3,15},{4,8},{5,9},{6,10},{7,11},{8,4},{9,5},... | collective-permute-start | bytes 811016 | tf_op jit(solution)/shard_map/ppermute | solution.py:42
  47.3 7.7 %collective-permute-start.7 = (bf16[32,4224]{1,0:T(8,128)(2,1)S(1)}, bf16[32,4224]{1,0:T(8,128)(2,1)S(1)}, u32[]{:S(2)}, u32[]{:S(2)}) collective-permute-start(bf16[32,4224]{1,0:T(8,128)(2,1)S(1)} %slice.86), channel_id=1, source_target_pairs={{0,3},{1,2},{2,1},{3,0},{4,7},{5,6},{6,5},{7,4},{8,11},{9,10},{10,... | collective-permute-start | bytes 811016 | tf_op jit(solution)/shard_map/ppermute | solution.py:42
  55.0 2.9 %collective-permute-start.10 = (bf16[64,4224]{1,0:T(8,128)(2,1)S(1)}, bf16[64,4224]{1,0:T(8,128)(2,1)S(1)}, u32[]{:S(2)}, u32[]{:S(2)}) collective-permute-start(bf16[64,4224]{1,0:T(8,128)(2,1)S(1)} %pad_maximum_fusion.2.refs_4_), channel_id=1, source_target_pairs={{0,16},{1,17},{2,18},{3,19},{4,20},{5,21},{6,22},{7,23},{8,24},{9,... | collective-permute-start | bytes 1622024 | tf_op jit(solution)/shard_map/ppermute | solution.py:62
  60.5 1.4 %collective-permute-start.11 = (f32[3,8,128]{2,1,0:T(8,128)S(1)}, f32[3,8,128]{2,1,0:T(8,128)S(1)}, u32[]{:S(2)}, u32[]{:S(2)}) collective-permute-start(f32[3,8,128]{2,1,0:T(8,128)S(1)} %get-tuple-element.29), channel_id=1, source_target_pairs={{0,16},{1,17},{2,18},{3,19},{4,20},{5,21},{6,22},{7,23},{8,24},{9,... | collective-permute-start | bytes 36872 | tf_op jit(solution)/shard_map/ppermute | solution.py:62
  61.9 4.7 %collective-permute-start.14 = (f32[3,8,128]{2,1,0:T(8,128)S(1)}, f32[3,8,128]{2,1,0:T(8,128)S(1)}, u32[]{:S(2)}, u32[]{:S(2)}) collective-permute-start(f32[3,8,128]{2,1,0:T(8,128)S(1)} %pad_maximum_fusion.3), channel_id=1, source_target_pairs={{0,80},{1,81},{2,82},{3,83},{4,84},{5,85},{6,86},{7,87},{8,88},{9,... | collective-permute-start | bytes 36872 | tf_op jit(solution)/shard_map/ppermute | solution.py:50
  62.2 4.5 %collective-permute-start.13 = (f32[3,8,128]{2,1,0:T(8,128)S(1)}, f32[3,8,128]{2,1,0:T(8,128)S(1)}, u32[]{:S(2)}, u32[]{:S(2)}) collective-permute-start(f32[3,8,128]{2,1,0:T(8,128)S(1)} %pad_maximum_fusion.3), channel_id=1, source_target_pairs={{0,112},{1,113},{2,114},{3,115},{4,116},{5,117},{6,118},{7,119},{8... | collective-permute-start | bytes 36872 | tf_op jit(solution)/shard_map/ppermute | solution.py:50
  64.6 3.1 %collective-permute-start.12 = (f32[3,8,128]{2,1,0:T(8,128)S(1)}, f32[3,8,128]{2,1,0:T(8,128)S(1)}, u32[]{:S(2)}, u32[]{:S(2)}) collective-permute-start(f32[3,8,128]{2,1,0:T(8,128)S(1)} %pad_maximum_fusion.3), channel_id=1, source_target_pairs={{0,48},{1,49},{2,50},{3,51},{4,52},{5,53},{6,54},{7,55},{8,56},{9,... | collective-permute-start | bytes 36872 | tf_op jit(solution)/shard_map/ppermute | solution.py:50
  67.8 4.7 %collective-permute-start.17 = (f32[3,8,128]{2,1,0:T(8,128)S(1)}, f32[3,8,128]{2,1,0:T(8,128)S(1)}, u32[]{:S(2)}, u32[]{:S(2)}) collective-permute-start(f32[3,8,128]{2,1,0:T(8,128)S(1)} %pad_maximum_fusion.4), channel_id=1, source_target_pairs={{0,24},{1,25},{2,26},{3,27},{4,28},{5,29},{6,30},{7,31},{8,16},{9,... | collective-permute-start | bytes 36872 | tf_op jit(solution)/shard_map/ppermute | solution.py:50
  67.9 4.6 %collective-permute-start.16 = (f32[3,8,128]{2,1,0:T(8,128)S(1)}, f32[3,8,128]{2,1,0:T(8,128)S(1)}, u32[]{:S(2)}, u32[]{:S(2)}) collective-permute-start(f32[3,8,128]{2,1,0:T(8,128)S(1)} %pad_maximum_fusion.4), channel_id=1, source_target_pairs={{0,28},{1,29},{2,30},{3,31},{4,24},{5,25},{6,26},{7,27},{8,20},{9,... | collective-permute-start | bytes 36872 | tf_op jit(solution)/shard_map/ppermute | solution.py:50
  69.3 3.2 %collective-permute-start.15 = (f32[3,8,128]{2,1,0:T(8,128)S(1)}, f32[3,8,128]{2,1,0:T(8,128)S(1)}, u32[]{:S(2)}, u32[]{:S(2)}) collective-permute-start(f32[3,8,128]{2,1,0:T(8,128)S(1)} %pad_maximum_fusion.4), channel_id=1, source_target_pairs={{0,20},{1,21},{2,22},{3,23},{4,16},{5,17},{6,18},{7,19},{8,28},{9,... | collective-permute-start | bytes 36872 | tf_op jit(solution)/shard_map/ppermute | solution.py:50
  72.5 4.7 %collective-permute-start.20 = (f32[3,8,128]{2,1,0:T(8,128)S(1)}, f32[3,8,128]{2,1,0:T(8,128)S(1)}, u32[]{:S(2)}, u32[]{:S(2)}) collective-permute-start(f32[3,8,128]{2,1,0:T(8,128)S(1)} %pad_maximum_fusion.5.refs_0_), channel_id=1, source_target_pairs={{0,18},{1,19},{2,16},{3,17},{4,22},{5,23},{6,20},{7,21},{8,26},{9,... | collective-permute-start | bytes 36872 | tf_op jit(solution)/shard_map/ppermute | solution.py:50
  73.9 4.3 %collective-permute-start.19 = (f32[3,8,128]{2,1,0:T(8,128)S(1)}, f32[3,8,128]{2,1,0:T(8,128)S(1)}, u32[]{:S(2)}, u32[]{:S(2)}) collective-permute-start(f32[3,8,128]{2,1,0:T(8,128)S(1)} %pad_maximum_fusion.5.refs_0_), channel_id=1, source_target_pairs={{0,19},{1,18},{2,17},{3,16},{4,23},{5,22},{6,21},{7,20},{8,27},{9,... | collective-permute-start | bytes 36872 | tf_op jit(solution)/shard_map/ppermute | solution.py:50
  74.7 3.6 %collective-permute-start.18 = (f32[3,8,128]{2,1,0:T(8,128)S(1)}, f32[3,8,128]{2,1,0:T(8,128)S(1)}, u32[]{:S(2)}, u32[]{:S(2)}) collective-permute-start(f32[3,8,128]{2,1,0:T(8,128)S(1)} %pad_maximum_fusion.5.refs_0_), channel_id=1, source_target_pairs={{0,17},{1,16},{2,19},{3,18},{4,21},{5,20},{6,23},{7,22},{8,25},{9,... | collective-permute-start | bytes 36872 | tf_op jit(solution)/shard_map/ppermute | solution.py:50

commit v7 on v6

--- a/solution.py
+++ b/solution.py
@@ -9,7 +9,7 @@
 BENCH = 40
 N_DEV = 128
 LAB = 128
-CUTS = (0, 32, 64)
+CUTS = (0, 24, 48, 64)
 SETS = ((0, 1, 2, 4), (3, 6, 5), (7,))
 F32 = jnp.float32
 LIMIT = 12 << 20

time: 80.3 us -> 81.1 us (level)
    ppermute x8 -> x9, starting transfers between devices: 14.5 us -> 15.1 us  [exchange(): lax.ppermute(v, 'd', [(d, flipped(d, by_core[coords(d)[1]])) for d in ran...]
    ppermute x8 -> x9, waiting for transfers between devices: 11.7 us -> 11.8 us  [exchange(): lax.ppermute(v, 'd', [(d, flipped(d, by_core[coords(d)[1]])) for d in ran...]
  transfers between devices with their start and end apart: 21 -> 22, of which waited for: 13 -> 12; matrix products, arithmetic and copies ran while one was open for 0% -> 0% of each run, Pallas kernels for 14% -> 14%
where the time goes in v7:
time: 81.1 us; the launch traced here: 79.6 us
  starting transfers between devices  25.6 us (32%)
  waiting for transfers between devices  19.2 us (24%)
  Pallas kernels  15 us (18%)
  blocking collectives  13.5 us (17%)
  local copies, waits for them, and re-layouts  4.29 us (5%)
  other arithmetic  1.13 us (1%)
    ppermute x9, starting transfers between devices, exchange(): lax.ppermute(v, 'd', [(d, flipped(d, by_core[coords(d)[1]])) for d in ran...  15.1 us
    all_to_all x1, blocking collectives, body(): lax.all_to_all(x, 'd', 0, 0, axis_index_groups=early_groups())  13.5 us
    ppermute x9, waiting for transfers between devices, exchange(): lax.ppermute(v, 'd', [(d, flipped(d, by_core[coords(d)[1]])) for d in ran...  11.8 us
    pallas_call x4, Pallas kernels, score(): pl.pallas_call(score_kernel, out_shape=jax.ShapeDtypeStruct((8, rows), F3...  10.5 us
    ppermute x9, starting transfers between devices, cross_exchange(): lax.ppermute(v, 'd', [(d, flipped(d, dims) ^ 16) for d in range(N_DEV)])  9.52 us
    ppermute x9, waiting for transfers between devices, cross_exchange(): lax.ppermute(v, 'd', [(d, flipped(d, dims) ^ 16) for d in range(N_DEV)])  6.57 us
    unnamed x4, local copies, waits for them, and re-layouts  4.25 us
    pallas_call x1, Pallas kernels, score_place(): pl.pallas_call(score_place_kernel, out_shape=(jax.ShapeDtypeStruct((3, 8,...  2.55 us
  transfers between devices with their start and end apart: 22, of which 12 were waited for; matrix products, arithmetic and copies ran while one was open for 0% of the time, Pallas kernels for 14%

profile of v7, /device:TPU:0, one launch (start us, length us, event | category | flops | bytes accessed | tf_op | source)
XLA Modules:
  0.0 79.6 jit_solution(3813453845042924809)
XLA Ops:
  1.4 0.9 %copy-done.1 = bf16[16,4096]{1,0:T(8,128)(2,1)S(1)} copy-done((bf16[16,4096]{1,0:T(8,128)(2,1)S(1)}, bf16[16,4096]{1,0:T(8,128)(2,1)}, u32[]{:S(2)}) %copy-start.1) | copy-done | bytes 131096
  2.8 13.5 %all_to_all.5 = bf16[8,8,4224]{2,1,0:T(8,128)(2,1)S(1)} all-to-all(bf16[8,8,4224]{2,1,0:T(8,128)(2,1)S(1)} %get-tuple-element.19), channel_id=1, replica_groups={{0,1,4,5,32,33,36,37},{3,2,7,6,35,34,39,38},{12,13,8,9,44,45,40,41},{15..., dimensions={0} | all-to-all | bytes 1081344 | tf_op jit(solution)/shard_map/all_to_all | solution.py:302
  16.3 2.1 %collective-permute-start = (bf16[64,4224]{1,0:T(8,128)(2,1)S(1)}, bf16[64,4224]{1,0:T(8,128)(2,1)S(1)}, u32[]{:S(2)}, u32[]{:S(2)}) collective-permute-start(bf16[64,4224]{1,0:T(8,128)(2,1)S(1)} %bitcast.8), channel_id=1, source_target_pairs={{0,3},{1,2},{2,1},{3,0},{4,7},{5,6},{6,5},{7,4},{8,11},{9,10},{10,... | collective-permute-start | bytes 1622024 | tf_op jit(solution)/shard_map/ppermute | solution.py:42
  18.4 2.7 %collective-permute-start.3 = (bf16[64,4224]{1,0:T(8,128)(2,1)S(1)}, bf16[64,4224]{1,0:T(8,128)(2,1)S(1)}, u32[]{:S(2)}, u32[]{:S(2)}) collective-permute-start(bf16[64,4224]{1,0:T(8,128)(2,1)S(1)} %bitcast.9), channel_id=1, source_target_pairs={{0,96},{1,97},{2,98},{3,99},{4,100},{5,101},{6,102},{7,103},{8,104... | collective-permute-start | bytes 1622024 | tf_op jit(solution)/shard_map/ppermute | solution.py:42
  21.1 2.5 %collective-permute-start.1 = (bf16[64,4224]{1,0:T(8,128)(2,1)S(1)}, bf16[64,4224]{1,0:T(8,128)(2,1)S(1)}, u32[]{:S(2)}, u32[]{:S(2)}) collective-permute-start(bf16[64,4224]{1,0:T(8,128)(2,1)S(1)} %bitcast.10), channel_id=1, source_target_pairs={{0,12},{1,13},{2,14},{3,15},{4,8},{5,9},{6,10},{7,11},{8,4},{9,5},... | collective-permute-start | bytes 1622024 | tf_op jit(solution)/shard_map/ppermute | solution.py:42
  23.6 3.3 %copy-done = bf16[4096,1002]{0,1:T(8,128)(2,1)S(1)} copy-done((bf16[4096,1002]{0,1:T(8,128)(2,1)S(1)}, bf16[4096,1002]{0,1:T(8,128)(2,1)}, u32[]{:S(2)}) %copy-start) | copy-done | bytes 8208408
  27.7 1.4 %collective-permute-done.3.refs_3_ = bf16[64,4224]{1,0:T(8,128)(2,1)S(1)} collective-permute-done((bf16[64,4224]{1,0:T(8,128)(2,1)S(1)}, bf16[64,4224]{1,0:T(8,128)(2,1)S(1)}, u32[]{:S(2)}, u32[]{:S(2)}) %collective-permute-start.3) | collective-permute-done | bytes 540704 | tf_op jit(solution)/shard_map/ppermute | solution.py:42
  29.1 2.6 %collective-permute-done.1.refs_2_ = bf16[64,4224]{1,0:T(8,128)(2,1)S(1)} collective-permute-done((bf16[64,4224]{1,0:T(8,128)(2,1)S(1)}, bf16[64,4224]{1,0:T(8,128)(2,1)S(1)}, u32[]{:S(2)}, u32[]{:S(2)}) %collective-permute-start.1) | collective-permute-done | bytes 540704 | tf_op jit(solution)/shard_map/ppermute | solution.py:42
  31.9 2.6 %collective-permute-start.4 = (bf16[64,4224]{1,0:T(8,128)(2,1)S(1)}, bf16[64,4224]{1,0:T(8,128)(2,1)S(1)}, u32[]{:S(2)}, u32[]{:S(2)}) collective-permute-start(bf16[64,4224]{1,0:T(8,128)(2,1)S(1)} %collective-permute-done.3.refs_3_), channel_id=1, source_target_pairs={{0,12},{1,13},{2,14},{3,15},{4,8},{5,9},{6,10},{7,11},{8,4},{9,5},... | collective-permute-start | bytes 1622024 | tf_op jit(solution)/shard_map/ppermute | solution.py:42
  34.5 0.8 %collective-permute-start.2 = (bf16[64,4224]{1,0:T(8,128)(2,1)S(1)}, bf16[64,4224]{1,0:T(8,128)(2,1)S(1)}, u32[]{:S(2)}, u32[]{:S(2)}) collective-permute-start(bf16[64,4224]{1,0:T(8,128)(2,1)S(1)} %collective-permute-done.1.refs_2_), channel_id=1, source_target_pairs={{0,3},{1,2},{2,1},{3,0},{4,7},{5,6},{6,5},{7,4},{8,11},{9,10},{10,... | collective-permute-start | bytes 1622024 | tf_op jit(solution)/shard_map/ppermute | solution.py:42
  35.8 2.6 %score.4.refs_0_ = f32[8,256]{1,0:T(8,128)S(1)} custom-call(bf16[1002,4096]{1,0:T(8,128)(2,1)S(1)} %fetch.1.w_ref, bf16[64,4224]{1,0:T(8,128)(2,1)S(1)} %bitcast.12, bf16[64,4224]{1,0:T(8,128)(2,1)S(1)} %collective-permute-done.refs_1_, bf16[64,4224]{1,0:T(8,128)(2,1)S(1)} %collective-permute-done.1.refs_2_, bf16[64,4224]{1,0:T(8,128)(2,1)S(1)} %collective-permute-done.3.refs_3_), custom_call_target="tpu_custom_call" | custom-call | flops 2101346304 | bytes 8208384 | tf_op jit(solution)/shard_map/score/pallas_call | solution.py:169
  38.4 2.6 %score.5.refs_1_ = f32[8,256]{1,0:T(8,128)S(1)} custom-call(bf16[1002,4096]{1,0:T(8,128)(2,1)S(1)} %fetch.1.w_ref, bf16[256,4224]{1,0:T(8,128)(2,1)S(1)} %collective-permute-done.6.refs_0_), custom_call_target="tpu_custom_call" | custom-call | flops 2101346304 | bytes 8208384 | tf_op jit(solution)/shard_map/score/pallas_call | solution.py:169
  41.0 1.5 %collective-permute-done.4.refs_1_ = bf16[64,4224]{1,0:T(8,128)(2,1)S(1)} collective-permute-done((bf16[64,4224]{1,0:T(8,128)(2,1)S(1)}, bf16[64,4224]{1,0:T(8,128)(2,1)S(1)}, u32[]{:S(2)}, u32[]{:S(2)}) %collective-permute-start.4) | collective-permute-done | bytes 540704 | tf_op jit(solution)/shard_map/ppermute | solution.py:42
  42.5 2.5 %collective-permute-done.2.refs_0_ = bf16[64,4224]{1,0:T(8,128)(2,1)S(1)} collective-permute-done((bf16[64,4224]{1,0:T(8,128)(2,1)S(1)}, bf16[64,4224]{1,0:T(8,128)(2,1)S(1)}, u32[]{:S(2)}, u32[]{:S(2)}) %collective-permute-start.2) | collective-permute-done | bytes 540704 | tf_op jit(solution)/shard_map/ppermute | solution.py:42
  45.0 0.8 %collective-permute-done.5.refs_2_ = bf16[64,4224]{1,0:T(8,128)(2,1)S(1)} collective-permute-done((bf16[64,4224]{1,0:T(8,128)(2,1)S(1)}, bf16[64,4224]{1,0:T(8,128)(2,1)S(1)}, u32[]{:S(2)}, u32[]{:S(2)}) %collective-permute-start.5) | collective-permute-done | bytes 540704 | tf_op jit(solution)/shard_map/ppermute | solution.py:42
  46.1 1.1 %collective-permute-start.8 = (bf16[24,4224]{1,0:T(8,128)(2,1)S(1)}, bf16[24,4224]{1,0:T(8,128)(2,1)S(1)}, u32[]{:S(2)}, u32[]{:S(2)}) collective-permute-start(bf16[24,4224]{1,0:T(8,128)(2,1)S(1)} %slice.90), channel_id=1, source_target_pairs={{0,12},{1,13},{2,14},{3,15},{4,8},{5,9},{6,10},{7,11},{8,4},{9,5},... | collective-permute-start | bytes 608264 | tf_op jit(solution)/shard_map/ppermute | solution.py:42
  47.2 2.1 %collective-permute-start.7 = (bf16[24,4224]{1,0:T(8,128)(2,1)S(1)}, bf16[24,4224]{1,0:T(8,128)(2,1)S(1)}, u32[]{:S(2)}, u32[]{:S(2)}) collective-permute-start(bf16[24,4224]{1,0:T(8,128)(2,1)S(1)} %slice.89), channel_id=1, source_target_pairs={{0,3},{1,2},{2,1},{3,0},{4,7},{5,6},{6,5},{7,4},{8,11},{9,10},{10,... | collective-permute-start | bytes 608264 | tf_op jit(solution)/shard_map/ppermute | solution.py:42
  50.0 2.7 %score.6.refs_2_ = f32[8,192]{1,0:T(8,128)S(1)} custom-call(bf16[1002,4096]{1,0:T(8,128)(2,1)S(1)} %fetch.1.w_ref, bf16[64,4224]{1,0:T(8,128)(2,1)S(1)} %collective-permute-done.2.refs_0_, bf16[64,4224]{1,0:T(8,128)(2,1)S(1)} %collective-permute-done.4.refs_1_, bf16[64,4224]{1,0:T(8,128)(2,1)S(1)} %collective-permute-done.5.refs_2_), custom_call_target="tpu_custom_call" | custom-call | flops 1576009728 | bytes 8208384 | tf_op jit(solution)/shard_map/score/pallas_call | solution.py:169
  52.6 3.0 %collective-permute-done.9 = bf16[16,4224]{1,0:T(8,128)(2,1)S(1)} collective-permute-done((bf16[16,4224]{1,0:T(8,128)(2,1)S(1)}, bf16[16,4224]{1,0:T(8,128)(2,1)S(1)}, u32[]{:S(2)}, u32[]{:S(2)}) %collective-permute-start.9) | collective-permute-done | bytes 135200 | tf_op jit(solution)/shard_map/ppermute | solution.py:42
  56.0 2.7 %score.7.refs_3_ = f32[8,192]{1,0:T(8,128)S(1)} custom-call(bf16[1002,4096]{1,0:T(8,128)(2,1)S(1)} %fetch.1.w_ref, bf16[192,4224]{1,0:T(8,128)(2,1)S(1)} %collective-permute-done.10.refs_0_), custom_call_target="tpu_custom_call" | custom-call | flops 1576009728 | bytes 8208384 | tf_op jit(solution)/shard_map/score/pallas_call | solution.py:169
  58.7 2.6 %score_place.1 = (f32[3,8,128]{2,1,0:T(8,128)S(1)}, f32[2,8,128]{2,1,0:T(8,128)S(1)}) custom-call(bf16[1002,4096]{1,0:T(8,128)(2,1)S(1)} %fetch.1.w_ref, f32[8,256]{1,0:T(8,128)S(1)} %score.4.refs_0_, f32[8,256]{1,0:T(8,128)S(1)} %score.5.refs_1_, f32[8,192]{1,0:T(8,128)S(1)} %score.6.refs_2_, f32[8,192]{1,0:T(8,128)S(1)} %score.7.refs_3_, ...), custom_call_target="tpu_custom_call" | custom-call | flops 1050673152 | bytes 8208384 | tf_op jit(solution)/shard_map/score_place/pallas_call | solution.py:210
  61.8 0.8 %collective-permute-done.12 = f32[3,8,128]{2,1,0:T(8,128)S(1)} collective-permute-done((f32[3,8,128]{2,1,0:T(8,128)S(1)}, f32[3,8,128]{2,1,0:T(8,128)S(1)}, u32[]{:S(2)}, u32[]{:S(2)}) %collective-permute-start.12) | collective-permute-done | bytes 12320 | tf_op jit(solution)/shard_map/ppermute | solution.py:62
  62.7 1.3 %collective-permute-start.14 = (f32[3,8,128]{2,1,0:T(8,128)S(1)}, f32[3,8,128]{2,1,0:T(8,128)S(1)}, u32[]{:S(2)}, u32[]{:S(2)}) collective-permute-start(f32[3,8,128]{2,1,0:T(8,128)S(1)} %pad_maximum_fusion.3), channel_id=1, source_target_pairs={{0,112},{1,113},{2,114},{3,115},{4,116},{5,117},{6,118},{7,119},{8... | collective-permute-start | bytes 36872 | tf_op jit(solution)/shard_map/ppermute | solution.py:50
  64.1 1.8 %collective-permute-start.13 = (f32[3,8,128]{2,1,0:T(8,128)S(1)}, f32[3,8,128]{2,1,0:T(8,128)S(1)}, u32[]{:S(2)}, u32[]{:S(2)}) collective-permute-start(f32[3,8,128]{2,1,0:T(8,128)S(1)} %pad_maximum_fusion.3), channel_id=1, source_target_pairs={{0,48},{1,49},{2,50},{3,51},{4,52},{5,53},{6,54},{7,55},{8,56},{9,... | collective-permute-start | bytes 36872 | tf_op jit(solution)/shard_map/ppermute | solution.py:50
  65.9 1.5 %collective-permute-done.15 = f32[3,8,128]{2,1,0:T(8,128)S(1)} collective-permute-done((f32[3,8,128]{2,1,0:T(8,128)S(1)}, f32[3,8,128]{2,1,0:T(8,128)S(1)}, u32[]{:S(2)}, u32[]{:S(2)}) %collective-permute-start.15) | collective-permute-done | bytes 12320 | tf_op jit(solution)/shard_map/ppermute | solution.py:50
  67.5 2.5 %collective-permute-start.17 = (f32[3,8,128]{2,1,0:T(8,128)S(1)}, f32[3,8,128]{2,1,0:T(8,128)S(1)}, u32[]{:S(2)}, u32[]{:S(2)}) collective-permute-start(f32[3,8,128]{2,1,0:T(8,128)S(1)} %pad_maximum_fusion.4), channel_id=1, source_target_pairs={{0,28},{1,29},{2,30},{3,31},{4,24},{5,25},{6,26},{7,27},{8,20},{9,... | collective-permute-start | bytes 36872 | tf_op jit(solution)/shard_map/ppermute | solution.py:50
  70.6 1.5 %collective-permute-done.18 = f32[3,8,128]{2,1,0:T(8,128)S(1)} collective-permute-done((f32[3,8,128]{2,1,0:T(8,128)S(1)}, f32[3,8,128]{2,1,0:T(8,128)S(1)}, u32[]{:S(2)}, u32[]{:S(2)}) %collective-permute-start.18) | collective-permute-done | bytes 12320 | tf_op jit(solution)/shard_map/ppermute | solution.py:50
  72.1 1.1 %collective-permute-done.16 = f32[3,8,128]{2,1,0:T(8,128)S(1)} collective-permute-done((f32[3,8,128]{2,1,0:T(8,128)S(1)}, f32[3,8,128]{2,1,0:T(8,128)S(1)}, u32[]{:S(2)}, u32[]{:S(2)}) %collective-permute-start.16) | collective-permute-done | bytes 12320 | tf_op jit(solution)/shard_map/ppermute | solution.py:50
  73.2 1.3 %collective-permute-start.21 = (f32[3,8,128]{2,1,0:T(8,128)S(1)}, f32[3,8,128]{2,1,0:T(8,128)S(1)}, u32[]{:S(2)}, u32[]{:S(2)}) collective-permute-start(f32[3,8,128]{2,1,0:T(8,128)S(1)} %pad_maximum_fusion.5.refs_0_), channel_id=1, source_target_pairs={{0,18},{1,19},{2,16},{3,17},{4,22},{5,23},{6,20},{7,21},{8,26},{9,... | collective-permute-start | bytes 36872 | tf_op jit(solution)/shard_map/ppermute | solution.py:50
  75.2 1.0 %collective-permute-start.19 = (f32[3,8,128]{2,1,0:T(8,128)S(1)}, f32[3,8,128]{2,1,0:T(8,128)S(1)}, u32[]{:S(2)}, u32[]{:S(2)}) collective-permute-start(f32[3,8,128]{2,1,0:T(8,128)S(1)} %pad_maximum_fusion.5.refs_0_), channel_id=1, source_target_pairs={{0,17},{1,16},{2,19},{3,18},{4,21},{5,20},{6,23},{7,22},{8,25},{9,... | collective-permute-start | bytes 36872 | tf_op jit(solution)/shard_map/ppermute | solution.py:50
  76.2 1.6 %collective-permute-done.21.refs_3_ = f32[3,8,128]{2,1,0:T(8,128)S(1)} collective-permute-done((f32[3,8,128]{2,1,0:T(8,128)S(1)}, f32[3,8,128]{2,1,0:T(8,128)S(1)}, u32[]{:S(2)}, u32[]{:S(2)}) %collective-permute-start.21) | collective-permute-done | bytes 12320 | tf_op jit(solution)/shard_map/ppermute | solution.py:50
  77.9 0.9 %collective-permute-done.20.refs_2_ = f32[3,8,128]{2,1,0:T(8,128)S(1)} collective-permute-done((f32[3,8,128]{2,1,0:T(8,128)S(1)}, f32[3,8,128]{2,1,0:T(8,128)S(1)}, u32[]{:S(2)}, u32[]{:S(2)}) %collective-permute-start.20) | collective-permute-done | bytes 12320 | tf_op jit(solution)/shard_map/ppermute | solution.py:50
  (38 shorter events, 6.9 us)
Async XLA Ops:
  1.4 0.9 %copy-start.1 = (bf16[16,4096]{1,0:T(8,128)(2,1)S(1)}, bf16[16,4096]{1,0:T(8,128)(2,1)}, u32[]{:S(2)}) copy-start(bf16[16,4096]{1,0:T(8,128)(2,1)} %hidden_ref.1) | copy-start | bytes 393220
  16.3 11.4 %collective-permute-start = (bf16[64,4224]{1,0:T(8,128)(2,1)S(1)}, bf16[64,4224]{1,0:T(8,128)(2,1)S(1)}, u32[]{:S(2)}, u32[]{:S(2)}) collective-permute-start(bf16[64,4224]{1,0:T(8,128)(2,1)S(1)} %bitcast.8), channel_id=1, source_target_pairs={{0,3},{1,2},{2,1},{3,0},{4,7},{5,6},{6,5},{7,4},{8,11},{9,10},{10,... | collective-permute-start | bytes 1622024 | tf_op jit(solution)/shard_map/ppermute | solution.py:42
  18.4 10.7 %collective-permute-start.3 = (bf16[64,4224]{1,0:T(8,128)(2,1)S(1)}, bf16[64,4224]{1,0:T(8,128)(2,1)S(1)}, u32[]{:S(2)}, u32[]{:S(2)}) collective-permute-start(bf16[64,4224]{1,0:T(8,128)(2,1)S(1)} %bitcast.9), channel_id=1, source_target_pairs={{0,96},{1,97},{2,98},{3,99},{4,100},{5,101},{6,102},{7,103},{8,104... | collective-permute-start | bytes 1622024 | tf_op jit(solution)/shard_map/ppermute | solution.py:42
  21.1 10.6 %collective-permute-start.1 = (bf16[64,4224]{1,0:T(8,128)(2,1)S(1)}, bf16[64,4224]{1,0:T(8,128)(2,1)S(1)}, u32[]{:S(2)}, u32[]{:S(2)}) collective-permute-start(bf16[64,4224]{1,0:T(8,128)(2,1)S(1)} %bitcast.10), channel_id=1, source_target_pairs={{0,12},{1,13},{2,14},{3,15},{4,8},{5,9},{6,10},{7,11},{8,4},{9,5},... | collective-permute-start | bytes 1622024 | tf_op jit(solution)/shard_map/ppermute | solution.py:42
  23.6 3.3 %copy-start = (bf16[4096,1002]{0,1:T(8,128)(2,1)S(1)}, bf16[4096,1002]{0,1:T(8,128)(2,1)}, u32[]{:S(2)}) copy-start(bf16[4096,1002]{0,1:T(8,128)(2,1)} %param.7) | copy-start | bytes 24625156
  31.8 6.6 %collective-permute-start.6 = (bf16[256,4224]{1,0:T(8,128)(2,1)S(1)}, bf16[256,4224]{1,0:T(8,128)(2,1)S(1)}, u32[]{:S(2)}, u32[]{:S(2)}) collective-permute-start(bf16[256,4224]{1,0:T(8,128)(2,1)S(1)} %pad_maximum_fusion), channel_id=1, source_target_pairs={{0,16},{1,17},{2,18},{3,19},{4,20},{5,21},{6,22},{7,23},{8,24},{9,... | collective-permute-start | bytes 6488072 | tf_op jit(solution)/shard_map/ppermute | solution.py:62
  31.9 10.6 %collective-permute-start.4 = (bf16[64,4224]{1,0:T(8,128)(2,1)S(1)}, bf16[64,4224]{1,0:T(8,128)(2,1)S(1)}, u32[]{:S(2)}, u32[]{:S(2)}) collective-permute-start(bf16[64,4224]{1,0:T(8,128)(2,1)S(1)} %collective-permute-done.3.refs_3_), channel_id=1, source_target_pairs={{0,12},{1,13},{2,14},{3,15},{4,8},{5,9},{6,10},{7,11},{8,4},{9,5},... | collective-permute-start | bytes 1622024 | tf_op jit(solution)/shard_map/ppermute | solution.py:42
  34.5 10.6 %collective-permute-start.2 = (bf16[64,4224]{1,0:T(8,128)(2,1)S(1)}, bf16[64,4224]{1,0:T(8,128)(2,1)S(1)}, u32[]{:S(2)}, u32[]{:S(2)}) collective-permute-start(bf16[64,4224]{1,0:T(8,128)(2,1)S(1)} %collective-permute-done.1.refs_2_), channel_id=1, source_target_pairs={{0,3},{1,2},{2,1},{3,0},{4,7},{5,6},{6,5},{7,4},{8,11},{9,10},{10,... | collective-permute-start | bytes 1622024 | tf_op jit(solution)/shard_map/ppermute | solution.py:42
  35.3 10.6 %collective-permute-start.5 = (bf16[64,4224]{1,0:T(8,128)(2,1)S(1)}, bf16[64,4224]{1,0:T(8,128)(2,1)S(1)}, u32[]{:S(2)}, u32[]{:S(2)}) collective-permute-start(bf16[64,4224]{1,0:T(8,128)(2,1)S(1)} %collective-permute-done.refs_1_), channel_id=1, source_target_pairs={{0,96},{1,97},{2,98},{3,99},{4,100},{5,101},{6,102},{7,103},{8,104... | collective-permute-start | bytes 1622024 | tf_op jit(solution)/shard_map/ppermute | solution.py:42
  46.0 10.0 %collective-permute-start.10 = (bf16[192,4224]{1,0:T(8,128)(2,1)S(1)}, bf16[192,4224]{1,0:T(8,128)(2,1)S(1)}, u32[]{:S(2)}, u32[]{:S(2)}) collective-permute-start(bf16[192,4224]{1,0:T(8,128)(2,1)S(1)} %pad_maximum_fusion.1), channel_id=1, source_target_pairs={{0,16},{1,17},{2,18},{3,19},{4,20},{5,21},{6,22},{7,23},{8,24},{9,... | collective-permute-start | bytes 4866056 | tf_op jit(solution)/shard_map/ppermute | solution.py:62
  46.1 9.6 %collective-permute-start.8 = (bf16[24,4224]{1,0:T(8,128)(2,1)S(1)}, bf16[24,4224]{1,0:T(8,128)(2,1)S(1)}, u32[]{:S(2)}, u32[]{:S(2)}) collective-permute-start(bf16[24,4224]{1,0:T(8,128)(2,1)S(1)} %slice.90), channel_id=1, source_target_pairs={{0,12},{1,13},{2,14},{3,15},{4,8},{5,9},{6,10},{7,11},{8,4},{9,5},... | collective-permute-start | bytes 608264 | tf_op jit(solution)/shard_map/ppermute | solution.py:42
  47.2 8.4 %collective-permute-start.7 = (bf16[24,4224]{1,0:T(8,128)(2,1)S(1)}, bf16[24,4224]{1,0:T(8,128)(2,1)S(1)}, u32[]{:S(2)}, u32[]{:S(2)}) collective-permute-start(bf16[24,4224]{1,0:T(8,128)(2,1)S(1)} %slice.89), channel_id=1, source_target_pairs={{0,3},{1,2},{2,1},{3,0},{4,7},{5,6},{6,5},{7,4},{8,11},{9,10},{10,... | collective-permute-start | bytes 608264 | tf_op jit(solution)/shard_map/ppermute | solution.py:42
  49.4 6.3 %collective-permute-start.9 = (bf16[16,4224]{1,0:T(8,128)(2,1)S(1)}, bf16[16,4224]{1,0:T(8,128)(2,1)S(1)}, u32[]{:S(2)}, u32[]{:S(2)}) collective-permute-start(bf16[16,4224]{1,0:T(8,128)(2,1)S(1)} %slice.91), channel_id=1, source_target_pairs={{0,96},{1,97},{2,98},{3,99},{4,100},{5,101},{6,102},{7,103},{8,104... | collective-permute-start | bytes 405512 | tf_op jit(solution)/shard_map/ppermute | solution.py:42
  55.7 2.9 %collective-permute-start.11 = (bf16[64,4224]{1,0:T(8,128)(2,1)S(1)}, bf16[64,4224]{1,0:T(8,128)(2,1)S(1)}, u32[]{:S(2)}, u32[]{:S(2)}) collective-permute-start(bf16[64,4224]{1,0:T(8,128)(2,1)S(1)} %pad_maximum_fusion.2.refs_4_), channel_id=1, source_target_pairs={{0,16},{1,17},{2,18},{3,19},{4,20},{5,21},{6,22},{7,23},{8,24},{9,... | collective-permute-start | bytes 1622024 | tf_op jit(solution)/shard_map/ppermute | solution.py:62
  61.2 1.4 %collective-permute-start.12 = (f32[3,8,128]{2,1,0:T(8,128)S(1)}, f32[3,8,128]{2,1,0:T(8,128)S(1)}, u32[]{:S(2)}, u32[]{:S(2)}) collective-permute-start(f32[3,8,128]{2,1,0:T(8,128)S(1)} %get-tuple-element.29), channel_id=1, source_target_pairs={{0,16},{1,17},{2,18},{3,19},{4,20},{5,21},{6,22},{7,23},{8,24},{9,... | collective-permute-start | bytes 36872 | tf_op jit(solution)/shard_map/ppermute | solution.py:62
  62.6 4.7 %collective-permute-start.15 = (f32[3,8,128]{2,1,0:T(8,128)S(1)}, f32[3,8,128]{2,1,0:T(8,128)S(1)}, u32[]{:S(2)}, u32[]{:S(2)}) collective-permute-start(f32[3,8,128]{2,1,0:T(8,128)S(1)} %pad_maximum_fusion.3), channel_id=1, source_target_pairs={{0,80},{1,81},{2,82},{3,83},{4,84},{5,85},{6,86},{7,87},{8,88},{9,... | collective-permute-start | bytes 36872 | tf_op jit(solution)/shard_map/ppermute | solution.py:50
  62.7 4.6 %collective-permute-start.14 = (f32[3,8,128]{2,1,0:T(8,128)S(1)}, f32[3,8,128]{2,1,0:T(8,128)S(1)}, u32[]{:S(2)}, u32[]{:S(2)}) collective-permute-start(f32[3,8,128]{2,1,0:T(8,128)S(1)} %pad_maximum_fusion.3), channel_id=1, source_target_pairs={{0,112},{1,113},{2,114},{3,115},{4,116},{5,117},{6,118},{7,119},{8... | collective-permute-start | bytes 36872 | tf_op jit(solution)/shard_map/ppermute | solution.py:50
  64.1 3.3 %collective-permute-start.13 = (f32[3,8,128]{2,1,0:T(8,128)S(1)}, f32[3,8,128]{2,1,0:T(8,128)S(1)}, u32[]{:S(2)}, u32[]{:S(2)}) collective-permute-start(f32[3,8,128]{2,1,0:T(8,128)S(1)} %pad_maximum_fusion.3), channel_id=1, source_target_pairs={{0,48},{1,49},{2,50},{3,51},{4,52},{5,53},{6,54},{7,55},{8,56},{9,... | collective-permute-start | bytes 36872 | tf_op jit(solution)/shard_map/ppermute | solution.py:50
  67.4 4.7 %collective-permute-start.18 = (f32[3,8,128]{2,1,0:T(8,128)S(1)}, f32[3,8,128]{2,1,0:T(8,128)S(1)}, u32[]{:S(2)}, u32[]{:S(2)}) collective-permute-start(f32[3,8,128]{2,1,0:T(8,128)S(1)} %pad_maximum_fusion.4), channel_id=1, source_target_pairs={{0,24},{1,25},{2,26},{3,27},{4,28},{5,29},{6,30},{7,31},{8,16},{9,... | collective-permute-start | bytes 36872 | tf_op jit(solution)/shard_map/ppermute | solution.py:50
  67.5 4.6 %collective-permute-start.17 = (f32[3,8,128]{2,1,0:T(8,128)S(1)}, f32[3,8,128]{2,1,0:T(8,128)S(1)}, u32[]{:S(2)}, u32[]{:S(2)}) collective-permute-start(f32[3,8,128]{2,1,0:T(8,128)S(1)} %pad_maximum_fusion.4), channel_id=1, source_target_pairs={{0,28},{1,29},{2,30},{3,31},{4,24},{5,25},{6,26},{7,27},{8,20},{9,... | collective-permute-start | bytes 36872 | tf_op jit(solution)/shard_map/ppermute | solution.py:50
  70.0 3.1 %collective-permute-start.16 = (f32[3,8,128]{2,1,0:T(8,128)S(1)}, f32[3,8,128]{2,1,0:T(8,128)S(1)}, u32[]{:S(2)}, u32[]{:S(2)}) collective-permute-start(f32[3,8,128]{2,1,0:T(8,128)S(1)} %pad_maximum_fusion.4), channel_id=1, source_target_pairs={{0,20},{1,21},{2,22},{3,23},{4,16},{5,17},{6,18},{7,19},{8,28},{9,... | collective-permute-start | bytes 36872 | tf_op jit(solution)/shard_map/ppermute | solution.py:50
  73.2 4.7 %collective-permute-start.21 = (f32[3,8,128]{2,1,0:T(8,128)S(1)}, f32[3,8,128]{2,1,0:T(8,128)S(1)}, u32[]{:S(2)}, u32[]{:S(2)}) collective-permute-start(f32[3,8,128]{2,1,0:T(8,128)S(1)} %pad_maximum_fusion.5.refs_0_), channel_id=1, source_target_pairs={{0,18},{1,19},{2,16},{3,17},{4,22},{5,23},{6,20},{7,21},{8,26},{9,... | collective-permute-start | bytes 36872 | tf_op jit(solution)/shard_map/ppermute | solution.py:50
  74.5 4.3 %collective-permute-start.20 = (f32[3,8,128]{2,1,0:T(8,128)S(1)}, f32[3,8,128]{2,1,0:T(8,128)S(1)}, u32[]{:S(2)}, u32[]{:S(2)}) collective-permute-start(f32[3,8,128]{2,1,0:T(8,128)S(1)} %pad_maximum_fusion.5.refs_0_), channel_id=1, source_target_pairs={{0,19},{1,18},{2,17},{3,16},{4,23},{5,22},{6,21},{7,20},{8,27},{9,... | collective-permute-start | bytes 36872 | tf_op jit(solution)/shard_map/ppermute | solution.py:50
  75.2 3.6 %collective-permute-start.19 = (f32[3,8,128]{2,1,0:T(8,128)S(1)}, f32[3,8,128]{2,1,0:T(8,128)S(1)}, u32[]{:S(2)}, u32[]{:S(2)}) collective-permute-start(f32[3,8,128]{2,1,0:T(8,128)S(1)} %pad_maximum_fusion.5.refs_0_), channel_id=1, source_target_pairs={{0,17},{1,16},{2,19},{3,18},{4,21},{5,20},{6,23},{7,22},{8,25},{9,... | collective-permute-start | bytes 36872 | tf_op jit(solution)/shard_map/ppermute | solution.py:50

commit v8 on v6

--- a/solution.py
+++ b/solution.py
@@ -301,7 +301,7 @@
     x, aux = pack(hidden, targets, bench_ids, valid, seq_lengths)
     x = lax.all_to_all(x, "d", 0, 0, axis_index_groups=early_groups()).reshape(-1, x.shape[-1])
     near = [late_exchange(x, k) for k in range(3)]
-    near[0], w = tied(near[0], fetch(head_weight.T))
+    near[1], w = tied(near[1], fetch(head_weight.T))
     near_rows = [x, *near]
     own1 = score(w, near_rows)
     sib1 = score(w, [core_swap(jnp.concatenate(near_rows, 0))])

time: 80.3 us -> 80.3 us (level)
  starting transfers between devices: 25.2 us -> 26.2 us
  waiting for transfers between devices: 19.1 us -> 18.1 us
    ppermute x9, waiting for transfers between devices: 6.58 us -> 5.34 us  [cross_exchange(): lax.ppermute(v, 'd', [(d, flipped(d, dims) ^ 16) for d in range(N_DEV)])]
    ppermute x8, starting transfers between devices: 14.5 us -> 15.4 us  [exchange(): lax.ppermute(v, 'd', [(d, flipped(d, by_core[coords(d)[1]])) for d in ran...]
where the time goes in v8:
time: 80.3 us; the launch traced here: 79 us
  starting transfers between devices  26.2 us (33%)
  waiting for transfers between devices  18.1 us (23%)
  Pallas kernels  15 us (19%)
  blocking collectives  13.5 us (17%)
  local copies, waits for them, and re-layouts  4.29 us (5%)
  other arithmetic  1.13 us (1%)
    ppermute x8, starting transfers between devices, exchange(): lax.ppermute(v, 'd', [(d, flipped(d, by_core[coords(d)[1]])) for d in ran...  15.4 us
    all_to_all x1, blocking collectives, body(): lax.all_to_all(x, 'd', 0, 0, axis_index_groups=early_groups())  13.5 us
    ppermute x8, waiting for transfers between devices, exchange(): lax.ppermute(v, 'd', [(d, flipped(d, by_core[coords(d)[1]])) for d in ran...  11.9 us
    pallas_call x4, Pallas kernels, score(): pl.pallas_call(score_kernel, out_shape=jax.ShapeDtypeStruct((8, rows), F3...  10.5 us
    ppermute x9, starting transfers between devices, cross_exchange(): lax.ppermute(v, 'd', [(d, flipped(d, dims) ^ 16) for d in range(N_DEV)])  9.51 us
    ppermute x9, waiting for transfers between devices, cross_exchange(): lax.ppermute(v, 'd', [(d, flipped(d, dims) ^ 16) for d in range(N_DEV)])  5.34 us
    unnamed x4, local copies, waits for them, and re-layouts  4.25 us
    pallas_call x1, Pallas kernels, score_place(): pl.pallas_call(score_place_kernel, out_shape=(jax.ShapeDtypeStruct((3, 8,...  2.55 us
  transfers between devices with their start and end apart: 21, of which 13 were waited for; matrix products, arithmetic and copies ran while one was open for 0% of the time, Pallas kernels for 14%

profile of v8, /device:TPU:0, one launch (start us, length us, event | category | flops | bytes accessed | tf_op | source)
XLA Modules:
  0.0 79.0 jit_solution(18137067031921120522)
XLA Ops:
  0.6 0.8 add_bitcast_fusion.ints_ref
  1.4 0.9 %copy-done.1 = bf16[16,4096]{1,0:T(8,128)(2,1)S(1)} copy-done((bf16[16,4096]{1,0:T(8,128)(2,1)S(1)}, bf16[16,4096]{1,0:T(8,128)(2,1)}, u32[]{:S(2)}) %copy-start.1) | copy-done | bytes 131096
  2.8 13.5 %all_to_all.5 = bf16[8,8,4224]{2,1,0:T(8,128)(2,1)S(1)} all-to-all(bf16[8,8,4224]{2,1,0:T(8,128)(2,1)S(1)} %get-tuple-element.19), channel_id=1, replica_groups={{0,1,4,5,32,33,36,37},{3,2,7,6,35,34,39,38},{12,13,8,9,44,45,40,41},{15..., dimensions={0} | all-to-all | bytes 1081344 | tf_op jit(solution)/shard_map/all_to_all | solution.py:302
  16.3 2.2 %collective-permute-start = (bf16[64,4224]{1,0:T(8,128)(2,1)S(1)}, bf16[64,4224]{1,0:T(8,128)(2,1)S(1)}, u32[]{:S(2)}, u32[]{:S(2)}) collective-permute-start(bf16[64,4224]{1,0:T(8,128)(2,1)S(1)} %bitcast.8), channel_id=1, source_target_pairs={{0,12},{1,13},{2,14},{3,15},{4,8},{5,9},{6,10},{7,11},{8,4},{9,5},... | collective-permute-start | bytes 1622024 | tf_op jit(solution)/shard_map/ppermute | solution.py:42
  18.5 2.1 %collective-permute-start.4 = (bf16[64,4224]{1,0:T(8,128)(2,1)S(1)}, bf16[64,4224]{1,0:T(8,128)(2,1)S(1)}, u32[]{:S(2)}, u32[]{:S(2)}) collective-permute-start(bf16[64,4224]{1,0:T(8,128)(2,1)S(1)} %bitcast.9), channel_id=1, source_target_pairs={{0,3},{1,2},{2,1},{3,0},{4,7},{5,6},{6,5},{7,4},{8,11},{9,10},{10,... | collective-permute-start | bytes 1622024 | tf_op jit(solution)/shard_map/ppermute | solution.py:42
  20.6 3.0 %collective-permute-start.2 = (bf16[64,4224]{1,0:T(8,128)(2,1)S(1)}, bf16[64,4224]{1,0:T(8,128)(2,1)S(1)}, u32[]{:S(2)}, u32[]{:S(2)}) collective-permute-start(bf16[64,4224]{1,0:T(8,128)(2,1)S(1)} %bitcast.10), channel_id=1, source_target_pairs={{0,96},{1,97},{2,98},{3,99},{4,100},{5,101},{6,102},{7,103},{8,104... | collective-permute-start | bytes 1622024 | tf_op jit(solution)/shard_map/ppermute | solution.py:42
  23.6 3.3 %copy-done = bf16[4096,1002]{0,1:T(8,128)(2,1)S(1)} copy-done((bf16[4096,1002]{0,1:T(8,128)(2,1)S(1)}, bf16[4096,1002]{0,1:T(8,128)(2,1)}, u32[]{:S(2)}) %copy-start) | copy-done | bytes 8208408
  27.7 1.4 %collective-permute-done.4.refs_1_ = bf16[64,4224]{1,0:T(8,128)(2,1)S(1)} collective-permute-done((bf16[64,4224]{1,0:T(8,128)(2,1)S(1)}, bf16[64,4224]{1,0:T(8,128)(2,1)S(1)}, u32[]{:S(2)}, u32[]{:S(2)}) %collective-permute-start.4) | collective-permute-done | bytes 540704 | tf_op jit(solution)/shard_map/ppermute | solution.py:42
  29.0 2.1 %collective-permute-done.2.refs_3_ = bf16[64,4224]{1,0:T(8,128)(2,1)S(1)} collective-permute-done((bf16[64,4224]{1,0:T(8,128)(2,1)S(1)}, bf16[64,4224]{1,0:T(8,128)(2,1)S(1)}, u32[]{:S(2)}, u32[]{:S(2)}) %collective-permute-start.2) | collective-permute-done | bytes 540704 | tf_op jit(solution)/shard_map/ppermute | solution.py:42
  31.6 2.9 %collective-permute-start.5 = (bf16[64,4224]{1,0:T(8,128)(2,1)S(1)}, bf16[64,4224]{1,0:T(8,128)(2,1)S(1)}, u32[]{:S(2)}, u32[]{:S(2)}) collective-permute-start(bf16[64,4224]{1,0:T(8,128)(2,1)S(1)} %collective-permute-done.4.refs_1_), channel_id=1, source_target_pairs={{0,96},{1,97},{2,98},{3,99},{4,100},{5,101},{6,102},{7,103},{8,104... | collective-permute-start | bytes 1622024 | tf_op jit(solution)/shard_map/ppermute | solution.py:42
  35.2 1.1 %collective-permute-start.1 = (bf16[64,4224]{1,0:T(8,128)(2,1)S(1)}, bf16[64,4224]{1,0:T(8,128)(2,1)S(1)}, u32[]{:S(2)}, u32[]{:S(2)}) collective-permute-start(bf16[64,4224]{1,0:T(8,128)(2,1)S(1)} %collective-permute-done.refs_2_), channel_id=1, source_target_pairs={{0,3},{1,2},{2,1},{3,0},{4,7},{5,6},{6,5},{7,4},{8,11},{9,10},{10,... | collective-permute-start | bytes 1622024 | tf_op jit(solution)/shard_map/ppermute | solution.py:42
  36.3 2.6 %score.4.refs_0_ = f32[8,256]{1,0:T(8,128)S(1)} custom-call(bf16[1002,4096]{1,0:T(8,128)(2,1)S(1)} %fetch.1.w_ref, bf16[64,4224]{1,0:T(8,128)(2,1)S(1)} %bitcast.12, bf16[64,4224]{1,0:T(8,128)(2,1)S(1)} %collective-permute-done.4.refs_1_, bf16[64,4224]{1,0:T(8,128)(2,1)S(1)} %collective-permute-done.refs_2_, bf16[64,4224]{1,0:T(8,128)(2,1)S(1)} %collective-permute-done.2.refs_3_), custom_call_target="tpu_custom_call" | custom-call | flops 2101346304 | bytes 8208384 | tf_op jit(solution)/shard_map/score/pallas_call | solution.py:169
  38.9 2.6 %score.5.refs_1_ = f32[8,256]{1,0:T(8,128)S(1)} custom-call(bf16[1002,4096]{1,0:T(8,128)(2,1)S(1)} %fetch.1.w_ref, bf16[256,4224]{1,0:T(8,128)(2,1)S(1)} %collective-permute-done.6.refs_0_), custom_call_target="tpu_custom_call" | custom-call | flops 2101346304 | bytes 8208384 | tf_op jit(solution)/shard_map/score/pallas_call | solution.py:169
  42.2 2.9 %collective-permute-done.3.refs_1_ = bf16[64,4224]{1,0:T(8,128)(2,1)S(1)} collective-permute-done((bf16[64,4224]{1,0:T(8,128)(2,1)S(1)}, bf16[64,4224]{1,0:T(8,128)(2,1)S(1)}, u32[]{:S(2)}, u32[]{:S(2)}) %collective-permute-start.3) | collective-permute-done | bytes 540704 | tf_op jit(solution)/shard_map/ppermute | solution.py:42
  46.0 2.6 %collective-permute-start.8 = (bf16[32,4224]{1,0:T(8,128)(2,1)S(1)}, bf16[32,4224]{1,0:T(8,128)(2,1)S(1)}, u32[]{:S(2)}, u32[]{:S(2)}) collective-permute-start(bf16[32,4224]{1,0:T(8,128)(2,1)S(1)} %slice.87), channel_id=1, source_target_pairs={{0,12},{1,13},{2,14},{3,15},{4,8},{5,9},{6,10},{7,11},{8,4},{9,5},... | collective-permute-start | bytes 811016 | tf_op jit(solution)/shard_map/ppermute | solution.py:42
  48.6 0.8 %collective-permute-start.7 = (bf16[32,4224]{1,0:T(8,128)(2,1)S(1)}, bf16[32,4224]{1,0:T(8,128)(2,1)S(1)}, u32[]{:S(2)}, u32[]{:S(2)}) collective-permute-start(bf16[32,4224]{1,0:T(8,128)(2,1)S(1)} %slice.86), channel_id=1, source_target_pairs={{0,3},{1,2},{2,1},{3,0},{4,7},{5,6},{6,5},{7,4},{8,11},{9,10},{10,... | collective-permute-start | bytes 811016 | tf_op jit(solution)/shard_map/ppermute | solution.py:42
  49.4 2.7 %score.6.refs_2_ = f32[8,192]{1,0:T(8,128)S(1)} custom-call(bf16[1002,4096]{1,0:T(8,128)(2,1)S(1)} %fetch.1.w_ref, bf16[64,4224]{1,0:T(8,128)(2,1)S(1)} %collective-permute-done.1.refs_0_, bf16[64,4224]{1,0:T(8,128)(2,1)S(1)} %collective-permute-done.3.refs_1_, bf16[64,4224]{1,0:T(8,128)(2,1)S(1)} %collective-permute-done.5.refs_2_), custom_call_target="tpu_custom_call" | custom-call | flops 1576009728 | bytes 8208384 | tf_op jit(solution)/shard_map/score/pallas_call | solution.py:169
  52.1 1.7 %collective-permute-done.8 = bf16[32,4224]{1,0:T(8,128)(2,1)S(1)} collective-permute-done((bf16[32,4224]{1,0:T(8,128)(2,1)S(1)}, bf16[32,4224]{1,0:T(8,128)(2,1)S(1)}, u32[]{:S(2)}, u32[]{:S(2)}) %collective-permute-start.8) | collective-permute-done | bytes 270368 | tf_op jit(solution)/shard_map/ppermute | solution.py:42
  53.8 2.5 %collective-permute-done.7 = bf16[32,4224]{1,0:T(8,128)(2,1)S(1)} collective-permute-done((bf16[32,4224]{1,0:T(8,128)(2,1)S(1)}, bf16[32,4224]{1,0:T(8,128)(2,1)S(1)}, u32[]{:S(2)}, u32[]{:S(2)}) %collective-permute-start.7) | collective-permute-done | bytes 270368 | tf_op jit(solution)/shard_map/ppermute | solution.py:42
  56.6 2.7 %score.7.refs_3_ = f32[8,192]{1,0:T(8,128)S(1)} custom-call(bf16[1002,4096]{1,0:T(8,128)(2,1)S(1)} %fetch.1.w_ref, bf16[192,4224]{1,0:T(8,128)(2,1)S(1)} %collective-permute-done.9.refs_0_), custom_call_target="tpu_custom_call" | custom-call | flops 1576009728 | bytes 8208384 | tf_op jit(solution)/shard_map/score/pallas_call | solution.py:169
  59.3 2.6 %score_place.1 = (f32[3,8,128]{2,1,0:T(8,128)S(1)}, f32[2,8,128]{2,1,0:T(8,128)S(1)}) custom-call(bf16[1002,4096]{1,0:T(8,128)(2,1)S(1)} %fetch.1.w_ref, f32[8,256]{1,0:T(8,128)S(1)} %score.4.refs_0_, f32[8,256]{1,0:T(8,128)S(1)} %score.5.refs_1_, f32[8,192]{1,0:T(8,128)S(1)} %score.6.refs_2_, f32[8,192]{1,0:T(8,128)S(1)} %score.7.refs_3_, ...), custom_call_target="tpu_custom_call" | custom-call | flops 1050673152 | bytes 8208384 | tf_op jit(solution)/shard_map/score_place/pallas_call | solution.py:210
  62.4 0.8 %collective-permute-done.11 = f32[3,8,128]{2,1,0:T(8,128)S(1)} collective-permute-done((f32[3,8,128]{2,1,0:T(8,128)S(1)}, f32[3,8,128]{2,1,0:T(8,128)S(1)}, u32[]{:S(2)}, u32[]{:S(2)}) %collective-permute-start.11) | collective-permute-done | bytes 12320 | tf_op jit(solution)/shard_map/ppermute | solution.py:62
  63.4 1.1 %collective-permute-start.13 = (f32[3,8,128]{2,1,0:T(8,128)S(1)}, f32[3,8,128]{2,1,0:T(8,128)S(1)}, u32[]{:S(2)}, u32[]{:S(2)}) collective-permute-start(f32[3,8,128]{2,1,0:T(8,128)S(1)} %pad_maximum_fusion.3), channel_id=1, source_target_pairs={{0,112},{1,113},{2,114},{3,115},{4,116},{5,117},{6,118},{7,119},{8... | collective-permute-start | bytes 36872 | tf_op jit(solution)/shard_map/ppermute | solution.py:50
  64.5 2.0 %collective-permute-start.12 = (f32[3,8,128]{2,1,0:T(8,128)S(1)}, f32[3,8,128]{2,1,0:T(8,128)S(1)}, u32[]{:S(2)}, u32[]{:S(2)}) collective-permute-start(f32[3,8,128]{2,1,0:T(8,128)S(1)} %pad_maximum_fusion.3), channel_id=1, source_target_pairs={{0,48},{1,49},{2,50},{3,51},{4,52},{5,53},{6,54},{7,55},{8,56},{9,... | collective-permute-start | bytes 36872 | tf_op jit(solution)/shard_map/ppermute | solution.py:50
  66.5 1.5 %collective-permute-done.14 = f32[3,8,128]{2,1,0:T(8,128)S(1)} collective-permute-done((f32[3,8,128]{2,1,0:T(8,128)S(1)}, f32[3,8,128]{2,1,0:T(8,128)S(1)}, u32[]{:S(2)}, u32[]{:S(2)}) %collective-permute-start.14) | collective-permute-done | bytes 12320 | tf_op jit(solution)/shard_map/ppermute | solution.py:50
  68.1 2.0 %collective-permute-start.16 = (f32[3,8,128]{2,1,0:T(8,128)S(1)}, f32[3,8,128]{2,1,0:T(8,128)S(1)}, u32[]{:S(2)}, u32[]{:S(2)}) collective-permute-start(f32[3,8,128]{2,1,0:T(8,128)S(1)} %pad_maximum_fusion.4), channel_id=1, source_target_pairs={{0,28},{1,29},{2,30},{3,31},{4,24},{5,25},{6,26},{7,27},{8,20},{9,... | collective-permute-start | bytes 36872 | tf_op jit(solution)/shard_map/ppermute | solution.py:50
  70.2 1.1 %collective-permute-start.15 = (f32[3,8,128]{2,1,0:T(8,128)S(1)}, f32[3,8,128]{2,1,0:T(8,128)S(1)}, u32[]{:S(2)}, u32[]{:S(2)}) collective-permute-start(f32[3,8,128]{2,1,0:T(8,128)S(1)} %pad_maximum_fusion.4), channel_id=1, source_target_pairs={{0,20},{1,21},{2,22},{3,23},{4,16},{5,17},{6,18},{7,19},{8,28},{9,... | collective-permute-start | bytes 36872 | tf_op jit(solution)/shard_map/ppermute | solution.py:50
  71.3 1.5 %collective-permute-done.17 = f32[3,8,128]{2,1,0:T(8,128)S(1)} collective-permute-done((f32[3,8,128]{2,1,0:T(8,128)S(1)}, f32[3,8,128]{2,1,0:T(8,128)S(1)}, u32[]{:S(2)}, u32[]{:S(2)}) %collective-permute-start.17) | collective-permute-done | bytes 12320 | tf_op jit(solution)/shard_map/ppermute | solution.py:50
  73.4 1.7 %collective-permute-start.19 = (f32[3,8,128]{2,1,0:T(8,128)S(1)}, f32[3,8,128]{2,1,0:T(8,128)S(1)}, u32[]{:S(2)}, u32[]{:S(2)}) collective-permute-start(f32[3,8,128]{2,1,0:T(8,128)S(1)} %pad_maximum_fusion.5.refs_0_), channel_id=1, source_target_pairs={{0,19},{1,18},{2,17},{3,16},{4,23},{5,22},{6,21},{7,20},{8,27},{9,... | collective-permute-start | bytes 36872 | tf_op jit(solution)/shard_map/ppermute | solution.py:50
  75.1 1.3 %collective-permute-start.18 = (f32[3,8,128]{2,1,0:T(8,128)S(1)}, f32[3,8,128]{2,1,0:T(8,128)S(1)}, u32[]{:S(2)}, u32[]{:S(2)}) collective-permute-start(f32[3,8,128]{2,1,0:T(8,128)S(1)} %pad_maximum_fusion.5.refs_0_), channel_id=1, source_target_pairs={{0,17},{1,16},{2,19},{3,18},{4,21},{5,20},{6,23},{7,22},{8,25},{9,... | collective-permute-start | bytes 36872 | tf_op jit(solution)/shard_map/ppermute | solution.py:50
  76.4 1.6 %collective-permute-done.20.refs_3_ = f32[3,8,128]{2,1,0:T(8,128)S(1)} collective-permute-done((f32[3,8,128]{2,1,0:T(8,128)S(1)}, f32[3,8,128]{2,1,0:T(8,128)S(1)}, u32[]{:S(2)}, u32[]{:S(2)}) %collective-permute-start.20) | collective-permute-done | bytes 12320 | tf_op jit(solution)/shard_map/ppermute | solution.py:50
  78.2 0.8 final.1
  (35 shorter events, 6.0 us)
Async XLA Ops:
  1.4 0.9 %copy-start.1 = (bf16[16,4096]{1,0:T(8,128)(2,1)S(1)}, bf16[16,4096]{1,0:T(8,128)(2,1)}, u32[]{:S(2)}) copy-start(bf16[16,4096]{1,0:T(8,128)(2,1)} %hidden_ref.1) | copy-start | bytes 393220
  16.3 11.4 %collective-permute-start = (bf16[64,4224]{1,0:T(8,128)(2,1)S(1)}, bf16[64,4224]{1,0:T(8,128)(2,1)S(1)}, u32[]{:S(2)}, u32[]{:S(2)}) collective-permute-start(bf16[64,4224]{1,0:T(8,128)(2,1)S(1)} %bitcast.8), channel_id=1, source_target_pairs={{0,12},{1,13},{2,14},{3,15},{4,8},{5,9},{6,10},{7,11},{8,4},{9,5},... | collective-permute-start | bytes 1622024 | tf_op jit(solution)/shard_map/ppermute | solution.py:42
  18.5 10.6 %collective-permute-start.4 = (bf16[64,4224]{1,0:T(8,128)(2,1)S(1)}, bf16[64,4224]{1,0:T(8,128)(2,1)S(1)}, u32[]{:S(2)}, u32[]{:S(2)}) collective-permute-start(bf16[64,4224]{1,0:T(8,128)(2,1)S(1)} %bitcast.9), channel_id=1, source_target_pairs={{0,3},{1,2},{2,1},{3,0},{4,7},{5,6},{6,5},{7,4},{8,11},{9,10},{10,... | collective-permute-start | bytes 1622024 | tf_op jit(solution)/shard_map/ppermute | solution.py:42
  20.6 10.6 %collective-permute-start.2 = (bf16[64,4224]{1,0:T(8,128)(2,1)S(1)}, bf16[64,4224]{1,0:T(8,128)(2,1)S(1)}, u32[]{:S(2)}, u32[]{:S(2)}) collective-permute-start(bf16[64,4224]{1,0:T(8,128)(2,1)S(1)} %bitcast.10), channel_id=1, source_target_pairs={{0,96},{1,97},{2,98},{3,99},{4,100},{5,101},{6,102},{7,103},{8,104... | collective-permute-start | bytes 1622024 | tf_op jit(solution)/shard_map/ppermute | solution.py:42
  23.6 3.3 %copy-start = (bf16[4096,1002]{0,1:T(8,128)(2,1)S(1)}, bf16[4096,1002]{0,1:T(8,128)(2,1)}, u32[]{:S(2)}) copy-start(bf16[4096,1002]{0,1:T(8,128)(2,1)} %param.7) | copy-start | bytes 24625156
  31.3 7.6 %collective-permute-start.6 = (bf16[256,4224]{1,0:T(8,128)(2,1)S(1)}, bf16[256,4224]{1,0:T(8,128)(2,1)S(1)}, u32[]{:S(2)}, u32[]{:S(2)}) collective-permute-start(bf16[256,4224]{1,0:T(8,128)(2,1)S(1)} %pad_maximum_fusion), channel_id=1, source_target_pairs={{0,16},{1,17},{2,18},{3,19},{4,20},{5,21},{6,22},{7,23},{8,24},{9,... | collective-permute-start | bytes 6488072 | tf_op jit(solution)/shard_map/ppermute | solution.py:62
  31.6 10.6 %collective-permute-start.5 = (bf16[64,4224]{1,0:T(8,128)(2,1)S(1)}, bf16[64,4224]{1,0:T(8,128)(2,1)S(1)}, u32[]{:S(2)}, u32[]{:S(2)}) collective-permute-start(bf16[64,4224]{1,0:T(8,128)(2,1)S(1)} %collective-permute-done.4.refs_1_), channel_id=1, source_target_pairs={{0,96},{1,97},{2,98},{3,99},{4,100},{5,101},{6,102},{7,103},{8,104... | collective-permute-start | bytes 1622024 | tf_op jit(solution)/shard_map/ppermute | solution.py:42
  34.5 10.6 %collective-permute-start.3 = (bf16[64,4224]{1,0:T(8,128)(2,1)S(1)}, bf16[64,4224]{1,0:T(8,128)(2,1)S(1)}, u32[]{:S(2)}, u32[]{:S(2)}) collective-permute-start(bf16[64,4224]{1,0:T(8,128)(2,1)S(1)} %collective-permute-done.2.refs_3_), channel_id=1, source_target_pairs={{0,12},{1,13},{2,14},{3,15},{4,8},{5,9},{6,10},{7,11},{8,4},{9,5},... | collective-permute-start | bytes 1622024 | tf_op jit(solution)/shard_map/ppermute | solution.py:42
  35.2 10.6 %collective-permute-start.1 = (bf16[64,4224]{1,0:T(8,128)(2,1)S(1)}, bf16[64,4224]{1,0:T(8,128)(2,1)S(1)}, u32[]{:S(2)}, u32[]{:S(2)}) collective-permute-start(bf16[64,4224]{1,0:T(8,128)(2,1)S(1)} %collective-permute-done.refs_2_), channel_id=1, source_target_pairs={{0,3},{1,2},{2,1},{3,0},{4,7},{5,6},{6,5},{7,4},{8,11},{9,10},{10,... | collective-permute-start | bytes 1622024 | tf_op jit(solution)/shard_map/ppermute | solution.py:42
  45.9 10.7 %collective-permute-start.9 = (bf16[192,4224]{1,0:T(8,128)(2,1)S(1)}, bf16[192,4224]{1,0:T(8,128)(2,1)S(1)}, u32[]{:S(2)}, u32[]{:S(2)}) collective-permute-start(bf16[192,4224]{1,0:T(8,128)(2,1)S(1)} %pad_maximum_fusion.1), channel_id=1, source_target_pairs={{0,16},{1,17},{2,18},{3,19},{4,20},{5,21},{6,22},{7,23},{8,24},{9,... | collective-permute-start | bytes 4866056 | tf_op jit(solution)/shard_map/ppermute | solution.py:62
  46.0 7.8 %collective-permute-start.8 = (bf16[32,4224]{1,0:T(8,128)(2,1)S(1)}, bf16[32,4224]{1,0:T(8,128)(2,1)S(1)}, u32[]{:S(2)}, u32[]{:S(2)}) collective-permute-start(bf16[32,4224]{1,0:T(8,128)(2,1)S(1)} %slice.87), channel_id=1, source_target_pairs={{0,12},{1,13},{2,14},{3,15},{4,8},{5,9},{6,10},{7,11},{8,4},{9,5},... | collective-permute-start | bytes 811016 | tf_op jit(solution)/shard_map/ppermute | solution.py:42
  48.6 7.7 %collective-permute-start.7 = (bf16[32,4224]{1,0:T(8,128)(2,1)S(1)}, bf16[32,4224]{1,0:T(8,128)(2,1)S(1)}, u32[]{:S(2)}, u32[]{:S(2)}) collective-permute-start(bf16[32,4224]{1,0:T(8,128)(2,1)S(1)} %slice.86), channel_id=1, source_target_pairs={{0,3},{1,2},{2,1},{3,0},{4,7},{5,6},{6,5},{7,4},{8,11},{9,10},{10,... | collective-permute-start | bytes 811016 | tf_op jit(solution)/shard_map/ppermute | solution.py:42
  56.3 2.9 %collective-permute-start.10 = (bf16[64,4224]{1,0:T(8,128)(2,1)S(1)}, bf16[64,4224]{1,0:T(8,128)(2,1)S(1)}, u32[]{:S(2)}, u32[]{:S(2)}) collective-permute-start(bf16[64,4224]{1,0:T(8,128)(2,1)S(1)} %pad_maximum_fusion.2.refs_4_), channel_id=1, source_target_pairs={{0,16},{1,17},{2,18},{3,19},{4,20},{5,21},{6,22},{7,23},{8,24},{9,... | collective-permute-start | bytes 1622024 | tf_op jit(solution)/shard_map/ppermute | solution.py:62
  61.9 1.4 %collective-permute-start.11 = (f32[3,8,128]{2,1,0:T(8,128)S(1)}, f32[3,8,128]{2,1,0:T(8,128)S(1)}, u32[]{:S(2)}, u32[]{:S(2)}) collective-permute-start(f32[3,8,128]{2,1,0:T(8,128)S(1)} %get-tuple-element.29), channel_id=1, source_target_pairs={{0,16},{1,17},{2,18},{3,19},{4,20},{5,21},{6,22},{7,23},{8,24},{9,... | collective-permute-start | bytes 36872 | tf_op jit(solution)/shard_map/ppermute | solution.py:62
  63.3 4.7 %collective-permute-start.14 = (f32[3,8,128]{2,1,0:T(8,128)S(1)}, f32[3,8,128]{2,1,0:T(8,128)S(1)}, u32[]{:S(2)}, u32[]{:S(2)}) collective-permute-start(f32[3,8,128]{2,1,0:T(8,128)S(1)} %pad_maximum_fusion.3), channel_id=1, source_target_pairs={{0,80},{1,81},{2,82},{3,83},{4,84},{5,85},{6,86},{7,87},{8,88},{9,... | collective-permute-start | bytes 36872 | tf_op jit(solution)/shard_map/ppermute | solution.py:50
  63.4 4.6 %collective-permute-start.13 = (f32[3,8,128]{2,1,0:T(8,128)S(1)}, f32[3,8,128]{2,1,0:T(8,128)S(1)}, u32[]{:S(2)}, u32[]{:S(2)}) collective-permute-start(f32[3,8,128]{2,1,0:T(8,128)S(1)} %pad_maximum_fusion.3), channel_id=1, source_target_pairs={{0,112},{1,113},{2,114},{3,115},{4,116},{5,117},{6,118},{7,119},{8... | collective-permute-start | bytes 36872 | tf_op jit(solution)/shard_map/ppermute | solution.py:50
  64.5 3.5 %collective-permute-start.12 = (f32[3,8,128]{2,1,0:T(8,128)S(1)}, f32[3,8,128]{2,1,0:T(8,128)S(1)}, u32[]{:S(2)}, u32[]{:S(2)}) collective-permute-start(f32[3,8,128]{2,1,0:T(8,128)S(1)} %pad_maximum_fusion.3), channel_id=1, source_target_pairs={{0,48},{1,49},{2,50},{3,51},{4,52},{5,53},{6,54},{7,55},{8,56},{9,... | collective-permute-start | bytes 36872 | tf_op jit(solution)/shard_map/ppermute | solution.py:50
  68.0 4.7 %collective-permute-start.17 = (f32[3,8,128]{2,1,0:T(8,128)S(1)}, f32[3,8,128]{2,1,0:T(8,128)S(1)}, u32[]{:S(2)}, u32[]{:S(2)}) collective-permute-start(f32[3,8,128]{2,1,0:T(8,128)S(1)} %pad_maximum_fusion.4), channel_id=1, source_target_pairs={{0,24},{1,25},{2,26},{3,27},{4,28},{5,29},{6,30},{7,31},{8,16},{9,... | collective-permute-start | bytes 36872 | tf_op jit(solution)/shard_map/ppermute | solution.py:50
  68.1 4.6 %collective-permute-start.16 = (f32[3,8,128]{2,1,0:T(8,128)S(1)}, f32[3,8,128]{2,1,0:T(8,128)S(1)}, u32[]{:S(2)}, u32[]{:S(2)}) collective-permute-start(f32[3,8,128]{2,1,0:T(8,128)S(1)} %pad_maximum_fusion.4), channel_id=1, source_target_pairs={{0,28},{1,29},{2,30},{3,31},{4,24},{5,25},{6,26},{7,27},{8,20},{9,... | collective-permute-start | bytes 36872 | tf_op jit(solution)/shard_map/ppermute | solution.py:50
  70.2 3.1 %collective-permute-start.15 = (f32[3,8,128]{2,1,0:T(8,128)S(1)}, f32[3,8,128]{2,1,0:T(8,128)S(1)}, u32[]{:S(2)}, u32[]{:S(2)}) collective-permute-start(f32[3,8,128]{2,1,0:T(8,128)S(1)} %pad_maximum_fusion.4), channel_id=1, source_target_pairs={{0,20},{1,21},{2,22},{3,23},{4,16},{5,17},{6,18},{7,19},{8,28},{9,... | collective-permute-start | bytes 36872 | tf_op jit(solution)/shard_map/ppermute | solution.py:50
  73.3 4.7 %collective-permute-start.20 = (f32[3,8,128]{2,1,0:T(8,128)S(1)}, f32[3,8,128]{2,1,0:T(8,128)S(1)}, u32[]{:S(2)}, u32[]{:S(2)}) collective-permute-start(f32[3,8,128]{2,1,0:T(8,128)S(1)} %pad_maximum_fusion.5.refs_0_), channel_id=1, source_target_pairs={{0,18},{1,19},{2,16},{3,17},{4,22},{5,23},{6,20},{7,21},{8,26},{9,... | collective-permute-start | bytes 36872 | tf_op jit(solution)/shard_map/ppermute | solution.py:50
  73.4 4.6 %collective-permute-start.19 = (f32[3,8,128]{2,1,0:T(8,128)S(1)}, f32[3,8,128]{2,1,0:T(8,128)S(1)}, u32[]{:S(2)}, u32[]{:S(2)}) collective-permute-start(f32[3,8,128]{2,1,0:T(8,128)S(1)} %pad_maximum_fusion.5.refs_0_), channel_id=1, source_target_pairs={{0,19},{1,18},{2,17},{3,16},{4,23},{5,22},{6,21},{7,20},{8,27},{9,... | collective-permute-start | bytes 36872 | tf_op jit(solution)/shard_map/ppermute | solution.py:50
  75.1 3.1 %collective-permute-start.18 = (f32[3,8,128]{2,1,0:T(8,128)S(1)}, f32[3,8,128]{2,1,0:T(8,128)S(1)}, u32[]{:S(2)}, u32[]{:S(2)}) collective-permute-start(f32[3,8,128]{2,1,0:T(8,128)S(1)} %pad_maximum_fusion.5.refs_0_), channel_id=1, source_target_pairs={{0,17},{1,16},{2,19},{3,18},{4,21},{5,20},{6,23},{7,22},{8,25},{9,... | collective-permute-start | bytes 36872 | tf_op jit(solution)/shard_map/ppermute | solution.py:50
